TPU v7x, 256 devices: a whole 4x4x8 slice. The times are simulated.
256 devices in a mesh: rows: 8 (over z_lo, x), cols: 32 (over y, z_hi, core).
Axes of the slice: x: 4, y: 4, z: 8 (z_hi: 4, z_lo: 2; z = z_hi * 2 + z_lo), core: 2. Of those that a mesh axis runs over, the one named last changes fastest.
Arguments:
- embeddings: float32 [1024, 16384], P('rows', 'cols'), may hold values from -70 to 70
Outputs:
- grad_scaled: float32 [1024, 16384], P('rows', 'cols')
- loss: float32 [], replicated
All inputs are finite; a program needn't handle non-finite values.
Results may differ from a plain program's by a relative error of at most 0.0003.
The roundings to bfloat16 on the way count: a program that leaves them out, or rounds other values in their place, can miss the bound.
Values may be sent and summed in bfloat16 or wider, within the bound.
No kernel may reach another device: no remote copies, remote signals or barrier semaphores. Data moves between devices by JAX's collectives and lax.ppermute only.
A program may use at most 64 MiB of HBM per device.

v0:
```python
import jax
import jax.numpy as jnp
from jax import lax
from jax.sharding import PartitionSpec as P


def on_device(embeddings):
    rows_here, col_width = embeddings.shape
    rows_count = lax.axis_size("rows")
    cols_count = lax.axis_size("cols")
    n_all = rows_here * rows_count
    width = col_width * cols_count
    col_sum = lax.psum(jnp.sum(embeddings, axis=0), "rows")
    mean = col_sum / n_all
    cz = embeddings - mean
    squares = lax.psum(jnp.sum(cz * cz, axis=0), "rows")
    var = squares / (n_all - 1)
    std = jnp.sqrt(var + 0.0001)
    var_share = jnp.sum(jax.nn.relu(1.0 - std))
    centered = cz.astype(jnp.bfloat16)
    centered_f32 = centered.astype(jnp.float32)
    scale = jnp.float32(n_all - 1)
    gathered = lax.all_gather(centered, "rows", axis=0, tiled=True)
    partial_gram = lax.dot_general(
        centered, gathered, (((1,), (1,)), ((), ())), preferred_element_type=jnp.float32
    )
    gram_here = lax.psum(partial_gram, "cols")
    gathered_f32 = gathered.astype(jnp.float32)
    col_norms = jnp.sum(gathered_f32 * gathered_f32, axis=0)
    grad_cov = (
        jnp.dot(gram_here, gathered_f32, precision=lax.Precision.HIGHEST) - centered_f32 * col_norms
    ) / scale
    cov_share = (
        jnp.sum(gram_here * gram_here) / cols_count - jnp.sum(col_norms * col_norms) / rows_count
    ) / (scale * scale)
    hinge = jnp.where(std < 1.0, cz / std, jnp.float32(0.0))
    grad_scaled = 4.0 / 25.0 * grad_cov - hinge
    share = cov_share / width + 25.0 * var_share / (width * rows_count)
    loss = lax.psum(share, ("rows", "cols"))
    return (grad_scaled, loss)


def solution(mesh):
    placed = (P("rows", "cols"),)
    return jax.shard_map(
        on_device, mesh=mesh, in_specs=placed, out_specs=(P("rows", "cols"), P()), check_vma=False
    )
```

profile of v0, /device:TPU:1, one launch (start us, length us, event | category | flops | bytes accessed | tf_op | source)
XLA Modules:
  0.0 447.0 jit_solution(5058714754237826495)
XLA Ops:
  7.2 0.0 all-gather.2.cloned.1.call-start
  7.2 1.0 reduce_sum.54
  8.2 17.2 %psum.28 = f32[512]{0:T(512)S(1)} all-reduce(f32[512]{0:T(512)S(1)} %reduce_sum.54), channel_id=1, replica_groups=mesh['rows'=8,'cols'=32] {'rows'}, use_global_device_ids=true, to_apply=%region_1.0 | all-reduce | flops 512 | bytes 4096 | tf_op jit(solution)/shard_map/psum | solution.py:13
  25.4 1.6 multiply_reduce_fusion.2
  27.0 0.0 all-gather.2.cloned.1.call-update
  27.1 0.0 all-reduce.2.cloned.1.call-start
  27.1 39.9 %all-gather.2.cloned.1.call-done = bf16[1024,512]{1,0:T(8,128)(2,1)} async-done(((bf16[128,512]{1,0:T(8,128)(2,1)}), bf16[1024,512]{1,0:T(8,128)(2,1)}) %all-gather.2.cloned.1.call-update) | async-done | bytes 1048592 | tf_op jit(solution)/shard_map/all_gather | solution.py:23
  67.0 0.0 copy-start
  67.0 2.7 fusion.2
  69.6 0.0 copy-start.1
  69.6 0.0 copy-start.2
  69.6 0.0 all-reduce.2.cloned.1.call-update
  69.7 14.0 %psum.30 = f32[512]{0:T(512)S(1)} all-reduce(f32[512]{0:T(512)S(1)} %get-tuple-element.2), channel_id=1, replica_groups=mesh['rows'=8,'cols'=32] {'rows'}, use_global_device_ids=true, to_apply=%region_5.6 | all-reduce | flops 512 | bytes 4096 | tf_op jit(solution)/shard_map/psum | solution.py:16
  83.6 0.6 maximum_reduce_fusion
  84.9 0.0 copy-done
  84.9 0.3 multiply_reduce_fusion
  85.2 0.6 multiply_reduce_fusion.3
  86.4 271.2 %all-reduce.2.cloned.1.call-done = f32[128,1024]{1,0:T(8,128)} async-done(((f32[128,1024]{1,0:T(8,128)}), f32[128,1024]{1,0:T(8,128)}) %all-reduce.2.cloned.1.call-update) | async-done | bytes 524304 | tf_op jit(solution)/shard_map/psum | solution.py:27
  357.7 1.8 multiply_reduce_fusion.1
  360.1 77.7 %psum.31 = f32[]{:T(128)} all-reduce(f32[]{:T(128)S(6)} %add.19), channel_id=1, replica_groups=mesh['rows'=8,'cols'=32] {'rows','cols'}, use_global_device_ids=true, to_apply=%region_9.10 | all-reduce | flops 1 | bytes 8 | tf_op jit(solution)/shard_map/psum | solution.py:39
  437.9 0.0 copy-done.1
  437.9 0.0 copy-done.2
  437.9 2.3 fusion.1
  (2 shorter events, 0.0 us)
Async XLA Ops:
  7.2 59.8 %all-gather.2.cloned.1.call-start = ((), (), s32[]{:S(2)}) async-start(), calls=%async_computation | async-start | bytes 1179648 | tf_op jit(solution)/shard_map/all_gather | solution.py:23
  27.1 330.6 %all-reduce.2.cloned.1.call-start = ((), (), s32[]{:S(2)}) async-start(), calls=%async_computation.1 | async-start | bytes 1048576 | tf_op jit(solution)/shard_map/psum | solution.py:27
  67.0 17.9 %copy-start = (bf16[1024,512]{1,0:T(8,128)(2,1)S(1)}, bf16[1024,512]{1,0:T(8,128)(2,1)}, u32[]{:S(2)}) copy-start(bf16[1024,512]{1,0:T(8,128)(2,1)} %all-gather.2.cloned.1.call-done) | copy-start | bytes 3145732
  69.6 368.2 %copy-start.1 = (bf16[128,512]{1,0:T(8,128)(2,1)S(1)}, bf16[128,512]{1,0:T(8,128)(2,1)}, u32[]{:S(2)}) copy-start(bf16[128,512]{1,0:T(8,128)(2,1)} %get-tuple-element.3) | copy-start | bytes 393220
  69.6 368.2 %copy-start.2 = (f32[128,512]{1,0:T(8,128)S(1)}, f32[128,512]{1,0:T(8,128)}, u32[]{:S(2)}) copy-start(f32[128,512]{1,0:T(8,128)} %param.1) | copy-start | bytes 786436
Sparse Core Ops, SparseCore 0:
  27.2 39.7 all-gather.1
  69.8 287.8 all-reduce.1
where the time goes:
time: 447 us
  waiting for transfers between devices  311 us (70%)
  blocking collectives  109 us (24%)
  between operations  16 us (4%)
  other arithmetic  5.91 us (1%)
  matrix products  5.01 us (1%)
    psum x1, waiting for transfers between devices, on_device(): gram_here = lax.psum(partial_gram, 'cols')  271 us
    psum x1, blocking collectives, on_device(): loss = lax.psum(share, ('rows', 'cols'))  77.7 us
    all_gather x1, waiting for transfers between devices, on_device(): gathered = lax.all_gather(centered, 'rows', axis=0, tiled=True)  39.9 us
    psum x1, blocking collectives, on_device(): col_sum = lax.psum(jnp.sum(embeddings, axis=0), 'rows')  17.2 us
    psum x1, blocking collectives, on_device(): squares = lax.psum(jnp.sum(cz * cz, axis=0), 'rows')  14 us
  transfers between devices with their start and end apart: 2, of which 2 were waited for; matrix products, arithmetic and copies ran while one was open for 0% of the time, Pallas kernels for 0%

commit v1 on v0

v1 whole, which is shorter than its diff:
```python
import jax
import jax.numpy as jnp
from jax import lax
from jax.sharding import Mesh
from jax.sharding import PartitionSpec as P

ROWS = ("zl", "x")
CHIPS = ("y", "zh")
SWAP = [(0, 1), (1, 0)]
F32 = jnp.float32
BF16 = jnp.bfloat16


def spread(block, axes, count):
    return lax.all_to_all(jnp.broadcast_to(block, (count,) + block.shape), axes, 0, 0)


def three_terms(a):
    high = lax.reduce_precision(a, 8, 7)
    rest = a - high
    mid = lax.reduce_precision(rest, 8, 7)
    low = rest - mid
    return jnp.concatenate([high.astype(BF16), mid.astype(BF16), low.astype(BF16)], axis=0)


def on_device(embeddings):
    rows_here, col_width = embeddings.shape
    rows_count = lax.axis_size(ROWS)
    chips_count = lax.axis_size(CHIPS)
    cols_count = chips_count * lax.axis_size("core")
    core = lax.axis_index("core")
    n_all = rows_here * rows_count
    width = col_width * cols_count
    scale = F32(n_all - 1)

    sum_here = jnp.sum(embeddings, axis=0)
    off_here = embeddings - sum_here / rows_here
    squares_here = jnp.sum(off_here * off_here, axis=0)
    stats = spread(jnp.stack([sum_here, squares_here]), ROWS, rows_count)
    sums, squares = stats[:, 0], stats[:, 1]
    mean = jnp.sum(sums, axis=0) / n_all
    gaps = sums / rows_here - mean
    var = (jnp.sum(squares, axis=0) + rows_here * jnp.sum(gaps * gaps, axis=0)) / scale
    std = jnp.sqrt(var + 0.0001)

    cz = embeddings - mean
    centered = cz.astype(BF16)
    gathered = spread(centered, ROWS, rows_count).reshape(n_all, col_width)

    gathered_f32 = gathered.astype(F32)
    col_norms = jnp.sum(gathered_f32 * gathered_f32, axis=0)
    block_share = (
        25.0 * jnp.sum(jax.nn.relu(1.0 - std)) - jnp.sum(col_norms * col_norms) / (scale * scale)
    ) / width

    half = rows_here // 2

    def half_gram(which):
        own = lax.dynamic_slice_in_dim(centered, which * half, half, 0)
        gram = lax.dot_general(
            own, gathered, (((1,), (1,)), ((), ())), preferred_element_type=F32
        )
        return jnp.concatenate([gram, jnp.full((half, 128), block_share)], axis=1)

    from_pair = lax.ppermute(half_gram(1 - core), "core", SWAP)
    chip_half = half_gram(core) + from_pair
    piece = half // chips_count
    pieces = lax.all_to_all(chip_half.reshape(chips_count, piece, n_all + 128), CHIPS, 0, 0)
    mine = jnp.sum(pieces, axis=0)
    blocks_share = mine[0, n_all]
    my_half = spread(mine[:, :n_all], CHIPS, chips_count).reshape(half, n_all)

    norm = jnp.sum(my_half * my_half)
    for axis, perm in (
        ("core", SWAP),
        ("zl", SWAP),
        ("x", [(0, 1), (1, 0), (2, 3), (3, 2)]),
        ("x", [(0, 2), (2, 0), (1, 3), (3, 1)]),
    ):
        norm = norm + lax.ppermute(norm, axis, perm)
    loss = norm / (scale * scale * width) + blocks_share

    other_half = lax.ppermute(my_half, "core", SWAP)
    first = jnp.where(core == 0, my_half, other_half)
    second = jnp.where(core == 0, other_half, my_half)
    gram = jnp.concatenate([first, second], axis=0)
    terms = jnp.dot(three_terms(gram), gathered, preferred_element_type=F32)
    product = terms[:rows_here] + terms[rows_here : 2 * rows_here] + terms[2 * rows_here :]
    grad_cov = (product - centered.astype(F32) * col_norms) / scale
    hinge = jnp.where(std < 1.0, cz / std, F32(0.0))
    return (4.0 / 25.0 * grad_cov - hinge, loss)


def solution(mesh):
    parts = Mesh(mesh.devices.reshape(2, 4, 4, 4, 2), ("zl", "x", "y", "zh", "core"))
    placed = P(("zl", "x"), ("y", "zh", "core"))
    return jax.shard_map(
        on_device, mesh=parts, in_specs=(placed,), out_specs=(placed, P()), check_vma=False
    )
```

time: 447 us -> 101 us (0.23)
  waiting for transfers between devices: 311 us -> 15.8 us
  blocking collectives: 109 us -> 48.8 us
  starting transfers between devices: 0.08 us -> 16.7 us
  between operations: 16 us -> 7.27 us
    psum x1 -> x0, waiting for transfers between devices: 271 us -> none  [on_device(): gram_here = lax.psum(partial_gram, 'cols')]
    psum x3 -> x0, blocking collectives: 109 us -> none  [the longest x1 77.7 us: on_device(): loss = lax.psum(share, ('rows', 'cols'))]
    all_to_all x0 -> x3, blocking collectives: none -> 48.8 us  [the longest x2 26.7 us: spread(): lax.all_to_all(jnp.broadcast_to(block, (count,) + block.shape), axes, 0, 0)]
    all_gather x1 -> x0, waiting for transfers between devices: 39.9 us -> none  [on_device(): gathered = lax.all_gather(centered, 'rows', axis=0, tiled=True)]
    ppermute x0 -> x6, starting transfers between devices: none -> 13.2 us  [the longest x4 6.11 us: on_device(): norm = norm + lax.ppermute(norm, axis, perm)]
    all_to_all x0 -> x1, waiting for transfers between devices: none -> 10.3 us  [spread(): lax.all_to_all(jnp.broadcast_to(block, (count,) + block.shape), axes, 0, 0)]
    ppermute x0 -> x6, waiting for transfers between devices: none -> 5.53 us  [the longest x4 4.75 us: on_device(): norm = norm + lax.ppermute(norm, axis, perm)]
  transfers between devices with their start and end apart: 2 -> 7, of which waited for: 2 -> 6; matrix products, arithmetic and copies ran while one was open for 0% -> 2% of each run, Pallas kernels for 0% -> 0%
where the time goes in v1:
time: 101 us; the launch traced here: 98.7 us
  blocking collectives  48.8 us (48%)
  starting transfers between devices  16.7 us (17%)
  waiting for transfers between devices  15.8 us (16%)
  between operations  7.27 us (7%)
  other arithmetic  6.37 us (6%)
  local copies, waits for them, and re-layouts  2.23 us (2%)
  matrix products  1.43 us (1%)
    all_to_all x2, blocking collectives, spread(): lax.all_to_all(jnp.broadcast_to(block, (count,) + block.shape), axes, 0, 0)  26.7 us
    all_to_all x1, blocking collectives, on_device(): lax.all_to_all(chip_half.reshape(chips_count, piece, n_all + 128), CHIPS,...  22.1 us
    all_to_all x1, waiting for transfers between devices, spread(): lax.all_to_all(jnp.broadcast_to(block, (count,) + block.shape), axes, 0, 0)  10.3 us
    ppermute x4, starting transfers between devices, on_device(): norm = norm + lax.ppermute(norm, axis, perm)  6.11 us
    ppermute x4, waiting for transfers between devices, on_device(): norm = norm + lax.ppermute(norm, axis, perm)  4.75 us
    ppermute x1, starting transfers between devices, on_device(): from_pair = lax.ppermute(half_gram(1 - core), 'core', SWAP)  4.15 us
    all_to_all x1, starting transfers between devices, spread(): lax.all_to_all(jnp.broadcast_to(block, (count,) + block.shape), axes, 0, 0)  3.56 us
    ppermute x1, starting transfers between devices, on_device(): other_half = lax.ppermute(my_half, 'core', SWAP)  2.91 us
  transfers between devices with their start and end apart: 7, of which 6 were waited for; matrix products, arithmetic and copies ran while one was open for 2% of the time, Pallas kernels for 0%

profile of v1, /device:TPU:1, one launch (start us, length us, event | category | flops | bytes accessed | tf_op | source)
XLA Modules:
  0.0 98.7 jit_solution(4711976071414024701)
XLA Ops:
  0.6 1.0 reduce_sum.90
  1.6 1.0 %multiply_reduce_fusion.1 = f32[512]{0:T(512)S(1)} fusion(f32[128,512]{1,0:T(8,128)} %param.1, f32[512]{0:T(512)S(1)} %broadcast_multiply_fusion.1), kind=kLoop, calls=%fused_computation.21 | loop fusion | flops 196096 | bytes 266240 | tf_op jit(solution)/shard_map/reduce_sum | solution.py:38
  2.7 11.1 %all_to_all.20 = f32[8,2,512]{2,1,0:T(2,128)S(1)} all-to-all(f32[8,2,512]{2,1,0:T(2,128)S(1)} %broadcast_in_dim.24), channel_id=1, replica_groups=mesh['zl'=2,'x'=4,'y'=4,'zh'=4,'core'=2] {'zl','x'}, dimensions={0} | all-to-all | bytes 65536 | tf_op jit(solution)/shard_map/all_to_all | solution.py:15
  13.8 1.0 subtract_convert_fusion
  14.8 1.1 %broadcast_in_dim.25 = bf16[8,128,512]{2,1,0:T(8,128)(2,1)} broadcast(bf16[128,512]{1,0:T(8,128)(2,1)S(1)} %subtract_convert_fusion), dimensions={1,2} | broadcast | bytes 1179648 | tf_op jit(solution)/shard_map/broadcast_in_dim | solution.py:15
  15.9 3.6 %all-to-all-start.1 = ((bf16[8,128,512]{2,1,0:T(8,128)(2,1)}), bf16[8,128,512]{2,1,0:T(8,128)(2,1)S(1)}, u32[]{:S(2)}, u32[]{:S(2)}) async-start(bf16[8,128,512]{2,1,0:T(8,128)(2,1)} %broadcast_in_dim.25), calls=%async_computation.1 | async-start | bytes 2097152 | tf_op jit(solution)/shard_map/all_to_all | solution.py:15
  19.5 0.6 maximum_reduce_fusion
  20.7 10.3 %all-to-all-done.1 = bf16[8,128,512]{2,1,0:T(8,128)(2,1)S(1)} async-done(((bf16[8,128,512]{2,1,0:T(8,128)(2,1)}), bf16[8,128,512]{2,1,0:T(8,128)(2,1)S(1)}, u32[]{:S(2)}, u32[]{:S(2)}) %all-to-all-start.1) | async-done | bytes 1048608 | tf_op jit(solution)/shard_map/all_to_all | solution.py:15
  31.1 0.3 multiply_reduce_fusion
  31.3 0.6 multiply_reduce_fusion.2
  32.6 0.4 fusion.11
  33.1 4.1 %collective-permute-start = (f32[64,1152]{1,0:T(8,128)S(1)}, f32[64,1152]{1,0:T(8,128)S(1)}, u32[]{:S(2)}, u32[]{:S(2)}) collective-permute-start(f32[64,1152]{1,0:T(8,128)S(1)} %concatenate.13), channel_id=1, source_target_pairs={{0,1},{1,0},{2,3},{3,2},{4,5},{5,4},{6,7},{7,6},{8,9},{9,8},{10,11... | collective-permute-start | bytes 884744 | tf_op jit(solution)/shard_map/ppermute | solution.py:65
  37.2 0.4 fusion.13
  37.6 0.8 collective-permute-done
  38.5 0.1 reshape.32
  38.5 22.1 %all_to_all.21 = f32[16,4,1152]{2,1,0:T(4,128)S(1)} all-to-all(f32[16,4,1152]{2,1,0:T(4,128)S(1)} %reshape.32), channel_id=1, replica_groups=mesh['zl'=2,'x'=4,'y'=4,'zh'=4,'core'=2] {'y','zh'}, dimensions={0} | all-to-all | bytes 589824 | tf_op jit(solution)/shard_map/all_to_all | solution.py:68
  60.8 15.6 %all_to_all.22 = f32[16,4,1024]{2,1,0:T(4,128)S(1)} all-to-all(f32[16,4,1024]{2,1,0:T(4,128)S(1)} %broadcast_in_dim.26), channel_id=1, replica_groups=mesh['zl'=2,'x'=4,'y'=4,'zh'=4,'core'=2] {'y','zh'}, dimensions={0} | all-to-all | bytes 524288 | tf_op jit(solution)/shard_map/all_to_all | solution.py:15
  76.4 0.1 reshape.33
  76.5 2.9 %collective-permute-start.1 = (f32[64,1024]{1,0:T(8,128)S(1)}, f32[64,1024]{1,0:T(8,128)S(1)}, u32[]{:S(2)}, u32[]{:S(2)}) collective-permute-start(f32[64,1024]{1,0:T(8,128)S(1)} %reshape.33), channel_id=1, source_target_pairs={{0,1},{1,0},{2,3},{3,2},{4,5},{5,4},{6,7},{7,6},{8,9},{9,8},{10,11... | collective-permute-start | bytes 786440 | tf_op jit(solution)/shard_map/ppermute | solution.py:83
  79.4 0.5 slice.34
  79.9 0.7 fusion.10
  80.7 1.2 %collective-permute-done.2 = f32[]{:T(128)} collective-permute-done((f32[]{:T(128)}, f32[]{:T(128)}, u32[]{:S(2)}, u32[]{:S(2)}) %collective-permute-start.2) | collective-permute-done | bytes 36 | tf_op jit(solution)/shard_map/ppermute | solution.py:80
  83.2 2.6 %collective-permute-start.3 = (f32[]{:T(128)}, f32[]{:T(128)}, u32[]{:S(2)}, u32[]{:S(2)}) collective-permute-start(f32[]{:T(128)} %add.59), channel_id=1, source_target_pairs={{0,128},{128,0},{1,129},{129,1},{2,130},{130,2},{3,131},{131,3},{4... | collective-permute-start | bytes 20 | tf_op jit(solution)/shard_map/ppermute | solution.py:80
  85.9 0.3 collective-permute-done.3
  86.9 1.4 %collective-permute-start.4 = (f32[]{:T(128)}, f32[]{:T(128)}, u32[]{:S(2)}, u32[]{:S(2)}) collective-permute-start(f32[]{:T(128)} %add.60), channel_id=1, source_target_pairs={{0,32},{32,0},{64,96},{96,64},{1,33},{33,1},{65,97},{97,65},{2,34}... | collective-permute-start | bytes 20 | tf_op jit(solution)/shard_map/ppermute | solution.py:80
  88.2 1.2 %collective-permute-done.4 = f32[]{:T(128)} collective-permute-done((f32[]{:T(128)}, f32[]{:T(128)}, u32[]{:S(2)}, u32[]{:S(2)}) %collective-permute-start.4) | collective-permute-done | bytes 36 | tf_op jit(solution)/shard_map/ppermute | solution.py:80
  90.1 2.1 %collective-permute-start.5 = (f32[]{:T(128)}, f32[]{:T(128)}, u32[]{:S(2)}, u32[]{:S(2)}) collective-permute-start(f32[]{:T(128)} %add.61), channel_id=1, source_target_pairs={{0,64},{64,0},{32,96},{96,32},{1,65},{65,1},{33,97},{97,33},{2,66}... | collective-permute-start | bytes 20 | tf_op jit(solution)/shard_map/ppermute | solution.py:80
  92.2 2.0 %collective-permute-done.5 = f32[]{:T(128)} collective-permute-done((f32[]{:T(128)}, f32[]{:T(128)}, u32[]{:S(2)}, u32[]{:S(2)}) %collective-permute-start.5) | collective-permute-done | bytes 36 | tf_op jit(solution)/shard_map/ppermute | solution.py:80
  95.6 0.1 reduce-precision_convert_fusion.1
  95.8 0.6 fusion
  96.4 0.4 copy-done
  96.7 0.8 fusion.9
  (16 shorter events, 0.4 us)
Async XLA Ops:
  15.9 15.2 %all-to-all-start.1 = ((bf16[8,128,512]{2,1,0:T(8,128)(2,1)}), bf16[8,128,512]{2,1,0:T(8,128)(2,1)S(1)}, u32[]{:S(2)}, u32[]{:S(2)}) async-start(bf16[8,128,512]{2,1,0:T(8,128)(2,1)} %broadcast_in_dim.25), calls=%async_computation.1 | async-start | bytes 2097152 | tf_op jit(solution)/shard_map/all_to_all | solution.py:15
  33.1 5.4 %collective-permute-start = (f32[64,1152]{1,0:T(8,128)S(1)}, f32[64,1152]{1,0:T(8,128)S(1)}, u32[]{:S(2)}, u32[]{:S(2)}) collective-permute-start(f32[64,1152]{1,0:T(8,128)S(1)} %concatenate.13), channel_id=1, source_target_pairs={{0,1},{1,0},{2,3},{3,2},{4,5},{5,4},{6,7},{7,6},{8,9},{9,8},{10,11... | collective-permute-start | bytes 884744 | tf_op jit(solution)/shard_map/ppermute | solution.py:65
  76.5 19.1 %collective-permute-start.1 = (f32[64,1024]{1,0:T(8,128)S(1)}, f32[64,1024]{1,0:T(8,128)S(1)}, u32[]{:S(2)}, u32[]{:S(2)}) collective-permute-start(f32[64,1024]{1,0:T(8,128)S(1)} %reshape.33), channel_id=1, source_target_pairs={{0,1},{1,0},{2,3},{3,2},{4,5},{5,4},{6,7},{7,6},{8,9},{9,8},{10,11... | collective-permute-start | bytes 786440 | tf_op jit(solution)/shard_map/ppermute | solution.py:83
  80.6 1.2 %collective-permute-start.2 = (f32[]{:T(128)}, f32[]{:T(128)}, u32[]{:S(2)}, u32[]{:S(2)}) collective-permute-start(f32[]{:T(128)} %fusion.10), channel_id=1, source_target_pairs={{0,1},{1,0},{2,3},{3,2},{4,5},{5,4},{6,7},{7,6},{8,9},{9,8},{10,11... | collective-permute-start | bytes 20 | tf_op jit(solution)/shard_map/ppermute | solution.py:80
  83.2 3.0 %collective-permute-start.3 = (f32[]{:T(128)}, f32[]{:T(128)}, u32[]{:S(2)}, u32[]{:S(2)}) collective-permute-start(f32[]{:T(128)} %add.59), channel_id=1, source_target_pairs={{0,128},{128,0},{1,129},{129,1},{2,130},{130,2},{3,131},{131,3},{4... | collective-permute-start | bytes 20 | tf_op jit(solution)/shard_map/ppermute | solution.py:80
  86.9 2.6 %collective-permute-start.4 = (f32[]{:T(128)}, f32[]{:T(128)}, u32[]{:S(2)}, u32[]{:S(2)}) collective-permute-start(f32[]{:T(128)} %add.60), channel_id=1, source_target_pairs={{0,32},{32,0},{64,96},{96,64},{1,33},{33,1},{65,97},{97,65},{2,34}... | collective-permute-start | bytes 20 | tf_op jit(solution)/shard_map/ppermute | solution.py:80
  90.1 4.1 %collective-permute-start.5 = (f32[]{:T(128)}, f32[]{:T(128)}, u32[]{:S(2)}, u32[]{:S(2)}) collective-permute-start(f32[]{:T(128)} %add.61), channel_id=1, source_target_pairs={{0,64},{64,0},{32,96},{96,32},{1,65},{65,1},{33,97},{97,33},{2,66}... | collective-permute-start | bytes 20 | tf_op jit(solution)/shard_map/ppermute | solution.py:80
  95.8 1.0 copy-start

commit v2 on v1

--- a/solution.py
+++ b/solution.py
@@ -5,7 +5,6 @@
 from jax.sharding import PartitionSpec as P
 
 ROWS = ("zl", "x")
-CHIPS = ("y", "zh")
 SWAP = [(0, 1), (1, 0)]
 F32 = jnp.float32
 BF16 = jnp.bfloat16
@@ -13,6 +12,11 @@
 
 def spread(block, axes, count):
     return lax.all_to_all(jnp.broadcast_to(block, (count,) + block.shape), axes, 0, 0)
+
+
+def shift(block, axis, k):
+    size = lax.axis_size(axis)
+    return lax.ppermute(block, axis, [(i, (i + k) % size) for i in range(size)])
 
 
 def three_terms(a):
@@ -26,9 +30,10 @@
 def on_device(embeddings):
     rows_here, col_width = embeddings.shape
     rows_count = lax.axis_size(ROWS)
-    chips_count = lax.axis_size(CHIPS)
-    cols_count = chips_count * lax.axis_size("core")
+    ys = lax.axis_size("y")
+    cols_count = ys * lax.axis_size("zh") * lax.axis_size("core")
     core = lax.axis_index("core")
+    y = lax.axis_index("y")
     n_all = rows_here * rows_count
     width = col_width * cols_count
     scale = F32(n_all - 1)
@@ -54,9 +59,11 @@
     ) / width
 
     half = rows_here // 2
+    piece = half // ys
 
     def half_gram(which):
         own = lax.dynamic_slice_in_dim(centered, which * half, half, 0)
+        own = lax.dynamic_slice_in_dim(jnp.concatenate([own, own]), y * piece, half, 0)
         gram = lax.dot_general(
             own, gathered, (((1,), (1,)), ((), ())), preferred_element_type=F32
         )
@@ -64,23 +71,21 @@
 
     from_pair = lax.ppermute(half_gram(1 - core), "core", SWAP)
     chip_half = half_gram(core) + from_pair
-    piece = half // chips_count
-    pieces = lax.all_to_all(chip_half.reshape(chips_count, piece, n_all + 128), CHIPS, 0, 0)
-    mine = jnp.sum(pieces, axis=0)
+    chunks = [chip_half[k * piece : (k + 1) * piece] for k in range(ys)]
+    over_y = chunks[0] + sum(shift(chunks[k], "y", k) for k in (2, 1, 3))
+    mine = over_y + sum(shift(over_y, "zh", k) for k in (2, 1, 3))
     blocks_share = mine[0, n_all]
-    my_half = spread(mine[:, :n_all], CHIPS, chips_count).reshape(half, n_all)
+    mine = mine[:, :n_all]
+    back = {k: shift(mine, "y", k) for k in (2, 1, 3)}
+    around = jnp.concatenate([back[3], back[2], back[1], mine] * 2)
+    my_half = lax.dynamic_slice_in_dim(around, (ys - 1 - y) * piece, half, 0)
+    other_half = lax.ppermute(my_half, "core", SWAP)
 
-    norm = jnp.sum(my_half * my_half)
-    for axis, perm in (
-        ("core", SWAP),
-        ("zl", SWAP),
-        ("x", [(0, 1), (1, 0), (2, 3), (3, 2)]),
-        ("x", [(0, 2), (2, 0), (1, 3), (3, 1)]),
-    ):
-        norm = norm + lax.ppermute(norm, axis, perm)
+    norm_here = jnp.sum(my_half * my_half)
+    norms = spread(jnp.full((128,), norm_here), ROWS + ("core",), 2 * rows_count)
+    norm = jnp.sum(norms[:, 0])
     loss = norm / (scale * scale * width) + blocks_share
 
-    other_half = lax.ppermute(my_half, "core", SWAP)
     first = jnp.where(core == 0, my_half, other_half)
     second = jnp.where(core == 0, other_half, my_half)
     gram = jnp.concatenate([first, second], axis=0)

time: 101 us -> 87.7 us (0.87); the launches traced: 98.7 us -> 87.3 us
  blocking collectives: 48.8 us -> 11.1 us
  starting transfers between devices: 16.7 us -> 32 us
  waiting for transfers between devices: 15.8 us -> 27.8 us
  between operations: 7.27 us -> 4.58 us
  local copies, waits for them, and re-layouts: 2.23 us -> 3.43 us
    all_to_all x1 -> x0, blocking collectives: 22.1 us -> none  [on_device(): lax.all_to_all(chip_half.reshape(chips_count, piece, n_all + 128), CHIPS,...]
    all_to_all x2 -> x1, blocking collectives: 26.7 us -> 11.1 us  [spread(): lax.all_to_all(jnp.broadcast_to(block, (count,) + block.shape), axes, 0, 0)]
    ppermute x4 -> x9, starting transfers between devices: 6.11 us -> 16 us  [shift(): return lax.ppermute(block, axis, [(i, (i + k) % size) for i in range(size)])]
    ppermute x4 -> x9, waiting for transfers between devices: 4.75 us -> 12 us  [shift(): return lax.ppermute(block, axis, [(i, (i + k) % size) for i in range(size)])]
    all_to_all x1 -> x2, waiting for transfers between devices: 10.3 us -> 15.1 us  [spread(): lax.all_to_all(jnp.broadcast_to(block, (count,) + block.shape), axes, 0, 0)]
    all_to_all x1 -> x2, starting transfers between devices: 3.56 us -> 7.78 us  [spread(): lax.all_to_all(jnp.broadcast_to(block, (count,) + block.shape), axes, 0, 0)]
    another operation x0 -> x1, local copies, waits for them, and re-layouts: none -> 1.25 us  [spread(): jnp.broadcast_to(block, (count,) + block.shape)]
    ppermute x1, starting transfers between devices: 2.91 us -> 4.12 us  [on_device(): other_half = lax.ppermute(my_half, 'core', SWAP)]
  transfers between devices with their start and end apart: 7 -> 13, of which waited for: 6 -> 10; matrix products, arithmetic and copies ran while one was open for 2% -> 4% of each run, Pallas kernels for 0% -> 0%
where the time goes in v2:
time: 87.7 us; the launch traced here: 87.3 us
  starting transfers between devices  32 us (36%)
  waiting for transfers between devices  27.8 us (32%)
  blocking collectives  11.1 us (13%)
  other arithmetic  6.9 us (8%)
  between operations  4.58 us (5%)
  local copies, waits for them, and re-layouts  3.43 us (4%)
  matrix products  1.4 us (2%)
    ppermute x9, starting transfers between devices, shift(): return lax.ppermute(block, axis, [(i, (i + k) % size) for i in range(size)])  16 us
    all_to_all x2, waiting for transfers between devices, spread(): lax.all_to_all(jnp.broadcast_to(block, (count,) + block.shape), axes, 0, 0)  15.1 us
    ppermute x9, waiting for transfers between devices, shift(): return lax.ppermute(block, axis, [(i, (i + k) % size) for i in range(size)])  12 us
    all_to_all x1, blocking collectives, spread(): lax.all_to_all(jnp.broadcast_to(block, (count,) + block.shape), axes, 0, 0)  11.1 us
    all_to_all x2, starting transfers between devices, spread(): lax.all_to_all(jnp.broadcast_to(block, (count,) + block.shape), axes, 0, 0)  7.78 us
    ppermute x1, starting transfers between devices, on_device(): from_pair = lax.ppermute(half_gram(1 - core), 'core', SWAP)  4.15 us
    ppermute x1, starting transfers between devices, on_device(): other_half = lax.ppermute(my_half, 'core', SWAP)  4.12 us
  transfers between devices with their start and end apart: 13, of which 10 were waited for; matrix products, arithmetic and copies ran while one was open for 4% of the time, Pallas kernels for 0%

profile of v2, /device:TPU:1, one launch (start us, length us, event | category | flops | bytes accessed | tf_op | source)
XLA Modules:
  0.0 87.3 jit_solution(15087902710016496109)
XLA Ops:
  0.6 1.0 %reduce_sum.90 = f32[512]{0:T(512)S(1)} reduce(f32[128,512]{1,0:T(8,128)} %param.1, f32[]{:T(128)} %constant.22.clone.1), dimensions={0}, to_apply=%region_0.0 | reduce | flops 65024 | bytes 264196 | tf_op jit(solution)/shard_map/reduce_sum | solution.py:41
  1.6 1.0 %multiply_reduce_fusion.2 = f32[512]{0:T(512)S(1)} fusion(f32[128,512]{1,0:T(8,128)} %param.1, f32[512]{0:T(512)S(1)} %broadcast_multiply_fusion.1), kind=kLoop, calls=%fused_computation.20 | loop fusion | flops 196096 | bytes 266240 | tf_op jit(solution)/shard_map/reduce_sum | solution.py:43
  2.7 11.1 %all_to_all.19 = f32[8,2,512]{2,1,0:T(2,128)S(1)} all-to-all(f32[8,2,512]{2,1,0:T(2,128)S(1)} %broadcast_in_dim.10), channel_id=1, replica_groups=mesh['zl'=2,'x'=4,'y'=4,'zh'=4,'core'=2] {'zl','x'}, dimensions={0} | all-to-all | bytes 65536 | tf_op jit(solution)/shard_map/all_to_all | solution.py:14
  13.8 1.0 %subtract_convert_fusion = bf16[128,512]{1,0:T(8,128)(2,1)S(1)} fusion(f32[128,512]{1,0:T(8,128)} %param.1, f32[512]{0:T(512)S(1)} %broadcast_multiply_fusion), kind=kLoop, calls=%fused_computation.21 | loop fusion | flops 131072 | bytes 395264 | tf_op jit(solution)/shard_map/convert_element_type | solution.py:52
  14.8 1.1 %broadcast_in_dim.22 = bf16[8,128,512]{2,1,0:T(8,128)(2,1)} broadcast(bf16[128,512]{1,0:T(8,128)(2,1)S(1)} %subtract_convert_fusion), dimensions={1,2} | broadcast | bytes 1179648 | tf_op jit(solution)/shard_map/broadcast_in_dim | solution.py:14
  15.9 3.6 %all-to-all-start.1 = ((bf16[8,128,512]{2,1,0:T(8,128)(2,1)}), bf16[8,128,512]{2,1,0:T(8,128)(2,1)S(1)}, u32[]{:S(2)}, u32[]{:S(2)}) async-start(bf16[8,128,512]{2,1,0:T(8,128)(2,1)} %broadcast_in_dim.22), calls=%async_computation.1 | async-start | bytes 2097152 | tf_op jit(solution)/shard_map/all_to_all | solution.py:14
  19.5 0.6 maximum_reduce_fusion
  20.8 10.3 %all-to-all-done.1 = bf16[8,128,512]{2,1,0:T(8,128)(2,1)S(1)} async-done(((bf16[8,128,512]{2,1,0:T(8,128)(2,1)}), bf16[8,128,512]{2,1,0:T(8,128)(2,1)S(1)}, u32[]{:S(2)}, u32[]{:S(2)}) %all-to-all-start.1) | async-done | bytes 1048608 | tf_op jit(solution)/shard_map/all_to_all | solution.py:14
  31.3 0.6 multiply_reduce_fusion.3
  33.1 4.1 %collective-permute-start = (f32[64,1152]{1,0:T(8,128)S(1)}, f32[64,1152]{1,0:T(8,128)S(1)}, u32[]{:S(2)}, u32[]{:S(2)}) collective-permute-start(f32[64,1152]{1,0:T(8,128)S(1)} %concatenate.24), channel_id=1, source_target_pairs={{0,1},{1,0},{2,3},{3,2},{4,5},{5,4},{6,7},{7,6},{8,9},{9,8},{10,11... | collective-permute-start | bytes 884744 | tf_op jit(solution)/shard_map/ppermute | solution.py:72
  37.6 0.8 collective-permute-done
  38.5 1.4 %collective-permute-start.2 = (f32[16,1152]{1,0:T(8,128)S(1)}, f32[16,1152]{1,0:T(8,128)S(1)}, u32[]{:S(2)}, u32[]{:S(2)}) collective-permute-start(f32[16,1152]{1,0:T(8,128)S(1)} %get-tuple-element.13), channel_id=1, source_target_pairs={{0,8},{8,16},{16,24},{24,0},{1,9},{9,17},{17,25},{25,1},{2,10},{10... | collective-permute-start | bytes 221192 | tf_op jit(solution)/shard_map/ppermute | solution.py:19
  39.8 1.5 %collective-permute-start.3 = (f32[16,1152]{1,0:T(8,128)S(1)}, f32[16,1152]{1,0:T(8,128)S(1)}, u32[]{:S(2)}, u32[]{:S(2)}) collective-permute-start(f32[16,1152]{1,0:T(8,128)S(1)} %get-tuple-element.14), channel_id=1, source_target_pairs={{0,24},{8,0},{16,8},{24,16},{1,25},{9,1},{17,9},{25,17},{2,26},{10... | collective-permute-start | bytes 221192 | tf_op jit(solution)/shard_map/ppermute | solution.py:19
  41.4 1.6 %collective-permute-start.1 = (f32[16,1152]{1,0:T(8,128)S(1)}, f32[16,1152]{1,0:T(8,128)S(1)}, u32[]{:S(2)}, u32[]{:S(2)}) collective-permute-start(f32[16,1152]{1,0:T(8,128)S(1)} %get-tuple-element.15), channel_id=1, source_target_pairs={{0,16},{8,24},{16,0},{24,8},{1,17},{9,25},{17,1},{25,9},{2,18},{10... | collective-permute-start | bytes 221192 | tf_op jit(solution)/shard_map/ppermute | solution.py:19
  42.9 0.4 collective-permute-done.2
  43.4 2.7 %collective-permute-done.1 = f32[16,1152]{1,0:T(8,128)S(1)} collective-permute-done((f32[16,1152]{1,0:T(8,128)S(1)}, f32[16,1152]{1,0:T(8,128)S(1)}, u32[]{:S(2)}, u32[]{:S(2)}) %collective-permute-start.1) | collective-permute-done | bytes 73760 | tf_op jit(solution)/shard_map/ppermute | solution.py:19
  46.1 5.2 %collective-permute-start.6 = (f32[16,1152]{1,0:T(8,128)S(1)}, f32[16,1152]{1,0:T(8,128)S(1)}, u32[]{:S(2)}, u32[]{:S(2)}) collective-permute-start(f32[16,1152]{1,0:T(8,128)S(1)} %slice_add_fusion.2), channel_id=1, source_target_pairs={{0,6},{2,0},{4,2},{6,4},{1,7},{3,1},{5,3},{7,5},{8,14},{10,8},{12,... | collective-permute-start | bytes 221192 | tf_op jit(solution)/shard_map/ppermute | solution.py:19
  51.3 3.3 %collective-permute-start.4 = (f32[16,1152]{1,0:T(8,128)S(1)}, f32[16,1152]{1,0:T(8,128)S(1)}, u32[]{:S(2)}, u32[]{:S(2)}) collective-permute-start(f32[16,1152]{1,0:T(8,128)S(1)} %slice_add_fusion.2), channel_id=1, source_target_pairs={{0,4},{2,6},{4,0},{6,2},{1,5},{3,7},{5,1},{7,3},{8,12},{10,14},{12... | collective-permute-start | bytes 221192 | tf_op jit(solution)/shard_map/ppermute | solution.py:19
  54.6 2.8 %collective-permute-done.5 = f32[16,1152]{1,0:T(8,128)S(1)} collective-permute-done((f32[16,1152]{1,0:T(8,128)S(1)}, f32[16,1152]{1,0:T(8,128)S(1)}, u32[]{:S(2)}, u32[]{:S(2)}) %collective-permute-start.5) | collective-permute-done | bytes 73760 | tf_op jit(solution)/shard_map/ppermute | solution.py:19
  57.4 2.5 %collective-permute-done.4 = f32[16,1152]{1,0:T(8,128)S(1)} collective-permute-done((f32[16,1152]{1,0:T(8,128)S(1)}, f32[16,1152]{1,0:T(8,128)S(1)}, u32[]{:S(2)}, u32[]{:S(2)}) %collective-permute-start.4) | collective-permute-done | bytes 73760 | tf_op jit(solution)/shard_map/ppermute | solution.py:19
  59.9 1.5 %collective-permute-start.7 = (f32[16,1024]{1,0:T(8,128)S(1)}, f32[16,1024]{1,0:T(8,128)S(1)}, u32[]{:S(2)}, u32[]{:S(2)}) collective-permute-start(f32[16,1024]{1,0:T(8,128)S(1)} %slice.54), channel_id=1, source_target_pairs={{0,24},{8,0},{16,8},{24,16},{1,25},{9,1},{17,9},{25,17},{2,26},{10... | collective-permute-start | bytes 196616 | tf_op jit(solution)/shard_map/ppermute | solution.py:19
  61.5 1.5 %collective-permute-start.8 = (f32[16,1024]{1,0:T(8,128)S(1)}, f32[16,1024]{1,0:T(8,128)S(1)}, u32[]{:S(2)}, u32[]{:S(2)}) collective-permute-start(f32[16,1024]{1,0:T(8,128)S(1)} %slice.54), channel_id=1, source_target_pairs={{0,16},{8,24},{16,0},{24,8},{1,17},{9,25},{17,1},{25,9},{2,18},{10... | collective-permute-start | bytes 196616 | tf_op jit(solution)/shard_map/ppermute | solution.py:19
  63.1 3.1 %collective-permute-done.8 = f32[16,1024]{1,0:T(8,128)S(1)} collective-permute-done((f32[16,1024]{1,0:T(8,128)S(1)}, f32[16,1024]{1,0:T(8,128)S(1)}, u32[]{:S(2)}, u32[]{:S(2)}) %collective-permute-start.8) | collective-permute-done | bytes 65568 | tf_op jit(solution)/shard_map/ppermute | solution.py:19
  66.6 0.7 multiply_reduce_fusion.1
  67.3 4.1 %collective-permute-start.10 = (f32[64,1024]{1,0:T(8,128)S(1)}, f32[64,1024]{1,0:T(8,128)S(1)}, u32[]{:S(2)}, u32[]{:S(2)}) collective-permute-start(f32[64,1024]{1,0:T(8,128)S(1)} %get-tuple-element.5), channel_id=1, source_target_pairs={{0,1},{1,0},{2,3},{3,2},{4,5},{5,4},{6,7},{7,6},{8,9},{9,8},{10,11... | collective-permute-start | bytes 786440 | tf_op jit(solution)/shard_map/ppermute | solution.py:82
  71.4 1.2 %broadcast_in_dim_broadcast_in_dim.3 = f32[16,1,128]{2,1,0:T(1,128)} broadcast(f32[]{:T(128)} %get-tuple-element.4), dimensions={} | broadcast | bytes 8196 | tf_op jit(solution)/shard_map/broadcast_in_dim;broadcast_in_dim | solution.py:14
  72.6 4.2 %all-to-all-start.2 = ((f32[16,1,128]{2,1,0:T(1,128)}), f32[16,1,128]{2,1,0:T(1,128)S(1)}, u32[]{:S(2)}, u32[]{:S(2)}) async-start(f32[16,1,128]{2,1,0:T(1,128)} %broadcast_in_dim_broadcast_in_dim.3), calls=%async_computation.2 | async-start | bytes 16384 | tf_op jit(solution)/shard_map/all_to_all | solution.py:14
  76.9 0.6 slice.59
  77.4 4.8 %all-to-all-done.2 = f32[16,1,128]{2,1,0:T(1,128)S(1)} async-done(((f32[16,1,128]{2,1,0:T(1,128)}), f32[16,1,128]{2,1,0:T(1,128)S(1)}, u32[]{:S(2)}, u32[]{:S(2)}) %all-to-all-start.2) | async-done | bytes 8224 | tf_op jit(solution)/shard_map/all_to_all | solution.py:14
  82.3 0.6 slice_reduce_fusion.2
  84.4 0.6 fusion
  85.4 0.8 fusion.9
  (36 shorter events, 2.4 us)
Async XLA Ops:
  15.9 15.2 %all-to-all-start.1 = ((bf16[8,128,512]{2,1,0:T(8,128)(2,1)}), bf16[8,128,512]{2,1,0:T(8,128)(2,1)S(1)}, u32[]{:S(2)}, u32[]{:S(2)}) async-start(bf16[8,128,512]{2,1,0:T(8,128)(2,1)} %broadcast_in_dim.22), calls=%async_computation.1 | async-start | bytes 2097152 | tf_op jit(solution)/shard_map/all_to_all | solution.py:14
  33.1 5.4 %collective-permute-start = (f32[64,1152]{1,0:T(8,128)S(1)}, f32[64,1152]{1,0:T(8,128)S(1)}, u32[]{:S(2)}, u32[]{:S(2)}) collective-permute-start(f32[64,1152]{1,0:T(8,128)S(1)} %concatenate.24), channel_id=1, source_target_pairs={{0,1},{1,0},{2,3},{3,2},{4,5},{5,4},{6,7},{7,6},{8,9},{9,8},{10,11... | collective-permute-start | bytes 884744 | tf_op jit(solution)/shard_map/ppermute | solution.py:72
  38.5 4.9 %collective-permute-start.2 = (f32[16,1152]{1,0:T(8,128)S(1)}, f32[16,1152]{1,0:T(8,128)S(1)}, u32[]{:S(2)}, u32[]{:S(2)}) collective-permute-start(f32[16,1152]{1,0:T(8,128)S(1)} %get-tuple-element.13), channel_id=1, source_target_pairs={{0,8},{8,16},{16,24},{24,0},{1,9},{9,17},{17,25},{25,1},{2,10},{10... | collective-permute-start | bytes 221192 | tf_op jit(solution)/shard_map/ppermute | solution.py:19
  39.8 3.5 %collective-permute-start.3 = (f32[16,1152]{1,0:T(8,128)S(1)}, f32[16,1152]{1,0:T(8,128)S(1)}, u32[]{:S(2)}, u32[]{:S(2)}) collective-permute-start(f32[16,1152]{1,0:T(8,128)S(1)} %get-tuple-element.14), channel_id=1, source_target_pairs={{0,24},{8,0},{16,8},{24,16},{1,25},{9,1},{17,9},{25,17},{2,26},{10... | collective-permute-start | bytes 221192 | tf_op jit(solution)/shard_map/ppermute | solution.py:19
  41.4 4.7 %collective-permute-start.1 = (f32[16,1152]{1,0:T(8,128)S(1)}, f32[16,1152]{1,0:T(8,128)S(1)}, u32[]{:S(2)}, u32[]{:S(2)}) collective-permute-start(f32[16,1152]{1,0:T(8,128)S(1)} %get-tuple-element.15), channel_id=1, source_target_pairs={{0,16},{8,24},{16,0},{24,8},{1,17},{9,25},{17,1},{25,9},{2,18},{10... | collective-permute-start | bytes 221192 | tf_op jit(solution)/shard_map/ppermute | solution.py:19
  46.1 8.5 %collective-permute-start.6 = (f32[16,1152]{1,0:T(8,128)S(1)}, f32[16,1152]{1,0:T(8,128)S(1)}, u32[]{:S(2)}, u32[]{:S(2)}) collective-permute-start(f32[16,1152]{1,0:T(8,128)S(1)} %slice_add_fusion.2), channel_id=1, source_target_pairs={{0,6},{2,0},{4,2},{6,4},{1,7},{3,1},{5,3},{7,5},{8,14},{10,8},{12,... | collective-permute-start | bytes 221192 | tf_op jit(solution)/shard_map/ppermute | solution.py:19
  51.3 6.1 %collective-permute-start.5 = (f32[16,1152]{1,0:T(8,128)S(1)}, f32[16,1152]{1,0:T(8,128)S(1)}, u32[]{:S(2)}, u32[]{:S(2)}) collective-permute-start(f32[16,1152]{1,0:T(8,128)S(1)} %slice_add_fusion.2), channel_id=1, source_target_pairs={{0,2},{2,4},{4,6},{6,0},{1,3},{3,5},{5,7},{7,1},{8,10},{10,12},{12... | collective-permute-start | bytes 221192 | tf_op jit(solution)/shard_map/ppermute | solution.py:19
  51.3 8.6 %collective-permute-start.4 = (f32[16,1152]{1,0:T(8,128)S(1)}, f32[16,1152]{1,0:T(8,128)S(1)}, u32[]{:S(2)}, u32[]{:S(2)}) collective-permute-start(f32[16,1152]{1,0:T(8,128)S(1)} %slice_add_fusion.2), channel_id=1, source_target_pairs={{0,4},{2,6},{4,0},{6,2},{1,5},{3,7},{5,1},{7,3},{8,12},{10,14},{12... | collective-permute-start | bytes 221192 | tf_op jit(solution)/shard_map/ppermute | solution.py:19
  59.9 3.2 %collective-permute-start.7 = (f32[16,1024]{1,0:T(8,128)S(1)}, f32[16,1024]{1,0:T(8,128)S(1)}, u32[]{:S(2)}, u32[]{:S(2)}) collective-permute-start(f32[16,1024]{1,0:T(8,128)S(1)} %slice.54), channel_id=1, source_target_pairs={{0,24},{8,0},{16,8},{24,16},{1,25},{9,1},{17,9},{25,17},{2,26},{10... | collective-permute-start | bytes 196616 | tf_op jit(solution)/shard_map/ppermute | solution.py:19
  61.5 5.0 %collective-permute-start.9 = (f32[16,1024]{1,0:T(8,128)S(1)}, f32[16,1024]{1,0:T(8,128)S(1)}, u32[]{:S(2)}, u32[]{:S(2)}) collective-permute-start(f32[16,1024]{1,0:T(8,128)S(1)} %slice.54), channel_id=1, source_target_pairs={{0,8},{8,16},{16,24},{24,0},{1,9},{9,17},{17,25},{25,1},{2,10},{10... | collective-permute-start | bytes 196616 | tf_op jit(solution)/shard_map/ppermute | solution.py:19
  61.5 4.7 %collective-permute-start.8 = (f32[16,1024]{1,0:T(8,128)S(1)}, f32[16,1024]{1,0:T(8,128)S(1)}, u32[]{:S(2)}, u32[]{:S(2)}) collective-permute-start(f32[16,1024]{1,0:T(8,128)S(1)} %slice.54), channel_id=1, source_target_pairs={{0,16},{8,24},{16,0},{24,8},{1,17},{9,25},{17,1},{25,9},{2,18},{10... | collective-permute-start | bytes 196616 | tf_op jit(solution)/shard_map/ppermute | solution.py:19
  67.3 16.9 %collective-permute-start.10 = (f32[64,1024]{1,0:T(8,128)S(1)}, f32[64,1024]{1,0:T(8,128)S(1)}, u32[]{:S(2)}, u32[]{:S(2)}) collective-permute-start(f32[64,1024]{1,0:T(8,128)S(1)} %get-tuple-element.5), channel_id=1, source_target_pairs={{0,1},{1,0},{2,3},{3,2},{4,5},{5,4},{6,7},{7,6},{8,9},{9,8},{10,11... | collective-permute-start | bytes 786440 | tf_op jit(solution)/shard_map/ppermute | solution.py:82
  72.6 9.6 %all-to-all-start.2 = ((f32[16,1,128]{2,1,0:T(1,128)}), f32[16,1,128]{2,1,0:T(1,128)S(1)}, u32[]{:S(2)}, u32[]{:S(2)}) async-start(f32[16,1,128]{2,1,0:T(1,128)} %broadcast_in_dim_broadcast_in_dim.3), calls=%async_computation.2 | async-start | bytes 16384 | tf_op jit(solution)/shard_map/all_to_all | solution.py:14
  84.4 1.0 %copy-start = (f32[128,512]{1,0:T(8,128)S(1)}, f32[128,512]{1,0:T(8,128)}, u32[]{:S(2)}) copy-start(f32[128,512]{1,0:T(8,128)} %param.1) | copy-start | bytes 786436

commit v3 on v2

--- a/solution.py
+++ b/solution.py
@@ -27,6 +27,10 @@
     return jnp.concatenate([high.astype(BF16), mid.astype(BF16), low.astype(BF16)], axis=0)
 
 
+def lanes(a):
+    return jnp.sum(a.reshape(-1, 128), axis=0)
+
+
 def on_device(embeddings):
     rows_here, col_width = embeddings.shape
     rows_count = lax.axis_size(ROWS)
@@ -52,48 +56,49 @@
     centered = cz.astype(BF16)
     gathered = spread(centered, ROWS, rows_count).reshape(n_all, col_width)
 
-    gathered_f32 = gathered.astype(F32)
-    col_norms = jnp.sum(gathered_f32 * gathered_f32, axis=0)
-    block_share = (
-        25.0 * jnp.sum(jax.nn.relu(1.0 - std)) - jnp.sum(col_norms * col_norms) / (scale * scale)
-    ) / width
-
     half = rows_here // 2
     piece = half // ys
 
     def half_gram(which):
         own = lax.dynamic_slice_in_dim(centered, which * half, half, 0)
         own = lax.dynamic_slice_in_dim(jnp.concatenate([own, own]), y * piece, half, 0)
-        gram = lax.dot_general(
+        return lax.dot_general(
             own, gathered, (((1,), (1,)), ((), ())), preferred_element_type=F32
         )
-        return jnp.concatenate([gram, jnp.full((half, 128), block_share)], axis=1)
 
     from_pair = lax.ppermute(half_gram(1 - core), "core", SWAP)
     chip_half = half_gram(core) + from_pair
     chunks = [chip_half[k * piece : (k + 1) * piece] for k in range(ys)]
     over_y = chunks[0] + sum(shift(chunks[k], "y", k) for k in (2, 1, 3))
+
+    gathered_f32 = gathered.astype(F32)
+    col_norms = jnp.sum(gathered_f32 * gathered_f32, axis=0)
+    block_share = (
+        25.0 * lanes(jax.nn.relu(1.0 - std)) - lanes(col_norms * col_norms) / (scale * scale)
+    ) / (width * rows_count)
+    over_y = jnp.concatenate([over_y, jnp.broadcast_to(block_share, (piece, 128))], axis=1)
     mine = over_y + sum(shift(over_y, "zh", k) for k in (2, 1, 3))
-    blocks_share = mine[0, n_all]
-    mine = mine[:, :n_all]
-    back = {k: shift(mine, "y", k) for k in (2, 1, 3)}
-    around = jnp.concatenate([back[3], back[2], back[1], mine] * 2)
-    my_half = lax.dynamic_slice_in_dim(around, (ys - 1 - y) * piece, half, 0)
+    blocks = [mine] + [shift(mine, "y", k) for k in (1, 2, 3)]
+    my_half = jnp.concatenate([block[:, :n_all] for block in blocks])
     other_half = lax.ppermute(my_half, "core", SWAP)
+    blocks_share = sum(block[0, n_all:] for block in blocks)
+    share = lanes(my_half * my_half) / (scale * scale * width) + blocks_share
+    shares = spread(share, ROWS + ("core",), rows_count * 2)
 
-    norm_here = jnp.sum(my_half * my_half)
-    norms = spread(jnp.full((128,), norm_here), ROWS + ("core",), 2 * rows_count)
-    norm = jnp.sum(norms[:, 0])
-    loss = norm / (scale * scale * width) + blocks_share
-
-    first = jnp.where(core == 0, my_half, other_half)
-    second = jnp.where(core == 0, other_half, my_half)
-    gram = jnp.concatenate([first, second], axis=0)
+    gram = jnp.zeros((rows_here, n_all), F32)
+    for k in range(ys):
+        owner = lax.rem(y + ys - k, ys)
+        for c, rows in enumerate((my_half, other_half)):
+            block = rows[k * piece : (k + 1) * piece]
+            start = lax.rem(core + c, 2) * half + owner * piece
+            gram = lax.dynamic_update_slice_in_dim(gram, block, start, 0)
     terms = jnp.dot(three_terms(gram), gathered, preferred_element_type=F32)
     product = terms[:rows_here] + terms[rows_here : 2 * rows_here] + terms[2 * rows_here :]
     grad_cov = (product - centered.astype(F32) * col_norms) / scale
     hinge = jnp.where(std < 1.0, cz / std, F32(0.0))
-    return (4.0 / 25.0 * grad_cov - hinge, loss)
+    grad_scaled = 4.0 / 25.0 * grad_cov - hinge
+    grad_scaled, shares = lax.optimization_barrier((grad_scaled, shares))
+    return (grad_scaled, jnp.sum(shares))
 
 
 def solution(mesh):

time: 87.7 us -> 80.4 us (0.917)
  waiting for transfers between devices: 27.8 us -> 23.1 us
  starting transfers between devices: 32 us -> 36.1 us
  between operations: 4.58 us -> 0.83 us
  other arithmetic: 6.9 us -> 5.12 us
  local copies, waits for them, and re-layouts: 3.43 us -> 2.31 us
    ppermute x9, waiting for transfers between devices: 12 us -> 7.32 us  [shift(): return lax.ppermute(block, axis, [(i, (i + k) % size) for i in range(size)])]
    ppermute x9, starting transfers between devices: 16 us -> 19.8 us  [shift(): return lax.ppermute(block, axis, [(i, (i + k) % size) for i in range(size)])]
    reduce_sum x4, other arithmetic: 2.48 us -> 0.72 us  [the longest x1 0.6 us: on_device(): return (grad_scaled, jnp.sum(shares))]
    another operation x1 -> x0, local copies, waits for them, and re-layouts: 1.25 us -> none  [spread(): jnp.broadcast_to(block, (count,) + block.shape)]
  transfers between devices with their start and end apart: 13 -> 13, of which waited for: 10 -> 8; matrix products, arithmetic and copies ran while one was open for 4% -> 3% of each run, Pallas kernels for 0% -> 0%
where the time goes in v3:
time: 80.4 us; the launch traced here: 80 us
  starting transfers between devices  36.1 us (45%)
  waiting for transfers between devices  23.1 us (29%)
  blocking collectives  11.1 us (14%)
  other arithmetic  5.12 us (6%)
  local copies, waits for them, and re-layouts  2.31 us (3%)
  matrix products  1.41 us (2%)
  between operations  0.83 us (1%)
    ppermute x9, starting transfers between devices, shift(): return lax.ppermute(block, axis, [(i, (i + k) % size) for i in range(size)])  19.8 us
    all_to_all x2, waiting for transfers between devices, spread(): lax.all_to_all(jnp.broadcast_to(block, (count,) + block.shape), axes, 0, 0)  14.9 us
    all_to_all x1, blocking collectives, spread(): lax.all_to_all(jnp.broadcast_to(block, (count,) + block.shape), axes, 0, 0)  11.1 us
    all_to_all x2, starting transfers between devices, spread(): lax.all_to_all(jnp.broadcast_to(block, (count,) + block.shape), axes, 0, 0)  7.66 us
    ppermute x9, waiting for transfers between devices, shift(): return lax.ppermute(block, axis, [(i, (i + k) % size) for i in range(size)])  7.32 us
    ppermute x1, starting transfers between devices, on_device(): other_half = lax.ppermute(my_half, 'core', SWAP)  4.53 us
    ppermute x1, starting transfers between devices, on_device(): from_pair = lax.ppermute(half_gram(1 - core), 'core', SWAP)  4.15 us
    broadcast_in_dim x3, local copies, waits for them, and re-layouts, spread(): jnp.broadcast_to(block, (count,) + block.shape)  1.7 us
  transfers between devices with their start and end apart: 13, of which 8 were waited for; matrix products, arithmetic and copies ran while one was open for 3% of the time, Pallas kernels for 0%

profile of v3, /device:TPU:1, one launch (start us, length us, event | category | flops | bytes accessed | tf_op | source)
XLA Modules:
  0.0 80.0 jit_solution(4857269313664955853)
XLA Ops:
  0.6 1.0 %reduce_sum.90 = f32[512]{0:T(512)S(1)} reduce(f32[128,512]{1,0:T(8,128)} %param.1, f32[]{:T(128)} %constant.58.clone.1), dimensions={0}, to_apply=%region_0.0 | reduce | flops 65024 | bytes 264196 | tf_op jit(solution)/shard_map/reduce_sum | solution.py:45
  1.6 1.0 %multiply_reduce_fusion.1 = f32[512]{0:T(512)S(1)} fusion(f32[128,512]{1,0:T(8,128)} %param.1, f32[512]{0:T(512)S(1)} %broadcast_multiply_fusion.1), kind=kLoop, calls=%fused_computation.19 | loop fusion | flops 196096 | bytes 266240 | tf_op jit(solution)/shard_map/reduce_sum | solution.py:47
  2.7 11.1 %all_to_all.19 = f32[8,2,512]{2,1,0:T(2,128)S(1)} all-to-all(f32[8,2,512]{2,1,0:T(2,128)S(1)} %broadcast_in_dim.29), channel_id=1, replica_groups=mesh['zl'=2,'x'=4,'y'=4,'zh'=4,'core'=2] {'zl','x'}, dimensions={0} | all-to-all | bytes 65536 | tf_op jit(solution)/shard_map/all_to_all | solution.py:14
  13.8 1.0 %subtract_convert_fusion = bf16[128,512]{1,0:T(8,128)(2,1)S(1)} fusion(f32[128,512]{1,0:T(8,128)} %param.1, f32[512]{0:T(512)S(1)} %broadcast_multiply_fusion), kind=kLoop, calls=%fused_computation.20 | loop fusion | flops 131072 | bytes 395264 | tf_op jit(solution)/shard_map/convert_element_type | solution.py:56
  14.8 1.1 %broadcast_in_dim.30 = bf16[8,128,512]{2,1,0:T(8,128)(2,1)} broadcast(bf16[128,512]{1,0:T(8,128)(2,1)S(1)} %subtract_convert_fusion), dimensions={1,2} | broadcast | bytes 1179648 | tf_op jit(solution)/shard_map/broadcast_in_dim | solution.py:14
  15.9 3.6 %all-to-all-start.1 = ((bf16[8,128,512]{2,1,0:T(8,128)(2,1)}), bf16[8,128,512]{2,1,0:T(8,128)(2,1)S(1)}, u32[]{:S(2)}, u32[]{:S(2)}) async-start(bf16[8,128,512]{2,1,0:T(8,128)(2,1)} %broadcast_in_dim.30), calls=%async_computation.1 | async-start | bytes 2097152 | tf_op jit(solution)/shard_map/all_to_all | solution.py:14
  19.5 11.5 %all-to-all-done.1 = bf16[8,128,512]{2,1,0:T(8,128)(2,1)S(1)} async-done(((bf16[8,128,512]{2,1,0:T(8,128)(2,1)}), bf16[8,128,512]{2,1,0:T(8,128)(2,1)S(1)}, u32[]{:S(2)}, u32[]{:S(2)}) %all-to-all-start.1) | async-done | bytes 1048608 | tf_op jit(solution)/shard_map/all_to_all | solution.py:14
  31.1 0.4 fusion.11
  31.5 4.1 %collective-permute-start = (f32[64,1024]{1,0:T(8,128)S(1)}, f32[64,1024]{1,0:T(8,128)S(1)}, u32[]{:S(2)}, u32[]{:S(2)}) collective-permute-start(f32[64,1024]{1,0:T(8,128)S(1)} %fusion.11), channel_id=1, source_target_pairs={{0,1},{1,0},{2,3},{3,2},{4,5},{5,4},{6,7},{7,6},{8,9},{9,8},{10,11... | collective-permute-start | bytes 786440 | tf_op jit(solution)/shard_map/ppermute | solution.py:69
  35.9 0.9 %collective-permute-done = f32[64,1024]{1,0:T(8,128)S(1)} collective-permute-done((f32[64,1024]{1,0:T(8,128)S(1)}, f32[64,1024]{1,0:T(8,128)S(1)}, u32[]{:S(2)}, u32[]{:S(2)}) %collective-permute-start) | collective-permute-done | bytes 262176 | tf_op jit(solution)/shard_map/ppermute | solution.py:69
  36.8 0.4 convolution_add_fusion
  37.2 3.0 %collective-permute-start.1 = (f32[16,1024]{1,0:T(8,128)S(1)}, f32[16,1024]{1,0:T(8,128)S(1)}, u32[]{:S(2)}, u32[]{:S(2)}) collective-permute-start(f32[16,1024]{1,0:T(8,128)S(1)} %get-tuple-element.17), channel_id=1, source_target_pairs={{0,16},{8,24},{16,0},{24,8},{1,17},{9,25},{17,1},{25,9},{2,18},{10... | collective-permute-start | bytes 196616 | tf_op jit(solution)/shard_map/ppermute | solution.py:19
  40.2 0.4 collective-permute-start.2
  40.6 2.3 %collective-permute-start.3 = (f32[16,1024]{1,0:T(8,128)S(1)}, f32[16,1024]{1,0:T(8,128)S(1)}, u32[]{:S(2)}, u32[]{:S(2)}) collective-permute-start(f32[16,1024]{1,0:T(8,128)S(1)} %get-tuple-element.16), channel_id=1, source_target_pairs={{0,24},{8,0},{16,8},{24,16},{1,25},{9,1},{17,9},{25,17},{2,26},{10... | collective-permute-start | bytes 196616 | tf_op jit(solution)/shard_map/ppermute | solution.py:19
  42.9 1.6 %collective-permute-done.2 = f32[16,1024]{1,0:T(8,128)S(1)} collective-permute-done((f32[16,1024]{1,0:T(8,128)S(1)}, f32[16,1024]{1,0:T(8,128)S(1)}, u32[]{:S(2)}, u32[]{:S(2)}) %collective-permute-start.2) | collective-permute-done | bytes 65568 | tf_op jit(solution)/shard_map/ppermute | solution.py:19
  44.6 6.1 %collective-permute-start.4 = (f32[16,1152]{1,0:T(8,128)S(1)}, f32[16,1152]{1,0:T(8,128)S(1)}, u32[]{:S(2)}, u32[]{:S(2)}) collective-permute-start(f32[16,1152]{1,0:T(8,128)S(1)} %pad_maximum_fusion.1), channel_id=1, source_target_pairs={{0,4},{2,6},{4,0},{6,2},{1,5},{3,7},{5,1},{7,3},{8,12},{10,14},{12... | collective-permute-start | bytes 221192 | tf_op jit(solution)/shard_map/ppermute | solution.py:19
  50.7 1.2 %collective-permute-start.5 = (f32[16,1152]{1,0:T(8,128)S(1)}, f32[16,1152]{1,0:T(8,128)S(1)}, u32[]{:S(2)}, u32[]{:S(2)}) collective-permute-start(f32[16,1152]{1,0:T(8,128)S(1)} %pad_maximum_fusion.1), channel_id=1, source_target_pairs={{0,2},{2,4},{4,6},{6,0},{1,3},{3,5},{5,7},{7,1},{8,10},{10,12},{12... | collective-permute-start | bytes 221192 | tf_op jit(solution)/shard_map/ppermute | solution.py:19
  51.9 2.4 %collective-permute-start.6 = (f32[16,1152]{1,0:T(8,128)S(1)}, f32[16,1152]{1,0:T(8,128)S(1)}, u32[]{:S(2)}, u32[]{:S(2)}) collective-permute-start(f32[16,1152]{1,0:T(8,128)S(1)} %pad_maximum_fusion.1), channel_id=1, source_target_pairs={{0,6},{2,0},{4,2},{6,4},{1,7},{3,1},{5,3},{7,5},{8,14},{10,8},{12,... | collective-permute-start | bytes 221192 | tf_op jit(solution)/shard_map/ppermute | solution.py:19
  54.3 2.6 %collective-permute-done.5 = f32[16,1152]{1,0:T(8,128)S(1)} collective-permute-done((f32[16,1152]{1,0:T(8,128)S(1)}, f32[16,1152]{1,0:T(8,128)S(1)}, u32[]{:S(2)}, u32[]{:S(2)}) %collective-permute-start.5) | collective-permute-done | bytes 73760 | tf_op jit(solution)/shard_map/ppermute | solution.py:19
  56.9 1.9 %collective-permute-start.7 = (f32[16,1152]{1,0:T(8,128)S(1)}, f32[16,1152]{1,0:T(8,128)S(1)}, u32[]{:S(2)}, u32[]{:S(2)}) collective-permute-start(f32[16,1152]{1,0:T(8,128)S(1)} %add_add_fusion), channel_id=1, source_target_pairs={{0,8},{8,16},{16,24},{24,0},{1,9},{9,17},{17,25},{25,1},{2,10},{10... | collective-permute-start | bytes 221192 | tf_op jit(solution)/shard_map/ppermute | solution.py:19
  58.8 2.2 %collective-permute-start.8 = (f32[16,1152]{1,0:T(8,128)S(1)}, f32[16,1152]{1,0:T(8,128)S(1)}, u32[]{:S(2)}, u32[]{:S(2)}) collective-permute-start(f32[16,1152]{1,0:T(8,128)S(1)} %add_add_fusion), channel_id=1, source_target_pairs={{0,16},{8,24},{16,0},{24,8},{1,17},{9,25},{17,1},{25,9},{2,18},{10... | collective-permute-start | bytes 221192 | tf_op jit(solution)/shard_map/ppermute | solution.py:19
  61.0 0.3 collective-permute-start.9
  61.6 2.0 %collective-permute-done.8 = f32[16,1152]{1,0:T(8,128)S(1)} collective-permute-done((f32[16,1152]{1,0:T(8,128)S(1)}, f32[16,1152]{1,0:T(8,128)S(1)}, u32[]{:S(2)}, u32[]{:S(2)}) %collective-permute-start.8) | collective-permute-done | bytes 73760 | tf_op jit(solution)/shard_map/ppermute | solution.py:19
  63.6 1.0 %collective-permute-done.9 = f32[16,1152]{1,0:T(8,128)S(1)} collective-permute-done((f32[16,1152]{1,0:T(8,128)S(1)}, f32[16,1152]{1,0:T(8,128)S(1)}, u32[]{:S(2)}, u32[]{:S(2)}) %collective-permute-start.9) | collective-permute-done | bytes 73760 | tf_op jit(solution)/shard_map/ppermute | solution.py:19
  64.6 4.5 %collective-permute-start.10 = (f32[64,1024]{1,0:T(8,128)S(1)}, f32[64,1024]{1,0:T(8,128)S(1)}, u32[]{:S(2)}, u32[]{:S(2)}) collective-permute-start(f32[64,1024]{1,0:T(8,128)S(1)} %get-tuple-element.14), channel_id=1, source_target_pairs={{0,1},{1,0},{2,3},{3,2},{4,5},{5,4},{6,7},{7,6},{8,9},{9,8},{10,11... | collective-permute-start | bytes 786440 | tf_op jit(solution)/shard_map/ppermute | solution.py:83
  69.2 0.6 broadcast_in_dim.34
  69.8 4.1 %all-to-all-start.2 = ((f32[16,1,128]{2,1,0:T(1,128)}), f32[16,1,128]{2,1,0:T(1,128)S(1)}, u32[]{:S(2)}, u32[]{:S(2)}) async-start(f32[16,1,128]{2,1,0:T(1,128)} %broadcast_in_dim.34), calls=%async_computation.2 | async-start | bytes 16384 | tf_op jit(solution)/shard_map/all_to_all | solution.py:14
  74.2 0.6 fusion
  74.8 0.4 copy-done
  75.2 0.8 %fusion.9 = f32[128,512]{1,0:T(8,128)} fusion(f32[384,512]{1,0:T(8,128)S(1)} %fusion, f32[128,512]{1,0:T(8,128)S(1)} %copy-done, f32[512]{0:T(512)S(1)} %get-tuple-element.9, f32[512]{0:T(512)S(1)} %multiply_reduce_fusion, f32[512]{0:T(512)S(1)} %broadcast_multiply_fusion, pred[512]{0:T(512)(128)(4,1)S(1)} %get-tuple-element.8), kind=kLoop, calls=%fused_computation.16 | loop fusion | flops 720896 | bytes 1317376 | tf_op jit(solution)/shard_map/sub | solution.py:99
  76.0 3.4 %all-to-all-done.2 = f32[16,1,128]{2,1,0:T(1,128)S(1)} async-done(((f32[16,1,128]{2,1,0:T(1,128)}), f32[16,1,128]{2,1,0:T(1,128)S(1)}, u32[]{:S(2)}, u32[]{:S(2)}) %all-to-all-start.2) | async-done | bytes 8224 | tf_op jit(solution)/shard_map/all_to_all | solution.py:14
  79.4 0.6 reduce_sum.99
  (41 shorter events, 1.2 us)
Async XLA Ops:
  15.9 15.2 %all-to-all-start.1 = ((bf16[8,128,512]{2,1,0:T(8,128)(2,1)}), bf16[8,128,512]{2,1,0:T(8,128)(2,1)S(1)}, u32[]{:S(2)}, u32[]{:S(2)}) async-start(bf16[8,128,512]{2,1,0:T(8,128)(2,1)} %broadcast_in_dim.30), calls=%async_computation.1 | async-start | bytes 2097152 | tf_op jit(solution)/shard_map/all_to_all | solution.py:14
  31.5 5.3 %collective-permute-start = (f32[64,1024]{1,0:T(8,128)S(1)}, f32[64,1024]{1,0:T(8,128)S(1)}, u32[]{:S(2)}, u32[]{:S(2)}) collective-permute-start(f32[64,1024]{1,0:T(8,128)S(1)} %fusion.11), channel_id=1, source_target_pairs={{0,1},{1,0},{2,3},{3,2},{4,5},{5,4},{6,7},{7,6},{8,9},{9,8},{10,11... | collective-permute-start | bytes 786440 | tf_op jit(solution)/shard_map/ppermute | solution.py:69
  37.2 5.7 %collective-permute-start.1 = (f32[16,1024]{1,0:T(8,128)S(1)}, f32[16,1024]{1,0:T(8,128)S(1)}, u32[]{:S(2)}, u32[]{:S(2)}) collective-permute-start(f32[16,1024]{1,0:T(8,128)S(1)} %get-tuple-element.17), channel_id=1, source_target_pairs={{0,16},{8,24},{16,0},{24,8},{1,17},{9,25},{17,1},{25,9},{2,18},{10... | collective-permute-start | bytes 196616 | tf_op jit(solution)/shard_map/ppermute | solution.py:19
  40.2 4.3 %collective-permute-start.2 = (f32[16,1024]{1,0:T(8,128)S(1)}, f32[16,1024]{1,0:T(8,128)S(1)}, u32[]{:S(2)}, u32[]{:S(2)}) collective-permute-start(f32[16,1024]{1,0:T(8,128)S(1)} %get-tuple-element.15), channel_id=1, source_target_pairs={{0,8},{8,16},{16,24},{24,0},{1,9},{9,17},{17,25},{25,1},{2,10},{10... | collective-permute-start | bytes 196616 | tf_op jit(solution)/shard_map/ppermute | solution.py:19
  40.6 3.9 %collective-permute-start.3 = (f32[16,1024]{1,0:T(8,128)S(1)}, f32[16,1024]{1,0:T(8,128)S(1)}, u32[]{:S(2)}, u32[]{:S(2)}) collective-permute-start(f32[16,1024]{1,0:T(8,128)S(1)} %get-tuple-element.16), channel_id=1, source_target_pairs={{0,24},{8,0},{16,8},{24,16},{1,25},{9,1},{17,9},{25,17},{2,26},{10... | collective-permute-start | bytes 196616 | tf_op jit(solution)/shard_map/ppermute | solution.py:19
  44.6 9.7 %collective-permute-start.4 = (f32[16,1152]{1,0:T(8,128)S(1)}, f32[16,1152]{1,0:T(8,128)S(1)}, u32[]{:S(2)}, u32[]{:S(2)}) collective-permute-start(f32[16,1152]{1,0:T(8,128)S(1)} %pad_maximum_fusion.1), channel_id=1, source_target_pairs={{0,4},{2,6},{4,0},{6,2},{1,5},{3,7},{5,1},{7,3},{8,12},{10,14},{12... | collective-permute-start | bytes 221192 | tf_op jit(solution)/shard_map/ppermute | solution.py:19
  50.7 6.2 %collective-permute-start.5 = (f32[16,1152]{1,0:T(8,128)S(1)}, f32[16,1152]{1,0:T(8,128)S(1)}, u32[]{:S(2)}, u32[]{:S(2)}) collective-permute-start(f32[16,1152]{1,0:T(8,128)S(1)} %pad_maximum_fusion.1), channel_id=1, source_target_pairs={{0,2},{2,4},{4,6},{6,0},{1,3},{3,5},{5,7},{7,1},{8,10},{10,12},{12... | collective-permute-start | bytes 221192 | tf_op jit(solution)/shard_map/ppermute | solution.py:19
  51.9 5.0 %collective-permute-start.6 = (f32[16,1152]{1,0:T(8,128)S(1)}, f32[16,1152]{1,0:T(8,128)S(1)}, u32[]{:S(2)}, u32[]{:S(2)}) collective-permute-start(f32[16,1152]{1,0:T(8,128)S(1)} %pad_maximum_fusion.1), channel_id=1, source_target_pairs={{0,6},{2,0},{4,2},{6,4},{1,7},{3,1},{5,3},{7,5},{8,14},{10,8},{12,... | collective-permute-start | bytes 221192 | tf_op jit(solution)/shard_map/ppermute | solution.py:19
  56.9 4.7 %collective-permute-start.7 = (f32[16,1152]{1,0:T(8,128)S(1)}, f32[16,1152]{1,0:T(8,128)S(1)}, u32[]{:S(2)}, u32[]{:S(2)}) collective-permute-start(f32[16,1152]{1,0:T(8,128)S(1)} %add_add_fusion), channel_id=1, source_target_pairs={{0,8},{8,16},{16,24},{24,0},{1,9},{9,17},{17,25},{25,1},{2,10},{10... | collective-permute-start | bytes 221192 | tf_op jit(solution)/shard_map/ppermute | solution.py:19
  58.8 4.7 %collective-permute-start.8 = (f32[16,1152]{1,0:T(8,128)S(1)}, f32[16,1152]{1,0:T(8,128)S(1)}, u32[]{:S(2)}, u32[]{:S(2)}) collective-permute-start(f32[16,1152]{1,0:T(8,128)S(1)} %add_add_fusion), channel_id=1, source_target_pairs={{0,16},{8,24},{16,0},{24,8},{1,17},{9,25},{17,1},{25,9},{2,18},{10... | collective-permute-start | bytes 221192 | tf_op jit(solution)/shard_map/ppermute | solution.py:19
  61.0 3.5 %collective-permute-start.9 = (f32[16,1152]{1,0:T(8,128)S(1)}, f32[16,1152]{1,0:T(8,128)S(1)}, u32[]{:S(2)}, u32[]{:S(2)}) collective-permute-start(f32[16,1152]{1,0:T(8,128)S(1)} %add_add_fusion), channel_id=1, source_target_pairs={{0,24},{8,0},{16,8},{24,16},{1,25},{9,1},{17,9},{25,17},{2,26},{10... | collective-permute-start | bytes 221192 | tf_op jit(solution)/shard_map/ppermute | solution.py:19
  64.6 9.4 %collective-permute-start.10 = (f32[64,1024]{1,0:T(8,128)S(1)}, f32[64,1024]{1,0:T(8,128)S(1)}, u32[]{:S(2)}, u32[]{:S(2)}) collective-permute-start(f32[64,1024]{1,0:T(8,128)S(1)} %get-tuple-element.14), channel_id=1, source_target_pairs={{0,1},{1,0},{2,3},{3,2},{4,5},{5,4},{6,7},{7,6},{8,9},{9,8},{10,11... | collective-permute-start | bytes 786440 | tf_op jit(solution)/shard_map/ppermute | solution.py:83
  69.8 9.6 %all-to-all-start.2 = ((f32[16,1,128]{2,1,0:T(1,128)}), f32[16,1,128]{2,1,0:T(1,128)S(1)}, u32[]{:S(2)}, u32[]{:S(2)}) async-start(f32[16,1,128]{2,1,0:T(1,128)} %broadcast_in_dim.34), calls=%async_computation.2 | async-start | bytes 16384 | tf_op jit(solution)/shard_map/all_to_all | solution.py:14
  74.2 1.0 %copy-start = (f32[128,512]{1,0:T(8,128)S(1)}, f32[128,512]{1,0:T(8,128)}, u32[]{:S(2)}) copy-start(f32[128,512]{1,0:T(8,128)} %param.1) | copy-start | bytes 786436

commit v4 on v3

--- a/solution.py
+++ b/solution.py
@@ -1,6 +1,8 @@
 import jax
 import jax.numpy as jnp
 from jax import lax
+from jax.experimental import pallas as pl
+from jax.experimental.pallas import tpu as pltpu
 from jax.sharding import Mesh
 from jax.sharding import PartitionSpec as P
 
@@ -17,6 +19,36 @@
 def shift(block, axis, k):
     size = lax.axis_size(axis)
     return lax.ppermute(block, axis, [(i, (i + k) % size) for i in range(size)])
+
+
+RAW_MOVES = ((1, 0), (0, 1), (0, 3))
+
+
+def move(block, along_zl, along_x):
+    zls, xs = lax.axis_size("zl"), lax.axis_size("x")
+    return lax.ppermute(
+        block,
+        ROWS,
+        [
+            (z * xs + x, (z + along_zl) % zls * xs + (x + along_x) % xs)
+            for z in range(zls)
+            for x in range(xs)
+        ],
+    )
+
+
+def stats_kernel(block_ref, out_ref):
+    block = block_ref[...]
+    total = jnp.sum(block, axis=0, keepdims=True)
+    off = block - total / block.shape[0]
+    squares = jnp.sum(off * off, axis=0, keepdims=True)
+    both = jnp.concatenate([total, squares], axis=0)
+    for k in range(out_ref.shape[0]):
+        out_ref[k] = both
+
+
+def whole(count):
+    return [pl.BlockSpec(memory_space=pltpu.VMEM)] * count
 
 
 def three_terms(a):
@@ -42,10 +74,17 @@
     width = col_width * cols_count
     scale = F32(n_all - 1)
 
-    sum_here = jnp.sum(embeddings, axis=0)
-    off_here = embeddings - sum_here / rows_here
-    squares_here = jnp.sum(off_here * off_here, axis=0)
-    stats = spread(jnp.stack([sum_here, squares_here]), ROWS, rows_count)
+    raw = [move(embeddings, *by) for by in RAW_MOVES]
+
+    stats_here = pl.pallas_call(
+        stats_kernel,
+        out_shape=jax.ShapeDtypeStruct((rows_count, 2, col_width), F32),
+        in_specs=whole(1),
+        out_specs=whole(1)[0],
+        name="stats",
+    )(embeddings)
+    stats = lax.all_to_all(stats_here, ROWS, 0, 0)
+    stats, raw = lax.optimization_barrier((stats, raw))
     sums, squares = stats[:, 0], stats[:, 1]
     mean = jnp.sum(sums, axis=0) / n_all
     gaps = sums / rows_here - mean
@@ -54,7 +93,11 @@
 
     cz = embeddings - mean
     centered = cz.astype(BF16)
-    gathered = spread(centered, ROWS, rows_count).reshape(n_all, col_width)
+    along_zl, along_x = (
+        jnp.concatenate([(block - mean).astype(BF16) for block in pair])
+        for pair in ((embeddings, raw[0]), raw[1:])
+    )
+    gathered = jnp.concatenate([along_zl, along_x, move(along_zl, 0, 2), move(along_x, 1, 0)])
 
     half = rows_here // 2
     piece = half // ys
@@ -83,7 +126,7 @@
     other_half = lax.ppermute(my_half, "core", SWAP)
     blocks_share = sum(block[0, n_all:] for block in blocks)
     share = lanes(my_half * my_half) / (scale * scale * width) + blocks_share
-    shares = spread(share, ROWS + ("core",), rows_count * 2)
+    shares = spread(jnp.broadcast_to(share, (8, 128)), ROWS + ("core",), rows_count * 2)
 
     gram = jnp.zeros((rows_here, n_all), F32)
     for k in range(ys):
@@ -98,7 +141,7 @@
     hinge = jnp.where(std < 1.0, cz / std, F32(0.0))
     grad_scaled = 4.0 / 25.0 * grad_cov - hinge
     grad_scaled, shares = lax.optimization_barrier((grad_scaled, shares))
-    return (grad_scaled, jnp.sum(shares))
+    return (grad_scaled, jnp.sum(shares[:, 0]))
 
 
 def solution(mesh):

time: 80.4 us -> 75.2 us (0.935)
  blocking collectives: 11.1 us -> 0 us
  starting transfers between devices: 36.1 us -> 43.3 us
  other arithmetic: 5.12 us -> 3.25 us
  Pallas kernels: 0 us -> 1.66 us
  local copies, waits for them, and re-layouts: 2.31 us -> 1.3 us
    all_to_all x2 -> x1, waiting for transfers between devices: 14.9 us -> 3.76 us  [spread(): lax.all_to_all(jnp.broadcast_to(block, (count,) + block.shape), axes, 0, 0)]
    all_to_all x1 -> x0, blocking collectives: 11.1 us -> none  [spread(): lax.all_to_all(jnp.broadcast_to(block, (count,) + block.shape), axes, 0, 0)]
    ppermute x0 -> x5, starting transfers between devices: none -> 6.89 us  [move(): lax.ppermute(block, ROWS, [(z * xs + x, (z + along_zl) % zls * xs + (x +...]
    ppermute x0 -> x5, waiting for transfers between devices: none -> 5.49 us  [move(): lax.ppermute(block, ROWS, [(z * xs + x, (z + along_zl) % zls * xs + (x +...]
    all_to_all x0 -> x1, waiting for transfers between devices: none -> 5.03 us  [on_device(): stats = lax.all_to_all(stats_here, ROWS, 0, 0)]
    all_to_all x2 -> x1, starting transfers between devices: 7.66 us -> 3.78 us  [spread(): lax.all_to_all(jnp.broadcast_to(block, (count,) + block.shape), axes, 0, 0)]
    all_to_all x0 -> x1, starting transfers between devices: none -> 3.34 us  [on_device(): stats = lax.all_to_all(stats_here, ROWS, 0, 0)]
    reduce_sum x3 -> x1, other arithmetic: 2.59 us -> 0.6 us  [on_device(): return (grad_scaled, jnp.sum(shares[:, 0]))]
  transfers between devices with their start and end apart: 13 -> 18, of which waited for: 8 -> 9; matrix products, arithmetic and copies ran while one was open for 3% -> 4% of each run, Pallas kernels for 0% -> 2%
where the time goes in v4:
time: 75.2 us; the launch traced here: 74.9 us
  starting transfers between devices  43.3 us (58%)
  waiting for transfers between devices  23.1 us (31%)
  other arithmetic  3.25 us (4%)
  Pallas kernels  1.66 us (2%)
  matrix products  1.42 us (2%)
  local copies, waits for them, and re-layouts  1.3 us (2%)
  between operations  0.89 us (1%)
    ppermute x9, starting transfers between devices, shift(): return lax.ppermute(block, axis, [(i, (i + k) % size) for i in range(size)])  19.8 us
    ppermute x9, waiting for transfers between devices, shift(): return lax.ppermute(block, axis, [(i, (i + k) % size) for i in range(size)])  7.95 us
    ppermute x5, starting transfers between devices, move(): lax.ppermute(block, ROWS, [(z * xs + x, (z + along_zl) % zls * xs + (x +...  6.89 us
    ppermute x5, waiting for transfers between devices, move(): lax.ppermute(block, ROWS, [(z * xs + x, (z + along_zl) % zls * xs + (x +...  5.49 us
    ppermute x1, starting transfers between devices, on_device(): other_half = lax.ppermute(my_half, 'core', SWAP)  5.38 us
    all_to_all x1, waiting for transfers between devices, on_device(): stats = lax.all_to_all(stats_here, ROWS, 0, 0)  5.03 us
    ppermute x1, starting transfers between devices, on_device(): from_pair = lax.ppermute(half_gram(1 - core), 'core', SWAP)  4.18 us
    all_to_all x1, starting transfers between devices, spread(): lax.all_to_all(jnp.broadcast_to(block, (count,) + block.shape), axes, 0, 0)  3.78 us
  transfers between devices with their start and end apart: 18, of which 9 were waited for; matrix products, arithmetic and copies ran while one was open for 4% of the time, Pallas kernels for 2%

profile of v4, /device:TPU:1, one launch (start us, length us, event | category | flops | bytes accessed | tf_op | source)
XLA Modules:
  0.0 74.9 jit_solution(13788363269507054528)
XLA Ops:
  0.6 2.6 %collective-permute-start = (f32[128,512]{1,0:T(8,128)}, f32[128,512]{1,0:T(8,128)S(1)}, u32[]{:S(2)}, u32[]{:S(2)}) collective-permute-start(f32[128,512]{1,0:T(8,128)} %block_ref.1), channel_id=1, source_target_pairs={{0,128},{32,160},{64,192},{96,224},{128,0},{160,32},{192,64},{224,... | collective-permute-start | bytes 786440 | tf_op jit(solution)/shard_map/ppermute | solution.py:29
  3.2 1.2 %collective-permute-start.1 = (f32[128,512]{1,0:T(8,128)}, f32[128,512]{1,0:T(8,128)S(1)}, u32[]{:S(2)}, u32[]{:S(2)}) collective-permute-start(f32[128,512]{1,0:T(8,128)} %block_ref.1), channel_id=1, source_target_pairs={{0,32},{32,64},{64,96},{96,0},{128,160},{160,192},{192,224},{224,1... | collective-permute-start | bytes 786440 | tf_op jit(solution)/shard_map/ppermute | solution.py:29
  4.4 1.5 %collective-permute-start.2 = (f32[128,512]{1,0:T(8,128)}, f32[128,512]{1,0:T(8,128)S(1)}, u32[]{:S(2)}, u32[]{:S(2)}) collective-permute-start(f32[128,512]{1,0:T(8,128)} %block_ref.1), channel_id=1, source_target_pairs={{0,96},{32,0},{64,32},{96,64},{128,224},{160,128},{192,160},{224,1... | collective-permute-start | bytes 786440 | tf_op jit(solution)/shard_map/ppermute | solution.py:29
  5.9 1.7 %stats.1 = f32[8,2,512]{2,1,0:T(2,128)} custom-call(f32[128,512]{1,0:T(8,128)} %block_ref.1), custom_call_target="tpu_custom_call" | custom-call | tf_op jit(solution)/shard_map/stats/pallas_call | solution.py:79
  7.5 3.3 %all-to-all-start = ((f32[8,2,512]{2,1,0:T(2,128)}), f32[8,2,512]{2,1,0:T(2,128)S(1)}, u32[]{:S(2)}, u32[]{:S(2)}) async-start(f32[8,2,512]{2,1,0:T(2,128)} %stats.1), calls=%async_computation | async-start | bytes 65536 | tf_op jit(solution)/shard_map/all_to_all | solution.py:86
  10.9 5.0 %all-to-all-done = f32[8,2,512]{2,1,0:T(2,128)S(1)} async-done(((f32[8,2,512]{2,1,0:T(2,128)}), f32[8,2,512]{2,1,0:T(2,128)S(1)}, u32[]{:S(2)}, u32[]{:S(2)}) %all-to-all-start) | async-done | bytes 32800 | tf_op jit(solution)/shard_map/all_to_all | solution.py:86
  16.0 1.0 %constant_dynamic-update-slice_fusion.5 = (bf16[1024,512]{1,0:T(8,128)(2,1)S(1)}, bf16[128,512]{1,0:T(8,128)(2,1)S(1)}) fusion(f32[128,512]{1,0:T(8,128)} %block_ref.1, f32[512]{0:T(512)S(1)} %broadcast_multiply_fusion), kind=kLoop, calls=%fused_computation.48 | loop fusion | flops 131071 | bytes 526336
  17.5 1.2 %collective-permute-start.3 = (bf16[256,512]{1,0:T(8,128)(2,1)S(1)}, bf16[256,512]{1,0:T(8,128)(2,1)S(1)}, u32[]{:S(2)}, u32[]{:S(2)}) collective-permute-start(bf16[256,512]{1,0:T(8,128)(2,1)S(1)} %pad_maximum_fusion), channel_id=1, source_target_pairs={{0,64},{32,96},{64,0},{96,32},{128,192},{160,224},{192,128},{224,1... | collective-permute-start | bytes 786440 | tf_op jit(solution)/shard_map/ppermute | solution.py:29
  18.9 5.5 %collective-permute-done.3 = bf16[256,512]{1,0:T(8,128)(2,1)S(1)} collective-permute-done((bf16[256,512]{1,0:T(8,128)(2,1)S(1)}, bf16[256,512]{1,0:T(8,128)(2,1)S(1)}, u32[]{:S(2)}, u32[]{:S(2)}) %collective-permute-start.3) | collective-permute-done | bytes 262176 | tf_op jit(solution)/shard_map/ppermute | solution.py:29
  24.4 0.4 fusion.11
  24.8 4.2 %collective-permute-start.5 = (f32[64,1024]{1,0:T(8,128)S(1)}, f32[64,1024]{1,0:T(8,128)S(1)}, u32[]{:S(2)}, u32[]{:S(2)}) collective-permute-start(f32[64,1024]{1,0:T(8,128)S(1)} %fusion.11), channel_id=1, source_target_pairs={{0,1},{1,0},{2,3},{3,2},{4,5},{5,4},{6,7},{7,6},{8,9},{9,8},{10,11... | collective-permute-start | bytes 786440 | tf_op jit(solution)/shard_map/ppermute | solution.py:112
  29.3 0.9 %collective-permute-done.5 = f32[64,1024]{1,0:T(8,128)S(1)} collective-permute-done((f32[64,1024]{1,0:T(8,128)S(1)}, f32[64,1024]{1,0:T(8,128)S(1)}, u32[]{:S(2)}, u32[]{:S(2)}) %collective-permute-start.5) | collective-permute-done | bytes 262176 | tf_op jit(solution)/shard_map/ppermute | solution.py:112
  30.2 0.4 convolution_add_fusion
  30.6 3.0 %collective-permute-start.6 = (f32[16,1024]{1,0:T(8,128)S(1)}, f32[16,1024]{1,0:T(8,128)S(1)}, u32[]{:S(2)}, u32[]{:S(2)}) collective-permute-start(f32[16,1024]{1,0:T(8,128)S(1)} %get-tuple-element.33), channel_id=1, source_target_pairs={{0,16},{8,24},{16,0},{24,8},{1,17},{9,25},{17,1},{25,9},{2,18},{10... | collective-permute-start | bytes 196616 | tf_op jit(solution)/shard_map/ppermute | solution.py:21
  34.0 2.3 %collective-permute-start.8 = (f32[16,1024]{1,0:T(8,128)S(1)}, f32[16,1024]{1,0:T(8,128)S(1)}, u32[]{:S(2)}, u32[]{:S(2)}) collective-permute-start(f32[16,1024]{1,0:T(8,128)S(1)} %get-tuple-element.32), channel_id=1, source_target_pairs={{0,24},{8,0},{16,8},{24,16},{1,25},{9,1},{17,9},{25,17},{2,26},{10... | collective-permute-start | bytes 196616 | tf_op jit(solution)/shard_map/ppermute | solution.py:21
  36.3 1.6 %collective-permute-done.7 = f32[16,1024]{1,0:T(8,128)S(1)} collective-permute-done((f32[16,1024]{1,0:T(8,128)S(1)}, f32[16,1024]{1,0:T(8,128)S(1)}, u32[]{:S(2)}, u32[]{:S(2)}) %collective-permute-start.7) | collective-permute-done | bytes 65568 | tf_op jit(solution)/shard_map/ppermute | solution.py:21
  38.0 3.1 %collective-permute-start.10 = (f32[16,1152]{1,0:T(8,128)S(1)}, f32[16,1152]{1,0:T(8,128)S(1)}, u32[]{:S(2)}, u32[]{:S(2)}) collective-permute-start(f32[16,1152]{1,0:T(8,128)S(1)} %pad_maximum_fusion.3), channel_id=1, source_target_pairs={{0,2},{2,4},{4,6},{6,0},{1,3},{3,5},{5,7},{7,1},{8,10},{10,12},{12... | collective-permute-start | bytes 221192 | tf_op jit(solution)/shard_map/ppermute | solution.py:21
  41.1 2.5 %collective-permute-start.11 = (f32[16,1152]{1,0:T(8,128)S(1)}, f32[16,1152]{1,0:T(8,128)S(1)}, u32[]{:S(2)}, u32[]{:S(2)}) collective-permute-start(f32[16,1152]{1,0:T(8,128)S(1)} %pad_maximum_fusion.3), channel_id=1, source_target_pairs={{0,6},{2,0},{4,2},{6,4},{1,7},{3,1},{5,3},{7,5},{8,14},{10,8},{12,... | collective-permute-start | bytes 221192 | tf_op jit(solution)/shard_map/ppermute | solution.py:21
  43.5 4.4 %collective-permute-start.9 = (f32[16,1152]{1,0:T(8,128)S(1)}, f32[16,1152]{1,0:T(8,128)S(1)}, u32[]{:S(2)}, u32[]{:S(2)}) collective-permute-start(f32[16,1152]{1,0:T(8,128)S(1)} %pad_maximum_fusion.3), channel_id=1, source_target_pairs={{0,4},{2,6},{4,0},{6,2},{1,5},{3,7},{5,1},{7,3},{8,12},{10,14},{12... | collective-permute-start | bytes 221192 | tf_op jit(solution)/shard_map/ppermute | solution.py:21
  47.9 3.2 %collective-permute-done.9 = f32[16,1152]{1,0:T(8,128)S(1)} collective-permute-done((f32[16,1152]{1,0:T(8,128)S(1)}, f32[16,1152]{1,0:T(8,128)S(1)}, u32[]{:S(2)}, u32[]{:S(2)}) %collective-permute-start.9) | collective-permute-done | bytes 73760 | tf_op jit(solution)/shard_map/ppermute | solution.py:21
  51.1 0.9 %collective-permute-start.12 = (f32[16,1152]{1,0:T(8,128)S(1)}, f32[16,1152]{1,0:T(8,128)S(1)}, u32[]{:S(2)}, u32[]{:S(2)}) collective-permute-start(f32[16,1152]{1,0:T(8,128)S(1)} %add_add_fusion), channel_id=1, source_target_pairs={{0,8},{8,16},{16,24},{24,0},{1,9},{9,17},{17,25},{25,1},{2,10},{10... | collective-permute-start | bytes 221192 | tf_op jit(solution)/shard_map/ppermute | solution.py:21
  52.1 3.2 %collective-permute-start.13 = (f32[16,1152]{1,0:T(8,128)S(1)}, f32[16,1152]{1,0:T(8,128)S(1)}, u32[]{:S(2)}, u32[]{:S(2)}) collective-permute-start(f32[16,1152]{1,0:T(8,128)S(1)} %add_add_fusion), channel_id=1, source_target_pairs={{0,16},{8,24},{16,0},{24,8},{1,17},{9,25},{17,1},{25,9},{2,18},{10... | collective-permute-start | bytes 221192 | tf_op jit(solution)/shard_map/ppermute | solution.py:21
  55.4 0.5 collective-permute-done.12
  55.9 2.0 %collective-permute-done.13 = f32[16,1152]{1,0:T(8,128)S(1)} collective-permute-done((f32[16,1152]{1,0:T(8,128)S(1)}, f32[16,1152]{1,0:T(8,128)S(1)}, u32[]{:S(2)}, u32[]{:S(2)}) %collective-permute-start.13) | collective-permute-done | bytes 73760 | tf_op jit(solution)/shard_map/ppermute | solution.py:21
  57.8 0.7 collective-permute-done.14
  58.6 5.4 %collective-permute-start.15 = (f32[64,1024]{1,0:T(8,128)S(1)}, f32[64,1024]{1,0:T(8,128)S(1)}, u32[]{:S(2)}, u32[]{:S(2)}) collective-permute-start(f32[64,1024]{1,0:T(8,128)S(1)} %get-tuple-element.30), channel_id=1, source_target_pairs={{0,1},{1,0},{2,3},{3,2},{4,5},{5,4},{6,7},{7,6},{8,9},{9,8},{10,11... | collective-permute-start | bytes 786440 | tf_op jit(solution)/shard_map/ppermute | solution.py:126
  64.1 0.6 broadcast_in_dim_broadcast_in_dim.3
  64.7 3.8 %all-to-all-start.1 = ((f32[16,8,128]{2,1,0:T(8,128)}), f32[16,8,128]{2,1,0:T(8,128)S(1)}, u32[]{:S(2)}, u32[]{:S(2)}) async-start(f32[16,8,128]{2,1,0:T(8,128)} %broadcast_in_dim_broadcast_in_dim.3), calls=%async_computation.1 | async-start | bytes 131072 | tf_op jit(solution)/shard_map/all_to_all | solution.py:16
  68.8 0.6 fusion
  69.7 0.8 %fusion.9 = f32[128,512]{1,0:T(8,128)} fusion(f32[384,512]{1,0:T(8,128)S(1)} %fusion, bf16[128,512]{1,0:T(8,128)(2,1)S(1)} %get-tuple-element.25, f32[128,512]{1,0:T(8,128)S(1)} %copy-done, f32[512]{0:T(512)S(1)} %get-tuple-element.17, f32[512]{0:T(512)S(1)} %multiply_reduce_fusion, f32[512]{0:T(512)S(1)} %broadcast_multiply_fusion, ...), kind=kLoop, calls=%fused_computation.16 | loop fusion | flops 655360 | bytes 1448448 | tf_op jit(solution)/shard_map/sub | solution.py:142
  70.6 3.8 %all-to-all-done.1 = f32[16,8,128]{2,1,0:T(8,128)S(1)} async-done(((f32[16,8,128]{2,1,0:T(8,128)}), f32[16,8,128]{2,1,0:T(8,128)S(1)}, u32[]{:S(2)}, u32[]{:S(2)}) %all-to-all-start.1) | async-done | bytes 65568 | tf_op jit(solution)/shard_map/all_to_all | solution.py:16
  74.3 0.6 reduce_sum.79
  (53 shorter events, 2.3 us)
Async XLA Ops:
  0.6 15.3 %collective-permute-start = (f32[128,512]{1,0:T(8,128)}, f32[128,512]{1,0:T(8,128)S(1)}, u32[]{:S(2)}, u32[]{:S(2)}) collective-permute-start(f32[128,512]{1,0:T(8,128)} %block_ref.1), channel_id=1, source_target_pairs={{0,128},{32,160},{64,192},{96,224},{128,0},{160,32},{192,64},{224,... | collective-permute-start | bytes 786440 | tf_op jit(solution)/shard_map/ppermute | solution.py:29
  3.2 12.7 %collective-permute-start.1 = (f32[128,512]{1,0:T(8,128)}, f32[128,512]{1,0:T(8,128)S(1)}, u32[]{:S(2)}, u32[]{:S(2)}) collective-permute-start(f32[128,512]{1,0:T(8,128)} %block_ref.1), channel_id=1, source_target_pairs={{0,32},{32,64},{64,96},{96,0},{128,160},{160,192},{192,224},{224,1... | collective-permute-start | bytes 786440 | tf_op jit(solution)/shard_map/ppermute | solution.py:29
  4.4 11.5 %collective-permute-start.2 = (f32[128,512]{1,0:T(8,128)}, f32[128,512]{1,0:T(8,128)S(1)}, u32[]{:S(2)}, u32[]{:S(2)}) collective-permute-start(f32[128,512]{1,0:T(8,128)} %block_ref.1), channel_id=1, source_target_pairs={{0,96},{32,0},{64,32},{96,64},{128,224},{160,128},{192,160},{224,1... | collective-permute-start | bytes 786440 | tf_op jit(solution)/shard_map/ppermute | solution.py:29
  7.5 8.4 %all-to-all-start = ((f32[8,2,512]{2,1,0:T(2,128)}), f32[8,2,512]{2,1,0:T(2,128)S(1)}, u32[]{:S(2)}, u32[]{:S(2)}) async-start(f32[8,2,512]{2,1,0:T(2,128)} %stats.1), calls=%async_computation | async-start | bytes 65536 | tf_op jit(solution)/shard_map/all_to_all | solution.py:86
  17.1 7.3 %collective-permute-start.4 = (bf16[256,512]{1,0:T(8,128)(2,1)S(1)}, bf16[256,512]{1,0:T(8,128)(2,1)S(1)}, u32[]{:S(2)}, u32[]{:S(2)}) collective-permute-start(bf16[256,512]{1,0:T(8,128)(2,1)S(1)} %pad_maximum_fusion.1), channel_id=1, source_target_pairs={{0,128},{32,160},{64,192},{96,224},{128,0},{160,32},{192,64},{224,... | collective-permute-start | bytes 786440 | tf_op jit(solution)/shard_map/ppermute | solution.py:29
  17.5 6.8 %collective-permute-start.3 = (bf16[256,512]{1,0:T(8,128)(2,1)S(1)}, bf16[256,512]{1,0:T(8,128)(2,1)S(1)}, u32[]{:S(2)}, u32[]{:S(2)}) collective-permute-start(bf16[256,512]{1,0:T(8,128)(2,1)S(1)} %pad_maximum_fusion), channel_id=1, source_target_pairs={{0,64},{32,96},{64,0},{96,32},{128,192},{160,224},{192,128},{224,1... | collective-permute-start | bytes 786440 | tf_op jit(solution)/shard_map/ppermute | solution.py:29
  24.8 5.3 %collective-permute-start.5 = (f32[64,1024]{1,0:T(8,128)S(1)}, f32[64,1024]{1,0:T(8,128)S(1)}, u32[]{:S(2)}, u32[]{:S(2)}) collective-permute-start(f32[64,1024]{1,0:T(8,128)S(1)} %fusion.11), channel_id=1, source_target_pairs={{0,1},{1,0},{2,3},{3,2},{4,5},{5,4},{6,7},{7,6},{8,9},{9,8},{10,11... | collective-permute-start | bytes 786440 | tf_op jit(solution)/shard_map/ppermute | solution.py:112
  30.6 5.7 %collective-permute-start.6 = (f32[16,1024]{1,0:T(8,128)S(1)}, f32[16,1024]{1,0:T(8,128)S(1)}, u32[]{:S(2)}, u32[]{:S(2)}) collective-permute-start(f32[16,1024]{1,0:T(8,128)S(1)} %get-tuple-element.33), channel_id=1, source_target_pairs={{0,16},{8,24},{16,0},{24,8},{1,17},{9,25},{17,1},{25,9},{2,18},{10... | collective-permute-start | bytes 196616 | tf_op jit(solution)/shard_map/ppermute | solution.py:21
  33.6 4.3 %collective-permute-start.7 = (f32[16,1024]{1,0:T(8,128)S(1)}, f32[16,1024]{1,0:T(8,128)S(1)}, u32[]{:S(2)}, u32[]{:S(2)}) collective-permute-start(f32[16,1024]{1,0:T(8,128)S(1)} %get-tuple-element.31), channel_id=1, source_target_pairs={{0,8},{8,16},{16,24},{24,0},{1,9},{9,17},{17,25},{25,1},{2,10},{10... | collective-permute-start | bytes 196616 | tf_op jit(solution)/shard_map/ppermute | solution.py:21
  34.0 3.9 %collective-permute-start.8 = (f32[16,1024]{1,0:T(8,128)S(1)}, f32[16,1024]{1,0:T(8,128)S(1)}, u32[]{:S(2)}, u32[]{:S(2)}) collective-permute-start(f32[16,1024]{1,0:T(8,128)S(1)} %get-tuple-element.32), channel_id=1, source_target_pairs={{0,24},{8,0},{16,8},{24,16},{1,25},{9,1},{17,9},{25,17},{2,26},{10... | collective-permute-start | bytes 196616 | tf_op jit(solution)/shard_map/ppermute | solution.py:21
  38.0 9.9 %collective-permute-start.10 = (f32[16,1152]{1,0:T(8,128)S(1)}, f32[16,1152]{1,0:T(8,128)S(1)}, u32[]{:S(2)}, u32[]{:S(2)}) collective-permute-start(f32[16,1152]{1,0:T(8,128)S(1)} %pad_maximum_fusion.3), channel_id=1, source_target_pairs={{0,2},{2,4},{4,6},{6,0},{1,3},{3,5},{5,7},{7,1},{8,10},{10,12},{12... | collective-permute-start | bytes 221192 | tf_op jit(solution)/shard_map/ppermute | solution.py:21
  41.1 6.9 %collective-permute-start.11 = (f32[16,1152]{1,0:T(8,128)S(1)}, f32[16,1152]{1,0:T(8,128)S(1)}, u32[]{:S(2)}, u32[]{:S(2)}) collective-permute-start(f32[16,1152]{1,0:T(8,128)S(1)} %pad_maximum_fusion.3), channel_id=1, source_target_pairs={{0,6},{2,0},{4,2},{6,4},{1,7},{3,1},{5,3},{7,5},{8,14},{10,8},{12,... | collective-permute-start | bytes 221192 | tf_op jit(solution)/shard_map/ppermute | solution.py:21
  43.5 7.6 %collective-permute-start.9 = (f32[16,1152]{1,0:T(8,128)S(1)}, f32[16,1152]{1,0:T(8,128)S(1)}, u32[]{:S(2)}, u32[]{:S(2)}) collective-permute-start(f32[16,1152]{1,0:T(8,128)S(1)} %pad_maximum_fusion.3), channel_id=1, source_target_pairs={{0,4},{2,6},{4,0},{6,2},{1,5},{3,7},{5,1},{7,3},{8,12},{10,14},{12... | collective-permute-start | bytes 221192 | tf_op jit(solution)/shard_map/ppermute | solution.py:21
  51.1 4.7 %collective-permute-start.12 = (f32[16,1152]{1,0:T(8,128)S(1)}, f32[16,1152]{1,0:T(8,128)S(1)}, u32[]{:S(2)}, u32[]{:S(2)}) collective-permute-start(f32[16,1152]{1,0:T(8,128)S(1)} %add_add_fusion), channel_id=1, source_target_pairs={{0,8},{8,16},{16,24},{24,0},{1,9},{9,17},{17,25},{25,1},{2,10},{10... | collective-permute-start | bytes 221192 | tf_op jit(solution)/shard_map/ppermute | solution.py:21
  52.1 5.8 %collective-permute-start.13 = (f32[16,1152]{1,0:T(8,128)S(1)}, f32[16,1152]{1,0:T(8,128)S(1)}, u32[]{:S(2)}, u32[]{:S(2)}) collective-permute-start(f32[16,1152]{1,0:T(8,128)S(1)} %add_add_fusion), channel_id=1, source_target_pairs={{0,16},{8,24},{16,0},{24,8},{1,17},{9,25},{17,1},{25,9},{2,18},{10... | collective-permute-start | bytes 221192 | tf_op jit(solution)/shard_map/ppermute | solution.py:21
  55.3 3.2 %collective-permute-start.14 = (f32[16,1152]{1,0:T(8,128)S(1)}, f32[16,1152]{1,0:T(8,128)S(1)}, u32[]{:S(2)}, u32[]{:S(2)}) collective-permute-start(f32[16,1152]{1,0:T(8,128)S(1)} %add_add_fusion), channel_id=1, source_target_pairs={{0,24},{8,0},{16,8},{24,16},{1,25},{9,1},{17,9},{25,17},{2,26},{10... | collective-permute-start | bytes 221192 | tf_op jit(solution)/shard_map/ppermute | solution.py:21
  58.6 10.0 %collective-permute-start.15 = (f32[64,1024]{1,0:T(8,128)S(1)}, f32[64,1024]{1,0:T(8,128)S(1)}, u32[]{:S(2)}, u32[]{:S(2)}) collective-permute-start(f32[64,1024]{1,0:T(8,128)S(1)} %get-tuple-element.30), channel_id=1, source_target_pairs={{0,1},{1,0},{2,3},{3,2},{4,5},{5,4},{6,7},{7,6},{8,9},{9,8},{10,11... | collective-permute-start | bytes 786440 | tf_op jit(solution)/shard_map/ppermute | solution.py:126
  64.7 9.6 %all-to-all-start.1 = ((f32[16,8,128]{2,1,0:T(8,128)}), f32[16,8,128]{2,1,0:T(8,128)S(1)}, u32[]{:S(2)}, u32[]{:S(2)}) async-start(f32[16,8,128]{2,1,0:T(8,128)} %broadcast_in_dim_broadcast_in_dim.3), calls=%async_computation.1 | async-start | bytes 131072 | tf_op jit(solution)/shard_map/all_to_all | solution.py:16
  68.8 1.0 %copy-start = (f32[128,512]{1,0:T(8,128)S(1)}, f32[128,512]{1,0:T(8,128)}, u32[]{:S(2)}) copy-start(f32[128,512]{1,0:T(8,128)} %block_ref.1) | copy-start | bytes 786436

commit v5 on v4

--- a/solution.py
+++ b/solution.py
@@ -84,19 +84,19 @@
         name="stats",
     )(embeddings)
     stats = lax.all_to_all(stats_here, ROWS, 0, 0)
-    stats, raw = lax.optimization_barrier((stats, raw))
+    stats, raw, minus = lax.optimization_barrier((stats, raw, -embeddings))
     sums, squares = stats[:, 0], stats[:, 1]
     mean = jnp.sum(sums, axis=0) / n_all
     gaps = sums / rows_here - mean
     var = (jnp.sum(squares, axis=0) + rows_here * jnp.sum(gaps * gaps, axis=0)) / scale
     std = jnp.sqrt(var + 0.0001)
 
-    cz = embeddings - mean
-    centered = cz.astype(BF16)
+    cz = -(minus + mean)
     along_zl, along_x = (
-        jnp.concatenate([(block - mean).astype(BF16) for block in pair])
-        for pair in ((embeddings, raw[0]), raw[1:])
+        jnp.concatenate([block.astype(BF16) for block in pair])
+        for pair in ((cz, raw[0] - mean), (raw[1] - mean, raw[2] - mean))
     )
+    centered = along_zl[:rows_here]
     gathered = jnp.concatenate([along_zl, along_x, move(along_zl, 0, 2), move(along_x, 1, 0)])
 
     half = rows_here // 2
@@ -110,7 +110,8 @@
         )
 
     from_pair = lax.ppermute(half_gram(1 - core), "core", SWAP)
-    chip_half = half_gram(core) + from_pair
+    from_pair, here = lax.optimization_barrier((from_pair, half_gram(core)))
+    chip_half = here + from_pair
     chunks = [chip_half[k * piece : (k + 1) * piece] for k in range(ys)]
     over_y = chunks[0] + sum(shift(chunks[k], "y", k) for k in (2, 1, 3))
 
@@ -120,8 +121,9 @@
         25.0 * lanes(jax.nn.relu(1.0 - std)) - lanes(col_norms * col_norms) / (scale * scale)
     ) / (width * rows_count)
     over_y = jnp.concatenate([over_y, jnp.broadcast_to(block_share, (piece, 128))], axis=1)
-    mine = over_y + sum(shift(over_y, "zh", k) for k in (2, 1, 3))
-    blocks = [mine] + [shift(mine, "y", k) for k in (1, 2, 3)]
+    mine = over_y + sum(shift(over_y, "zh", k) for k in (3, 2, 1))
+    back = {k: shift(mine, "y", k) for k in (2, 1, 3)}
+    blocks = [mine, back[1], back[2], back[3]]
     my_half = jnp.concatenate([block[:, :n_all] for block in blocks])
     other_half = lax.ppermute(my_half, "core", SWAP)
     blocks_share = sum(block[0, n_all:] for block in blocks)

time: 75.2 us -> 72.4 us (0.963)
  starting transfers between devices: 43.3 us -> 41.8 us
  waiting for transfers between devices: 23.1 us -> 22.2 us
    all_to_all x1, waiting for transfers between devices: 5.03 us -> 4.06 us  [on_device(): stats = lax.all_to_all(stats_here, ROWS, 0, 0)]
    neg x0 -> x1, other arithmetic: none -> 0.97 us  [on_device(): stats, raw, minus = lax.optimization_barrier((stats, raw, -embeddings))]
    unnamed x4, other arithmetic: 1.05 us -> 0.11 us
    ppermute x1, starting transfers between devices: 5.38 us -> 4.51 us  [on_device(): other_half = lax.ppermute(my_half, 'core', SWAP)]
  transfers between devices with their start and end apart: 18 -> 18, of which waited for: 9 -> 10; matrix products, arithmetic and copies ran while one was open for 4% -> 6% of each run, Pallas kernels for 2% -> 2%
where the time goes in v5:
time: 72.4 us; the launch traced here: 72.2 us
  starting transfers between devices  41.8 us (58%)
  waiting for transfers between devices  22.2 us (31%)
  other arithmetic  3.3 us (5%)
  Pallas kernels  1.66 us (2%)
  matrix products  1.4 us (2%)
  local copies, waits for them, and re-layouts  0.91 us (1%)
  between operations  0.89 us (1%)
    ppermute x9, starting transfers between devices, shift(): return lax.ppermute(block, axis, [(i, (i + k) % size) for i in range(size)])  19.6 us
    ppermute x9, waiting for transfers between devices, shift(): return lax.ppermute(block, axis, [(i, (i + k) % size) for i in range(size)])  8.29 us
    ppermute x5, starting transfers between devices, move(): lax.ppermute(block, ROWS, [(z * xs + x, (z + along_zl) % zls * xs + (x +...  6.89 us
    ppermute x5, waiting for transfers between devices, move(): lax.ppermute(block, ROWS, [(z * xs + x, (z + along_zl) % zls * xs + (x +...  4.99 us
    ppermute x1, starting transfers between devices, on_device(): other_half = lax.ppermute(my_half, 'core', SWAP)  4.51 us
    all_to_all x1, waiting for transfers between devices, spread(): lax.all_to_all(jnp.broadcast_to(block, (count,) + block.shape), axes, 0, 0)  4.13 us
    all_to_all x1, waiting for transfers between devices, on_device(): stats = lax.all_to_all(stats_here, ROWS, 0, 0)  4.06 us
    ppermute x1, starting transfers between devices, on_device(): from_pair = lax.ppermute(half_gram(1 - core), 'core', SWAP)  3.9 us
  transfers between devices with their start and end apart: 18, of which 10 were waited for; matrix products, arithmetic and copies ran while one was open for 6% of the time, Pallas kernels for 2%

profile of v5, /device:TPU:1, one launch (start us, length us, event | category | flops | bytes accessed | tf_op | source)
XLA Modules:
  0.0 72.2 jit_solution(17514225973310261244)
XLA Ops:
  0.6 2.6 %collective-permute-start = (f32[128,512]{1,0:T(8,128)}, f32[128,512]{1,0:T(8,128)S(1)}, u32[]{:S(2)}, u32[]{:S(2)}) collective-permute-start(f32[128,512]{1,0:T(8,128)} %block_ref.1), channel_id=1, source_target_pairs={{0,128},{32,160},{64,192},{96,224},{128,0},{160,32},{192,64},{224,... | collective-permute-start | bytes 786440 | tf_op jit(solution)/shard_map/ppermute | solution.py:29
  3.2 1.2 %collective-permute-start.1 = (f32[128,512]{1,0:T(8,128)}, f32[128,512]{1,0:T(8,128)S(1)}, u32[]{:S(2)}, u32[]{:S(2)}) collective-permute-start(f32[128,512]{1,0:T(8,128)} %block_ref.1), channel_id=1, source_target_pairs={{0,32},{32,64},{64,96},{96,0},{128,160},{160,192},{192,224},{224,1... | collective-permute-start | bytes 786440 | tf_op jit(solution)/shard_map/ppermute | solution.py:29
  4.4 1.5 %collective-permute-start.2 = (f32[128,512]{1,0:T(8,128)}, f32[128,512]{1,0:T(8,128)S(1)}, u32[]{:S(2)}, u32[]{:S(2)}) collective-permute-start(f32[128,512]{1,0:T(8,128)} %block_ref.1), channel_id=1, source_target_pairs={{0,96},{32,0},{64,32},{96,64},{128,224},{160,128},{192,160},{224,1... | collective-permute-start | bytes 786440 | tf_op jit(solution)/shard_map/ppermute | solution.py:29
  5.9 1.7 %stats.1 = f32[8,2,512]{2,1,0:T(2,128)} custom-call(f32[128,512]{1,0:T(8,128)} %block_ref.1), custom_call_target="tpu_custom_call" | custom-call | tf_op jit(solution)/shard_map/stats/pallas_call | solution.py:79
  7.5 3.3 %all-to-all-start = ((f32[8,2,512]{2,1,0:T(2,128)}), f32[8,2,512]{2,1,0:T(2,128)S(1)}, u32[]{:S(2)}, u32[]{:S(2)}) async-start(f32[8,2,512]{2,1,0:T(2,128)} %stats.1), calls=%async_computation | async-start | bytes 65536 | tf_op jit(solution)/shard_map/all_to_all | solution.py:86
  10.9 1.0 %neg.6 = f32[128,512]{1,0:T(8,128)S(1)} negate(f32[128,512]{1,0:T(8,128)} %block_ref.1) | non-fusion elementwise | flops 65536 | bytes 524288 | tf_op jit(solution)/shard_map/neg | solution.py:87
  11.9 4.1 %all-to-all-done = f32[8,2,512]{2,1,0:T(2,128)S(1)} async-done(((f32[8,2,512]{2,1,0:T(2,128)}), f32[8,2,512]{2,1,0:T(2,128)S(1)}, u32[]{:S(2)}, u32[]{:S(2)}) %all-to-all-start) | async-done | bytes 32800 | tf_op jit(solution)/shard_map/all_to_all | solution.py:86
  16.1 1.2 %collective-permute-start.3 = (bf16[256,512]{1,0:T(8,128)(2,1)S(1)}, bf16[256,512]{1,0:T(8,128)(2,1)S(1)}, u32[]{:S(2)}, u32[]{:S(2)}) collective-permute-start(bf16[256,512]{1,0:T(8,128)(2,1)S(1)} %pad_maximum_fusion), channel_id=1, source_target_pairs={{0,64},{32,96},{64,0},{96,32},{128,192},{160,224},{192,128},{224,1... | collective-permute-start | bytes 786440 | tf_op jit(solution)/shard_map/ppermute | solution.py:29
  17.4 0.5 collective-permute-start.4
  17.9 5.0 %collective-permute-done.3 = bf16[256,512]{1,0:T(8,128)(2,1)S(1)} collective-permute-done((bf16[256,512]{1,0:T(8,128)(2,1)S(1)}, bf16[256,512]{1,0:T(8,128)(2,1)S(1)}, u32[]{:S(2)}, u32[]{:S(2)}) %collective-permute-start.3) | collective-permute-done | bytes 262176 | tf_op jit(solution)/shard_map/ppermute | solution.py:29
  23.7 3.9 %collective-permute-start.5 = (f32[64,1024]{1,0:T(8,128)S(1)}, f32[64,1024]{1,0:T(8,128)S(1)}, u32[]{:S(2)}, u32[]{:S(2)}) collective-permute-start(f32[64,1024]{1,0:T(8,128)S(1)} %fusion.15), channel_id=1, source_target_pairs={{0,1},{1,0},{2,3},{3,2},{4,5},{5,4},{6,7},{7,6},{8,9},{9,8},{10,11... | collective-permute-start | bytes 786440 | tf_op jit(solution)/shard_map/ppermute | solution.py:112
  28.0 0.7 collective-permute-done.5
  28.8 3.0 %collective-permute-start.6 = (f32[16,1024]{1,0:T(8,128)S(1)}, f32[16,1024]{1,0:T(8,128)S(1)}, u32[]{:S(2)}, u32[]{:S(2)}) collective-permute-start(f32[16,1024]{1,0:T(8,128)S(1)} %get-tuple-element.39), channel_id=1, source_target_pairs={{0,16},{8,24},{16,0},{24,8},{1,17},{9,25},{17,1},{25,9},{2,18},{10... | collective-permute-start | bytes 196616 | tf_op jit(solution)/shard_map/ppermute | solution.py:21
  32.2 2.3 %collective-permute-start.8 = (f32[16,1024]{1,0:T(8,128)S(1)}, f32[16,1024]{1,0:T(8,128)S(1)}, u32[]{:S(2)}, u32[]{:S(2)}) collective-permute-start(f32[16,1024]{1,0:T(8,128)S(1)} %get-tuple-element.38), channel_id=1, source_target_pairs={{0,24},{8,0},{16,8},{24,16},{1,25},{9,1},{17,9},{25,17},{2,26},{10... | collective-permute-start | bytes 196616 | tf_op jit(solution)/shard_map/ppermute | solution.py:21
  34.5 1.6 %collective-permute-done.7 = f32[16,1024]{1,0:T(8,128)S(1)} collective-permute-done((f32[16,1024]{1,0:T(8,128)S(1)}, f32[16,1024]{1,0:T(8,128)S(1)}, u32[]{:S(2)}, u32[]{:S(2)}) %collective-permute-start.7) | collective-permute-done | bytes 65568 | tf_op jit(solution)/shard_map/ppermute | solution.py:21
  36.1 6.4 %collective-permute-start.10 = (f32[16,1152]{1,0:T(8,128)S(1)}, f32[16,1152]{1,0:T(8,128)S(1)}, u32[]{:S(2)}, u32[]{:S(2)}) collective-permute-start(f32[16,1152]{1,0:T(8,128)S(1)} %pad_maximum_fusion.3), channel_id=1, source_target_pairs={{0,4},{2,6},{4,0},{6,2},{1,5},{3,7},{5,1},{7,3},{8,12},{10,14},{12... | collective-permute-start | bytes 221192 | tf_op jit(solution)/shard_map/ppermute | solution.py:21
  42.5 1.2 %collective-permute-start.11 = (f32[16,1152]{1,0:T(8,128)S(1)}, f32[16,1152]{1,0:T(8,128)S(1)}, u32[]{:S(2)}, u32[]{:S(2)}) collective-permute-start(f32[16,1152]{1,0:T(8,128)S(1)} %pad_maximum_fusion.3), channel_id=1, source_target_pairs={{0,2},{2,4},{4,6},{6,0},{1,3},{3,5},{5,7},{7,1},{8,10},{10,12},{12... | collective-permute-start | bytes 221192 | tf_op jit(solution)/shard_map/ppermute | solution.py:21
  43.7 2.4 %collective-permute-start.9 = (f32[16,1152]{1,0:T(8,128)S(1)}, f32[16,1152]{1,0:T(8,128)S(1)}, u32[]{:S(2)}, u32[]{:S(2)}) collective-permute-start(f32[16,1152]{1,0:T(8,128)S(1)} %pad_maximum_fusion.3), channel_id=1, source_target_pairs={{0,6},{2,0},{4,2},{6,4},{1,7},{3,1},{5,3},{7,5},{8,14},{10,8},{12,... | collective-permute-start | bytes 221192 | tf_op jit(solution)/shard_map/ppermute | solution.py:21
  46.1 2.7 %collective-permute-done.11 = f32[16,1152]{1,0:T(8,128)S(1)} collective-permute-done((f32[16,1152]{1,0:T(8,128)S(1)}, f32[16,1152]{1,0:T(8,128)S(1)}, u32[]{:S(2)}, u32[]{:S(2)}) %collective-permute-start.11) | collective-permute-done | bytes 73760 | tf_op jit(solution)/shard_map/ppermute | solution.py:21
  48.8 0.5 collective-permute-done.9
  49.3 1.3 %collective-permute-start.12 = (f32[16,1152]{1,0:T(8,128)S(1)}, f32[16,1152]{1,0:T(8,128)S(1)}, u32[]{:S(2)}, u32[]{:S(2)}) collective-permute-start(f32[16,1152]{1,0:T(8,128)S(1)} %add_add_fusion), channel_id=1, source_target_pairs={{0,8},{8,16},{16,24},{24,0},{1,9},{9,17},{17,25},{25,1},{2,10},{10... | collective-permute-start | bytes 221192 | tf_op jit(solution)/shard_map/ppermute | solution.py:21
  50.7 2.7 %collective-permute-start.13 = (f32[16,1152]{1,0:T(8,128)S(1)}, f32[16,1152]{1,0:T(8,128)S(1)}, u32[]{:S(2)}, u32[]{:S(2)}) collective-permute-start(f32[16,1152]{1,0:T(8,128)S(1)} %add_add_fusion), channel_id=1, source_target_pairs={{0,16},{8,24},{16,0},{24,8},{1,17},{9,25},{17,1},{25,9},{2,18},{10... | collective-permute-start | bytes 221192 | tf_op jit(solution)/shard_map/ppermute | solution.py:21
  53.4 0.5 collective-permute-done.12
  53.9 2.0 %collective-permute-done.13 = f32[16,1152]{1,0:T(8,128)S(1)} collective-permute-done((f32[16,1152]{1,0:T(8,128)S(1)}, f32[16,1152]{1,0:T(8,128)S(1)}, u32[]{:S(2)}, u32[]{:S(2)}) %collective-permute-start.13) | collective-permute-done | bytes 73760 | tf_op jit(solution)/shard_map/ppermute | solution.py:21
  55.9 1.0 %collective-permute-done.14 = f32[16,1152]{1,0:T(8,128)S(1)} collective-permute-done((f32[16,1152]{1,0:T(8,128)S(1)}, f32[16,1152]{1,0:T(8,128)S(1)}, u32[]{:S(2)}, u32[]{:S(2)}) %collective-permute-start.14) | collective-permute-done | bytes 73760 | tf_op jit(solution)/shard_map/ppermute | solution.py:21
  56.9 4.5 %collective-permute-start.15 = (f32[64,1024]{1,0:T(8,128)S(1)}, f32[64,1024]{1,0:T(8,128)S(1)}, u32[]{:S(2)}, u32[]{:S(2)}) collective-permute-start(f32[64,1024]{1,0:T(8,128)S(1)} %get-tuple-element.36), channel_id=1, source_target_pairs={{0,1},{1,0},{2,3},{3,2},{4,5},{5,4},{6,7},{7,6},{8,9},{9,8},{10,11... | collective-permute-start | bytes 786440 | tf_op jit(solution)/shard_map/ppermute | solution.py:128
  61.5 0.6 broadcast_in_dim_broadcast_in_dim.3
  62.2 3.6 %all-to-all-start.1 = ((f32[16,8,128]{2,1,0:T(8,128)}), f32[16,8,128]{2,1,0:T(8,128)S(1)}, u32[]{:S(2)}, u32[]{:S(2)}) async-start(f32[16,8,128]{2,1,0:T(8,128)} %broadcast_in_dim_broadcast_in_dim.3), calls=%async_computation.1 | async-start | bytes 131072 | tf_op jit(solution)/shard_map/all_to_all | solution.py:16
  66.0 0.6 fusion
  66.6 0.8 %fusion.9 = f32[128,512]{1,0:T(8,128)} fusion(f32[384,512]{1,0:T(8,128)S(1)} %fusion, bf16[128,512]{1,0:T(8,128)(2,1)S(1)} %get-tuple-element.31, f32[128,512]{1,0:T(8,128)S(1)} %neg.6, f32[512]{0:T(512)S(1)} %get-tuple-element.23, f32[512]{0:T(512)S(1)} %multiply_reduce_fusion, f32[512]{0:T(512)S(1)} %broadcast_multiply_fusion, ...), kind=kLoop, calls=%fused_computation.15 | loop fusion | flops 720896 | bytes 1448448 | tf_op jit(solution)/shard_map/sub | solution.py:144
  67.4 4.1 %all-to-all-done.1 = f32[16,8,128]{2,1,0:T(8,128)S(1)} async-done(((f32[16,8,128]{2,1,0:T(8,128)}), f32[16,8,128]{2,1,0:T(8,128)S(1)}, u32[]{:S(2)}, u32[]{:S(2)}) %all-to-all-start.1) | async-done | bytes 65568 | tf_op jit(solution)/shard_map/all_to_all | solution.py:16
  71.6 0.6 reduce_sum.79
  (53 shorter events, 2.4 us)
Async XLA Ops:
  0.6 15.3 %collective-permute-start = (f32[128,512]{1,0:T(8,128)}, f32[128,512]{1,0:T(8,128)S(1)}, u32[]{:S(2)}, u32[]{:S(2)}) collective-permute-start(f32[128,512]{1,0:T(8,128)} %block_ref.1), channel_id=1, source_target_pairs={{0,128},{32,160},{64,192},{96,224},{128,0},{160,32},{192,64},{224,... | collective-permute-start | bytes 786440 | tf_op jit(solution)/shard_map/ppermute | solution.py:29
  3.2 12.7 %collective-permute-start.1 = (f32[128,512]{1,0:T(8,128)}, f32[128,512]{1,0:T(8,128)S(1)}, u32[]{:S(2)}, u32[]{:S(2)}) collective-permute-start(f32[128,512]{1,0:T(8,128)} %block_ref.1), channel_id=1, source_target_pairs={{0,32},{32,64},{64,96},{96,0},{128,160},{160,192},{192,224},{224,1... | collective-permute-start | bytes 786440 | tf_op jit(solution)/shard_map/ppermute | solution.py:29
  4.4 11.5 %collective-permute-start.2 = (f32[128,512]{1,0:T(8,128)}, f32[128,512]{1,0:T(8,128)S(1)}, u32[]{:S(2)}, u32[]{:S(2)}) collective-permute-start(f32[128,512]{1,0:T(8,128)} %block_ref.1), channel_id=1, source_target_pairs={{0,96},{32,0},{64,32},{96,64},{128,224},{160,128},{192,160},{224,1... | collective-permute-start | bytes 786440 | tf_op jit(solution)/shard_map/ppermute | solution.py:29
  7.5 8.4 %all-to-all-start = ((f32[8,2,512]{2,1,0:T(2,128)}), f32[8,2,512]{2,1,0:T(2,128)S(1)}, u32[]{:S(2)}, u32[]{:S(2)}) async-start(f32[8,2,512]{2,1,0:T(2,128)} %stats.1), calls=%async_computation | async-start | bytes 65536 | tf_op jit(solution)/shard_map/all_to_all | solution.py:86
  16.1 6.8 %collective-permute-start.3 = (bf16[256,512]{1,0:T(8,128)(2,1)S(1)}, bf16[256,512]{1,0:T(8,128)(2,1)S(1)}, u32[]{:S(2)}, u32[]{:S(2)}) collective-permute-start(bf16[256,512]{1,0:T(8,128)(2,1)S(1)} %pad_maximum_fusion), channel_id=1, source_target_pairs={{0,64},{32,96},{64,0},{96,32},{128,192},{160,224},{192,128},{224,1... | collective-permute-start | bytes 786440 | tf_op jit(solution)/shard_map/ppermute | solution.py:29
  17.4 5.6 %collective-permute-start.4 = (bf16[256,512]{1,0:T(8,128)(2,1)S(1)}, bf16[256,512]{1,0:T(8,128)(2,1)S(1)}, u32[]{:S(2)}, u32[]{:S(2)}) collective-permute-start(bf16[256,512]{1,0:T(8,128)(2,1)S(1)} %pad_maximum_fusion.1), channel_id=1, source_target_pairs={{0,128},{32,160},{64,192},{96,224},{128,0},{160,32},{192,64},{224,... | collective-permute-start | bytes 786440 | tf_op jit(solution)/shard_map/ppermute | solution.py:29
  23.7 5.1 %collective-permute-start.5 = (f32[64,1024]{1,0:T(8,128)S(1)}, f32[64,1024]{1,0:T(8,128)S(1)}, u32[]{:S(2)}, u32[]{:S(2)}) collective-permute-start(f32[64,1024]{1,0:T(8,128)S(1)} %fusion.15), channel_id=1, source_target_pairs={{0,1},{1,0},{2,3},{3,2},{4,5},{5,4},{6,7},{7,6},{8,9},{9,8},{10,11... | collective-permute-start | bytes 786440 | tf_op jit(solution)/shard_map/ppermute | solution.py:112
  28.8 5.7 %collective-permute-start.6 = (f32[16,1024]{1,0:T(8,128)S(1)}, f32[16,1024]{1,0:T(8,128)S(1)}, u32[]{:S(2)}, u32[]{:S(2)}) collective-permute-start(f32[16,1024]{1,0:T(8,128)S(1)} %get-tuple-element.39), channel_id=1, source_target_pairs={{0,16},{8,24},{16,0},{24,8},{1,17},{9,25},{17,1},{25,9},{2,18},{10... | collective-permute-start | bytes 196616 | tf_op jit(solution)/shard_map/ppermute | solution.py:21
  31.8 4.3 %collective-permute-start.7 = (f32[16,1024]{1,0:T(8,128)S(1)}, f32[16,1024]{1,0:T(8,128)S(1)}, u32[]{:S(2)}, u32[]{:S(2)}) collective-permute-start(f32[16,1024]{1,0:T(8,128)S(1)} %get-tuple-element.37), channel_id=1, source_target_pairs={{0,8},{8,16},{16,24},{24,0},{1,9},{9,17},{17,25},{25,1},{2,10},{10... | collective-permute-start | bytes 196616 | tf_op jit(solution)/shard_map/ppermute | solution.py:21
  32.2 3.9 %collective-permute-start.8 = (f32[16,1024]{1,0:T(8,128)S(1)}, f32[16,1024]{1,0:T(8,128)S(1)}, u32[]{:S(2)}, u32[]{:S(2)}) collective-permute-start(f32[16,1024]{1,0:T(8,128)S(1)} %get-tuple-element.38), channel_id=1, source_target_pairs={{0,24},{8,0},{16,8},{24,16},{1,25},{9,1},{17,9},{25,17},{2,26},{10... | collective-permute-start | bytes 196616 | tf_op jit(solution)/shard_map/ppermute | solution.py:21
  36.1 9.9 %collective-permute-start.10 = (f32[16,1152]{1,0:T(8,128)S(1)}, f32[16,1152]{1,0:T(8,128)S(1)}, u32[]{:S(2)}, u32[]{:S(2)}) collective-permute-start(f32[16,1152]{1,0:T(8,128)S(1)} %pad_maximum_fusion.3), channel_id=1, source_target_pairs={{0,4},{2,6},{4,0},{6,2},{1,5},{3,7},{5,1},{7,3},{8,12},{10,14},{12... | collective-permute-start | bytes 221192 | tf_op jit(solution)/shard_map/ppermute | solution.py:21
  42.5 6.3 %collective-permute-start.11 = (f32[16,1152]{1,0:T(8,128)S(1)}, f32[16,1152]{1,0:T(8,128)S(1)}, u32[]{:S(2)}, u32[]{:S(2)}) collective-permute-start(f32[16,1152]{1,0:T(8,128)S(1)} %pad_maximum_fusion.3), channel_id=1, source_target_pairs={{0,2},{2,4},{4,6},{6,0},{1,3},{3,5},{5,7},{7,1},{8,10},{10,12},{12... | collective-permute-start | bytes 221192 | tf_op jit(solution)/shard_map/ppermute | solution.py:21
  43.7 5.6 %collective-permute-start.9 = (f32[16,1152]{1,0:T(8,128)S(1)}, f32[16,1152]{1,0:T(8,128)S(1)}, u32[]{:S(2)}, u32[]{:S(2)}) collective-permute-start(f32[16,1152]{1,0:T(8,128)S(1)} %pad_maximum_fusion.3), channel_id=1, source_target_pairs={{0,6},{2,0},{4,2},{6,4},{1,7},{3,1},{5,3},{7,5},{8,14},{10,8},{12,... | collective-permute-start | bytes 221192 | tf_op jit(solution)/shard_map/ppermute | solution.py:21
  49.3 4.5 %collective-permute-start.12 = (f32[16,1152]{1,0:T(8,128)S(1)}, f32[16,1152]{1,0:T(8,128)S(1)}, u32[]{:S(2)}, u32[]{:S(2)}) collective-permute-start(f32[16,1152]{1,0:T(8,128)S(1)} %add_add_fusion), channel_id=1, source_target_pairs={{0,8},{8,16},{16,24},{24,0},{1,9},{9,17},{17,25},{25,1},{2,10},{10... | collective-permute-start | bytes 221192 | tf_op jit(solution)/shard_map/ppermute | solution.py:21
  50.7 5.2 %collective-permute-start.13 = (f32[16,1152]{1,0:T(8,128)S(1)}, f32[16,1152]{1,0:T(8,128)S(1)}, u32[]{:S(2)}, u32[]{:S(2)}) collective-permute-start(f32[16,1152]{1,0:T(8,128)S(1)} %add_add_fusion), channel_id=1, source_target_pairs={{0,16},{8,24},{16,0},{24,8},{1,17},{9,25},{17,1},{25,9},{2,18},{10... | collective-permute-start | bytes 221192 | tf_op jit(solution)/shard_map/ppermute | solution.py:21
  53.3 3.5 %collective-permute-start.14 = (f32[16,1152]{1,0:T(8,128)S(1)}, f32[16,1152]{1,0:T(8,128)S(1)}, u32[]{:S(2)}, u32[]{:S(2)}) collective-permute-start(f32[16,1152]{1,0:T(8,128)S(1)} %add_add_fusion), channel_id=1, source_target_pairs={{0,24},{8,0},{16,8},{24,16},{1,25},{9,1},{17,9},{25,17},{2,26},{10... | collective-permute-start | bytes 221192 | tf_op jit(solution)/shard_map/ppermute | solution.py:21
  56.9 8.8 %collective-permute-start.15 = (f32[64,1024]{1,0:T(8,128)S(1)}, f32[64,1024]{1,0:T(8,128)S(1)}, u32[]{:S(2)}, u32[]{:S(2)}) collective-permute-start(f32[64,1024]{1,0:T(8,128)S(1)} %get-tuple-element.36), channel_id=1, source_target_pairs={{0,1},{1,0},{2,3},{3,2},{4,5},{5,4},{6,7},{7,6},{8,9},{9,8},{10,11... | collective-permute-start | bytes 786440 | tf_op jit(solution)/shard_map/ppermute | solution.py:128
  62.2 9.4 %all-to-all-start.1 = ((f32[16,8,128]{2,1,0:T(8,128)}), f32[16,8,128]{2,1,0:T(8,128)S(1)}, u32[]{:S(2)}, u32[]{:S(2)}) async-start(f32[16,8,128]{2,1,0:T(8,128)} %broadcast_in_dim_broadcast_in_dim.3), calls=%async_computation.1 | async-start | bytes 131072 | tf_op jit(solution)/shard_map/all_to_all | solution.py:16

commit v6 on v5

--- a/solution.py
+++ b/solution.py
@@ -75,6 +75,7 @@
     scale = F32(n_all - 1)
 
     raw = [move(embeddings, *by) for by in RAW_MOVES]
+    raw_far = move(embeddings, 0, 2)
 
     stats_here = pl.pallas_call(
         stats_kernel,
@@ -97,7 +98,8 @@
         for pair in ((cz, raw[0] - mean), (raw[1] - mean, raw[2] - mean))
     )
     centered = along_zl[:rows_here]
-    gathered = jnp.concatenate([along_zl, along_x, move(along_zl, 0, 2), move(along_x, 1, 0)])
+    far = [(raw_far - mean).astype(BF16), move(along_zl[rows_here:], 0, 2)]
+    gathered = jnp.concatenate([along_zl, along_x, move(along_x, 1, 0)] + far)
 
     half = rows_here // 2
     piece = half // ys
@@ -121,9 +123,9 @@
         25.0 * lanes(jax.nn.relu(1.0 - std)) - lanes(col_norms * col_norms) / (scale * scale)
     ) / (width * rows_count)
     over_y = jnp.concatenate([over_y, jnp.broadcast_to(block_share, (piece, 128))], axis=1)
-    mine = over_y + sum(shift(over_y, "zh", k) for k in (3, 2, 1))
+    mine = over_y + sum(shift(over_y, "zh", k) for k in (2, 1, 3))
     back = {k: shift(mine, "y", k) for k in (2, 1, 3)}
-    blocks = [mine, back[1], back[2], back[3]]
+    blocks = [mine, back[2], back[1], back[3]]
     my_half = jnp.concatenate([block[:, :n_all] for block in blocks])
     other_half = lax.ppermute(my_half, "core", SWAP)
     blocks_share = sum(block[0, n_all:] for block in blocks)
@@ -131,8 +133,8 @@
     shares = spread(jnp.broadcast_to(share, (8, 128)), ROWS + ("core",), rows_count * 2)
 
     gram = jnp.zeros((rows_here, n_all), F32)
-    for k in range(ys):
-        owner = lax.rem(y + ys - k, ys)
+    for k, away in enumerate((0, 2, 1, 3)):
+        owner = lax.rem(y + ys - away, ys)
         for c, rows in enumerate((my_half, other_half)):
             block = rows[k * piece : (k + 1) * piece]
             start = lax.rem(core + c, 2) * half + owner * piece

time: 72.4 us -> 70.8 us (0.978)
  waiting for transfers between devices: 22.2 us -> 18.2 us
  starting transfers between devices: 41.8 us -> 44.1 us
    all_to_all x1, waiting for transfers between devices: 4.06 us -> 1.3 us  [on_device(): stats = lax.all_to_all(stats_here, ROWS, 0, 0)]
    ppermute x5 -> x6, starting transfers between devices: 6.89 us -> 9.53 us  [move(): lax.ppermute(block, ROWS, [(z * xs + x, (z + along_zl) % zls * xs + (x +...]
    ppermute x5 -> x6, waiting for transfers between devices: 4.99 us -> 4.51 us  [move(): lax.ppermute(block, ROWS, [(z * xs + x, (z + along_zl) % zls * xs + (x +...]
  transfers between devices with their start and end apart: 18 -> 19, of which waited for: 10 -> 10; matrix products, arithmetic and copies ran while one was open for 6% -> 6% of each run, Pallas kernels for 2% -> 2%
where the time goes in v6:
time: 70.8 us; the launch traced here: 70.5 us
  starting transfers between devices  44.1 us (62%)
  waiting for transfers between devices  18.2 us (26%)
  other arithmetic  3.35 us (5%)
  Pallas kernels  1.66 us (2%)
  matrix products  1.41 us (2%)
  local copies, waits for them, and re-layouts  0.91 us (1%)
  between operations  0.9 us (1%)
    ppermute x9, starting transfers between devices, shift(): return lax.ppermute(block, axis, [(i, (i + k) % size) for i in range(size)])  19.5 us
    ppermute x6, starting transfers between devices, move(): lax.ppermute(block, ROWS, [(z * xs + x, (z + along_zl) % zls * xs + (x +...  9.53 us
    ppermute x9, waiting for transfers between devices, shift(): return lax.ppermute(block, axis, [(i, (i + k) % size) for i in range(size)])  7.57 us
    ppermute x6, waiting for transfers between devices, move(): lax.ppermute(block, ROWS, [(z * xs + x, (z + along_zl) % zls * xs + (x +...  4.51 us
    ppermute x1, starting transfers between devices, on_device(): other_half = lax.ppermute(my_half, 'core', SWAP)  4.19 us
    all_to_all x1, waiting for transfers between devices, spread(): lax.all_to_all(jnp.broadcast_to(block, (count,) + block.shape), axes, 0, 0)  4.12 us
    ppermute x1, starting transfers between devices, on_device(): from_pair = lax.ppermute(half_gram(1 - core), 'core', SWAP)  3.85 us
    all_to_all x1, starting transfers between devices, spread(): lax.all_to_all(jnp.broadcast_to(block, (count,) + block.shape), axes, 0, 0)  3.68 us
  transfers between devices with their start and end apart: 19, of which 10 were waited for; matrix products, arithmetic and copies ran while one was open for 6% of the time, Pallas kernels for 2%

profile of v6, /device:TPU:1, one launch (start us, length us, event | category | flops | bytes accessed | tf_op | source)
XLA Modules:
  0.0 70.5 jit_solution(12463394630058167633)
XLA Ops:
  0.6 2.6 %collective-permute-start = (f32[128,512]{1,0:T(8,128)}, f32[128,512]{1,0:T(8,128)S(1)}, u32[]{:S(2)}, u32[]{:S(2)}) collective-permute-start(f32[128,512]{1,0:T(8,128)} %block_ref.1), channel_id=1, source_target_pairs={{0,128},{32,160},{64,192},{96,224},{128,0},{160,32},{192,64},{224,... | collective-permute-start | bytes 786440 | tf_op jit(solution)/shard_map/ppermute | solution.py:29
  3.2 1.2 %collective-permute-start.1 = (f32[128,512]{1,0:T(8,128)}, f32[128,512]{1,0:T(8,128)S(1)}, u32[]{:S(2)}, u32[]{:S(2)}) collective-permute-start(f32[128,512]{1,0:T(8,128)} %block_ref.1), channel_id=1, source_target_pairs={{0,32},{32,64},{64,96},{96,0},{128,160},{160,192},{192,224},{224,1... | collective-permute-start | bytes 786440 | tf_op jit(solution)/shard_map/ppermute | solution.py:29
  4.4 1.5 %collective-permute-start.2 = (f32[128,512]{1,0:T(8,128)}, f32[128,512]{1,0:T(8,128)S(1)}, u32[]{:S(2)}, u32[]{:S(2)}) collective-permute-start(f32[128,512]{1,0:T(8,128)} %block_ref.1), channel_id=1, source_target_pairs={{0,96},{32,0},{64,32},{96,64},{128,224},{160,128},{192,160},{224,1... | collective-permute-start | bytes 786440 | tf_op jit(solution)/shard_map/ppermute | solution.py:29
  5.9 1.7 %stats.1 = f32[8,2,512]{2,1,0:T(2,128)} custom-call(f32[128,512]{1,0:T(8,128)} %block_ref.1), custom_call_target="tpu_custom_call" | custom-call | tf_op jit(solution)/shard_map/stats/pallas_call | solution.py:80
  7.5 3.3 %all-to-all-start = ((f32[8,2,512]{2,1,0:T(2,128)}), f32[8,2,512]{2,1,0:T(2,128)S(1)}, u32[]{:S(2)}, u32[]{:S(2)}) async-start(f32[8,2,512]{2,1,0:T(2,128)} %stats.1), calls=%async_computation | async-start | bytes 65536 | tf_op jit(solution)/shard_map/all_to_all | solution.py:87
  10.9 2.9 %collective-permute-start.4 = (f32[128,512]{1,0:T(8,128)}, f32[128,512]{1,0:T(8,128)S(1)}, u32[]{:S(2)}, u32[]{:S(2)}) collective-permute-start(f32[128,512]{1,0:T(8,128)} %block_ref.1), channel_id=1, source_target_pairs={{0,64},{32,96},{64,0},{96,32},{128,192},{160,224},{192,128},{224,1... | collective-permute-start | bytes 786440 | tf_op jit(solution)/shard_map/ppermute | solution.py:29
  13.7 1.0 %neg.6 = f32[128,512]{1,0:T(8,128)S(1)} negate(f32[128,512]{1,0:T(8,128)} %block_ref.1) | non-fusion elementwise | flops 65536 | bytes 524288 | tf_op jit(solution)/shard_map/neg | solution.py:88
  14.8 1.3 %all-to-all-done = f32[8,2,512]{2,1,0:T(2,128)S(1)} async-done(((f32[8,2,512]{2,1,0:T(2,128)}), f32[8,2,512]{2,1,0:T(2,128)S(1)}, u32[]{:S(2)}, u32[]{:S(2)}) %all-to-all-start) | async-done | bytes 32800 | tf_op jit(solution)/shard_map/all_to_all | solution.py:87
  16.6 1.2 %collective-permute-start.5 = (bf16[128,512]{1,0:T(8,128)(2,1)S(1)}, bf16[128,512]{1,0:T(8,128)(2,1)S(1)}, u32[]{:S(2)}, u32[]{:S(2)}) collective-permute-start(bf16[128,512]{1,0:T(8,128)(2,1)S(1)} %get-tuple-element.29), channel_id=1, source_target_pairs={{0,64},{32,96},{64,0},{96,32},{128,192},{160,224},{192,128},{224,1... | collective-permute-start | bytes 393224 | tf_op jit(solution)/shard_map/ppermute | solution.py:29
  17.8 3.9 %collective-permute-done.3 = bf16[256,512]{1,0:T(8,128)(2,1)S(1)} collective-permute-done((bf16[256,512]{1,0:T(8,128)(2,1)S(1)}, bf16[256,512]{1,0:T(8,128)(2,1)S(1)}, u32[]{:S(2)}, u32[]{:S(2)}) %collective-permute-start.3) | collective-permute-done | bytes 262176 | tf_op jit(solution)/shard_map/ppermute | solution.py:29
  21.7 0.6 collective-permute-done.5
  23.1 3.9 %collective-permute-start.6 = (f32[64,1024]{1,0:T(8,128)S(1)}, f32[64,1024]{1,0:T(8,128)S(1)}, u32[]{:S(2)}, u32[]{:S(2)}) collective-permute-start(f32[64,1024]{1,0:T(8,128)S(1)} %fusion.16), channel_id=1, source_target_pairs={{0,1},{1,0},{2,3},{3,2},{4,5},{5,4},{6,7},{7,6},{8,9},{9,8},{10,11... | collective-permute-start | bytes 786440 | tf_op jit(solution)/shard_map/ppermute | solution.py:114
  27.4 0.7 %collective-permute-done.6 = f32[64,1024]{1,0:T(8,128)S(1)} collective-permute-done((f32[64,1024]{1,0:T(8,128)S(1)}, f32[64,1024]{1,0:T(8,128)S(1)}, u32[]{:S(2)}, u32[]{:S(2)}) %collective-permute-start.6) | collective-permute-done | bytes 262176 | tf_op jit(solution)/shard_map/ppermute | solution.py:114
  28.2 3.0 %collective-permute-start.7 = (f32[16,1024]{1,0:T(8,128)S(1)}, f32[16,1024]{1,0:T(8,128)S(1)}, u32[]{:S(2)}, u32[]{:S(2)}) collective-permute-start(f32[16,1024]{1,0:T(8,128)S(1)} %get-tuple-element.39), channel_id=1, source_target_pairs={{0,16},{8,24},{16,0},{24,8},{1,17},{9,25},{17,1},{25,9},{2,18},{10... | collective-permute-start | bytes 196616 | tf_op jit(solution)/shard_map/ppermute | solution.py:21
  31.6 2.3 %collective-permute-start.9 = (f32[16,1024]{1,0:T(8,128)S(1)}, f32[16,1024]{1,0:T(8,128)S(1)}, u32[]{:S(2)}, u32[]{:S(2)}) collective-permute-start(f32[16,1024]{1,0:T(8,128)S(1)} %get-tuple-element.38), channel_id=1, source_target_pairs={{0,24},{8,0},{16,8},{24,16},{1,25},{9,1},{17,9},{25,17},{2,26},{10... | collective-permute-start | bytes 196616 | tf_op jit(solution)/shard_map/ppermute | solution.py:21
  33.9 1.6 %collective-permute-done.8 = f32[16,1024]{1,0:T(8,128)S(1)} collective-permute-done((f32[16,1024]{1,0:T(8,128)S(1)}, f32[16,1024]{1,0:T(8,128)S(1)}, u32[]{:S(2)}, u32[]{:S(2)}) %collective-permute-start.8) | collective-permute-done | bytes 65568 | tf_op jit(solution)/shard_map/ppermute | solution.py:21
  35.5 6.3 %collective-permute-start.10 = (f32[16,1152]{1,0:T(8,128)S(1)}, f32[16,1152]{1,0:T(8,128)S(1)}, u32[]{:S(2)}, u32[]{:S(2)}) collective-permute-start(f32[16,1152]{1,0:T(8,128)S(1)} %pad_maximum_fusion.2), channel_id=1, source_target_pairs={{0,4},{2,6},{4,0},{6,2},{1,5},{3,7},{5,1},{7,3},{8,12},{10,14},{12... | collective-permute-start | bytes 221192 | tf_op jit(solution)/shard_map/ppermute | solution.py:21
  41.9 1.2 %collective-permute-start.11 = (f32[16,1152]{1,0:T(8,128)S(1)}, f32[16,1152]{1,0:T(8,128)S(1)}, u32[]{:S(2)}, u32[]{:S(2)}) collective-permute-start(f32[16,1152]{1,0:T(8,128)S(1)} %pad_maximum_fusion.2), channel_id=1, source_target_pairs={{0,2},{2,4},{4,6},{6,0},{1,3},{3,5},{5,7},{7,1},{8,10},{10,12},{12... | collective-permute-start | bytes 221192 | tf_op jit(solution)/shard_map/ppermute | solution.py:21
  43.1 2.4 %collective-permute-start.12 = (f32[16,1152]{1,0:T(8,128)S(1)}, f32[16,1152]{1,0:T(8,128)S(1)}, u32[]{:S(2)}, u32[]{:S(2)}) collective-permute-start(f32[16,1152]{1,0:T(8,128)S(1)} %pad_maximum_fusion.2), channel_id=1, source_target_pairs={{0,6},{2,0},{4,2},{6,4},{1,7},{3,1},{5,3},{7,5},{8,14},{10,8},{12,... | collective-permute-start | bytes 221192 | tf_op jit(solution)/shard_map/ppermute | solution.py:21
  45.5 2.5 %collective-permute-done.11 = f32[16,1152]{1,0:T(8,128)S(1)} collective-permute-done((f32[16,1152]{1,0:T(8,128)S(1)}, f32[16,1152]{1,0:T(8,128)S(1)}, u32[]{:S(2)}, u32[]{:S(2)}) %collective-permute-start.11) | collective-permute-done | bytes 73760 | tf_op jit(solution)/shard_map/ppermute | solution.py:21
  48.0 1.7 %collective-permute-done.12 = f32[16,1152]{1,0:T(8,128)S(1)} collective-permute-done((f32[16,1152]{1,0:T(8,128)S(1)}, f32[16,1152]{1,0:T(8,128)S(1)}, u32[]{:S(2)}, u32[]{:S(2)}) %collective-permute-start.12) | collective-permute-done | bytes 73760 | tf_op jit(solution)/shard_map/ppermute | solution.py:21
  49.8 1.2 %collective-permute-start.13 = (f32[16,1152]{1,0:T(8,128)S(1)}, f32[16,1152]{1,0:T(8,128)S(1)}, u32[]{:S(2)}, u32[]{:S(2)}) collective-permute-start(f32[16,1152]{1,0:T(8,128)S(1)} %add_add_fusion), channel_id=1, source_target_pairs={{0,16},{8,24},{16,0},{24,8},{1,17},{9,25},{17,1},{25,9},{2,18},{10... | collective-permute-start | bytes 221192 | tf_op jit(solution)/shard_map/ppermute | solution.py:21
  50.9 0.6 collective-permute-start.14
  51.5 2.1 %collective-permute-start.15 = (f32[16,1152]{1,0:T(8,128)S(1)}, f32[16,1152]{1,0:T(8,128)S(1)}, u32[]{:S(2)}, u32[]{:S(2)}) collective-permute-start(f32[16,1152]{1,0:T(8,128)S(1)} %add_add_fusion), channel_id=1, source_target_pairs={{0,24},{8,0},{16,8},{24,16},{1,25},{9,1},{17,9},{25,17},{2,26},{10... | collective-permute-start | bytes 221192 | tf_op jit(solution)/shard_map/ppermute | solution.py:21
  53.7 0.9 %collective-permute-done.13 = f32[16,1152]{1,0:T(8,128)S(1)} collective-permute-done((f32[16,1152]{1,0:T(8,128)S(1)}, f32[16,1152]{1,0:T(8,128)S(1)}, u32[]{:S(2)}, u32[]{:S(2)}) %collective-permute-start.13) | collective-permute-done | bytes 73760 | tf_op jit(solution)/shard_map/ppermute | solution.py:21
  54.6 0.8 %collective-permute-done.14 = f32[16,1152]{1,0:T(8,128)S(1)} collective-permute-done((f32[16,1152]{1,0:T(8,128)S(1)}, f32[16,1152]{1,0:T(8,128)S(1)}, u32[]{:S(2)}, u32[]{:S(2)}) %collective-permute-start.14) | collective-permute-done | bytes 73760 | tf_op jit(solution)/shard_map/ppermute | solution.py:21
  55.4 4.2 %collective-permute-start.16 = (f32[64,1024]{1,0:T(8,128)S(1)}, f32[64,1024]{1,0:T(8,128)S(1)}, u32[]{:S(2)}, u32[]{:S(2)}) collective-permute-start(f32[64,1024]{1,0:T(8,128)S(1)} %get-tuple-element.36), channel_id=1, source_target_pairs={{0,1},{1,0},{2,3},{3,2},{4,5},{5,4},{6,7},{7,6},{8,9},{9,8},{10,11... | collective-permute-start | bytes 786440 | tf_op jit(solution)/shard_map/ppermute | solution.py:130
  59.8 0.6 broadcast_in_dim_broadcast_in_dim.3
  60.4 3.7 %all-to-all-start.1 = ((f32[16,8,128]{2,1,0:T(8,128)}), f32[16,8,128]{2,1,0:T(8,128)S(1)}, u32[]{:S(2)}, u32[]{:S(2)}) async-start(f32[16,8,128]{2,1,0:T(8,128)} %broadcast_in_dim_broadcast_in_dim.3), calls=%async_computation.1 | async-start | bytes 131072 | tf_op jit(solution)/shard_map/all_to_all | solution.py:16
  64.9 0.8 %fusion.9 = f32[128,512]{1,0:T(8,128)} fusion(f32[384,512]{1,0:T(8,128)S(1)} %fusion, bf16[128,512]{1,0:T(8,128)(2,1)S(1)} %get-tuple-element.31, f32[128,512]{1,0:T(8,128)S(1)} %neg.6, f32[512]{0:T(512)S(1)} %get-tuple-element.23, f32[512]{0:T(512)S(1)} %multiply_reduce_fusion, f32[512]{0:T(512)S(1)} %broadcast_multiply_fusion, ...), kind=kLoop, calls=%fused_computation.15 | loop fusion | flops 720896 | bytes 1448448 | tf_op jit(solution)/shard_map/sub | solution.py:146
  65.8 4.1 %all-to-all-done.1 = f32[16,8,128]{2,1,0:T(8,128)S(1)} async-done(((f32[16,8,128]{2,1,0:T(8,128)}), f32[16,8,128]{2,1,0:T(8,128)S(1)}, u32[]{:S(2)}, u32[]{:S(2)}) %all-to-all-start.1) | async-done | bytes 65568 | tf_op jit(solution)/shard_map/all_to_all | solution.py:16
  69.9 0.6 reduce_sum.79
  (55 shorter events, 3.3 us)
Async XLA Ops:
  0.6 15.4 %collective-permute-start = (f32[128,512]{1,0:T(8,128)}, f32[128,512]{1,0:T(8,128)S(1)}, u32[]{:S(2)}, u32[]{:S(2)}) collective-permute-start(f32[128,512]{1,0:T(8,128)} %block_ref.1), channel_id=1, source_target_pairs={{0,128},{32,160},{64,192},{96,224},{128,0},{160,32},{192,64},{224,... | collective-permute-start | bytes 786440 | tf_op jit(solution)/shard_map/ppermute | solution.py:29
  3.2 12.9 %collective-permute-start.1 = (f32[128,512]{1,0:T(8,128)}, f32[128,512]{1,0:T(8,128)S(1)}, u32[]{:S(2)}, u32[]{:S(2)}) collective-permute-start(f32[128,512]{1,0:T(8,128)} %block_ref.1), channel_id=1, source_target_pairs={{0,32},{32,64},{64,96},{96,0},{128,160},{160,192},{192,224},{224,1... | collective-permute-start | bytes 786440 | tf_op jit(solution)/shard_map/ppermute | solution.py:29
  4.4 11.7 %collective-permute-start.2 = (f32[128,512]{1,0:T(8,128)}, f32[128,512]{1,0:T(8,128)S(1)}, u32[]{:S(2)}, u32[]{:S(2)}) collective-permute-start(f32[128,512]{1,0:T(8,128)} %block_ref.1), channel_id=1, source_target_pairs={{0,96},{32,0},{64,32},{96,64},{128,224},{160,128},{192,160},{224,1... | collective-permute-start | bytes 786440 | tf_op jit(solution)/shard_map/ppermute | solution.py:29
  7.5 8.5 %all-to-all-start = ((f32[8,2,512]{2,1,0:T(2,128)}), f32[8,2,512]{2,1,0:T(2,128)S(1)}, u32[]{:S(2)}, u32[]{:S(2)}) async-start(f32[8,2,512]{2,1,0:T(2,128)} %stats.1), calls=%async_computation | async-start | bytes 65536 | tf_op jit(solution)/shard_map/all_to_all | solution.py:87
  10.9 10.8 %collective-permute-start.4 = (f32[128,512]{1,0:T(8,128)}, f32[128,512]{1,0:T(8,128)S(1)}, u32[]{:S(2)}, u32[]{:S(2)}) collective-permute-start(f32[128,512]{1,0:T(8,128)} %block_ref.1), channel_id=1, source_target_pairs={{0,64},{32,96},{64,0},{96,32},{128,192},{160,224},{192,128},{224,1... | collective-permute-start | bytes 786440 | tf_op jit(solution)/shard_map/ppermute | solution.py:29
  16.3 5.4 %collective-permute-start.3 = (bf16[256,512]{1,0:T(8,128)(2,1)S(1)}, bf16[256,512]{1,0:T(8,128)(2,1)S(1)}, u32[]{:S(2)}, u32[]{:S(2)}) collective-permute-start(bf16[256,512]{1,0:T(8,128)(2,1)S(1)} %pad_maximum_fusion), channel_id=1, source_target_pairs={{0,128},{32,160},{64,192},{96,224},{128,0},{160,32},{192,64},{224,... | collective-permute-start | bytes 786440 | tf_op jit(solution)/shard_map/ppermute | solution.py:29
  16.6 5.8 %collective-permute-start.5 = (bf16[128,512]{1,0:T(8,128)(2,1)S(1)}, bf16[128,512]{1,0:T(8,128)(2,1)S(1)}, u32[]{:S(2)}, u32[]{:S(2)}) collective-permute-start(bf16[128,512]{1,0:T(8,128)(2,1)S(1)} %get-tuple-element.29), channel_id=1, source_target_pairs={{0,64},{32,96},{64,0},{96,32},{128,192},{160,224},{192,128},{224,1... | collective-permute-start | bytes 393224 | tf_op jit(solution)/shard_map/ppermute | solution.py:29
  23.1 5.0 %collective-permute-start.6 = (f32[64,1024]{1,0:T(8,128)S(1)}, f32[64,1024]{1,0:T(8,128)S(1)}, u32[]{:S(2)}, u32[]{:S(2)}) collective-permute-start(f32[64,1024]{1,0:T(8,128)S(1)} %fusion.16), channel_id=1, source_target_pairs={{0,1},{1,0},{2,3},{3,2},{4,5},{5,4},{6,7},{7,6},{8,9},{9,8},{10,11... | collective-permute-start | bytes 786440 | tf_op jit(solution)/shard_map/ppermute | solution.py:114
  28.2 5.7 %collective-permute-start.7 = (f32[16,1024]{1,0:T(8,128)S(1)}, f32[16,1024]{1,0:T(8,128)S(1)}, u32[]{:S(2)}, u32[]{:S(2)}) collective-permute-start(f32[16,1024]{1,0:T(8,128)S(1)} %get-tuple-element.39), channel_id=1, source_target_pairs={{0,16},{8,24},{16,0},{24,8},{1,17},{9,25},{17,1},{25,9},{2,18},{10... | collective-permute-start | bytes 196616 | tf_op jit(solution)/shard_map/ppermute | solution.py:21
  31.2 4.3 %collective-permute-start.8 = (f32[16,1024]{1,0:T(8,128)S(1)}, f32[16,1024]{1,0:T(8,128)S(1)}, u32[]{:S(2)}, u32[]{:S(2)}) collective-permute-start(f32[16,1024]{1,0:T(8,128)S(1)} %get-tuple-element.37), channel_id=1, source_target_pairs={{0,8},{8,16},{16,24},{24,0},{1,9},{9,17},{17,25},{25,1},{2,10},{10... | collective-permute-start | bytes 196616 | tf_op jit(solution)/shard_map/ppermute | solution.py:21
  31.6 3.9 %collective-permute-start.9 = (f32[16,1024]{1,0:T(8,128)S(1)}, f32[16,1024]{1,0:T(8,128)S(1)}, u32[]{:S(2)}, u32[]{:S(2)}) collective-permute-start(f32[16,1024]{1,0:T(8,128)S(1)} %get-tuple-element.38), channel_id=1, source_target_pairs={{0,24},{8,0},{16,8},{24,16},{1,25},{9,1},{17,9},{25,17},{2,26},{10... | collective-permute-start | bytes 196616 | tf_op jit(solution)/shard_map/ppermute | solution.py:21
  35.5 9.9 %collective-permute-start.10 = (f32[16,1152]{1,0:T(8,128)S(1)}, f32[16,1152]{1,0:T(8,128)S(1)}, u32[]{:S(2)}, u32[]{:S(2)}) collective-permute-start(f32[16,1152]{1,0:T(8,128)S(1)} %pad_maximum_fusion.2), channel_id=1, source_target_pairs={{0,4},{2,6},{4,0},{6,2},{1,5},{3,7},{5,1},{7,3},{8,12},{10,14},{12... | collective-permute-start | bytes 221192 | tf_op jit(solution)/shard_map/ppermute | solution.py:21
  41.9 6.1 %collective-permute-start.11 = (f32[16,1152]{1,0:T(8,128)S(1)}, f32[16,1152]{1,0:T(8,128)S(1)}, u32[]{:S(2)}, u32[]{:S(2)}) collective-permute-start(f32[16,1152]{1,0:T(8,128)S(1)} %pad_maximum_fusion.2), channel_id=1, source_target_pairs={{0,2},{2,4},{4,6},{6,0},{1,3},{3,5},{5,7},{7,1},{8,10},{10,12},{12... | collective-permute-start | bytes 221192 | tf_op jit(solution)/shard_map/ppermute | solution.py:21
  43.1 6.7 %collective-permute-start.12 = (f32[16,1152]{1,0:T(8,128)S(1)}, f32[16,1152]{1,0:T(8,128)S(1)}, u32[]{:S(2)}, u32[]{:S(2)}) collective-permute-start(f32[16,1152]{1,0:T(8,128)S(1)} %pad_maximum_fusion.2), channel_id=1, source_target_pairs={{0,6},{2,0},{4,2},{6,4},{1,7},{3,1},{5,3},{7,5},{8,14},{10,8},{12,... | collective-permute-start | bytes 221192 | tf_op jit(solution)/shard_map/ppermute | solution.py:21
  49.8 4.8 %collective-permute-start.13 = (f32[16,1152]{1,0:T(8,128)S(1)}, f32[16,1152]{1,0:T(8,128)S(1)}, u32[]{:S(2)}, u32[]{:S(2)}) collective-permute-start(f32[16,1152]{1,0:T(8,128)S(1)} %add_add_fusion), channel_id=1, source_target_pairs={{0,16},{8,24},{16,0},{24,8},{1,17},{9,25},{17,1},{25,9},{2,18},{10... | collective-permute-start | bytes 221192 | tf_op jit(solution)/shard_map/ppermute | solution.py:21
  50.9 4.4 %collective-permute-start.14 = (f32[16,1152]{1,0:T(8,128)S(1)}, f32[16,1152]{1,0:T(8,128)S(1)}, u32[]{:S(2)}, u32[]{:S(2)}) collective-permute-start(f32[16,1152]{1,0:T(8,128)S(1)} %add_add_fusion), channel_id=1, source_target_pairs={{0,8},{8,16},{16,24},{24,0},{1,9},{9,17},{17,25},{25,1},{2,10},{10... | collective-permute-start | bytes 221192 | tf_op jit(solution)/shard_map/ppermute | solution.py:21
  51.5 3.8 %collective-permute-start.15 = (f32[16,1152]{1,0:T(8,128)S(1)}, f32[16,1152]{1,0:T(8,128)S(1)}, u32[]{:S(2)}, u32[]{:S(2)}) collective-permute-start(f32[16,1152]{1,0:T(8,128)S(1)} %add_add_fusion), channel_id=1, source_target_pairs={{0,24},{8,0},{16,8},{24,16},{1,25},{9,1},{17,9},{25,17},{2,26},{10... | collective-permute-start | bytes 221192 | tf_op jit(solution)/shard_map/ppermute | solution.py:21
  55.4 8.7 %collective-permute-start.16 = (f32[64,1024]{1,0:T(8,128)S(1)}, f32[64,1024]{1,0:T(8,128)S(1)}, u32[]{:S(2)}, u32[]{:S(2)}) collective-permute-start(f32[64,1024]{1,0:T(8,128)S(1)} %get-tuple-element.36), channel_id=1, source_target_pairs={{0,1},{1,0},{2,3},{3,2},{4,5},{5,4},{6,7},{7,6},{8,9},{9,8},{10,11... | collective-permute-start | bytes 786440 | tf_op jit(solution)/shard_map/ppermute | solution.py:130
  60.4 9.5 %all-to-all-start.1 = ((f32[16,8,128]{2,1,0:T(8,128)}), f32[16,8,128]{2,1,0:T(8,128)S(1)}, u32[]{:S(2)}, u32[]{:S(2)}) async-start(f32[16,8,128]{2,1,0:T(8,128)} %broadcast_in_dim_broadcast_in_dim.3), calls=%async_computation.1 | async-start | bytes 131072 | tf_op jit(solution)/shard_map/all_to_all | solution.py:16

commit v7 on v6

--- a/solution.py
+++ b/solution.py
@@ -1,3 +1,5 @@
+import functools
+
 import jax
 import jax.numpy as jnp
 from jax import lax
@@ -45,6 +47,21 @@
     both = jnp.concatenate([total, squares], axis=0)
     for k in range(out_ref.shape[0]):
         out_ref[k] = both
+
+
+def share_kernel(n_all, factor, *refs):
+    blocks, out_ref = refs[:-1], refs[-1]
+    rows = blocks[0].shape[0]
+    squares = jnp.zeros((rows, 128), F32)
+    beside = jnp.zeros((1, 128), F32)
+    for block_ref in blocks:
+        for first in range(0, n_all, 128):
+            part = block_ref[:, first : first + 128]
+            squares += part * part
+        beside += block_ref[:1, n_all:]
+    share = jnp.sum(squares, axis=0, keepdims=True) * factor + beside
+    for k in range(out_ref.shape[0]):
+        out_ref[k] = jnp.broadcast_to(share, (8, 128))
 
 
 def whole(count):
@@ -99,26 +116,29 @@
     )
     centered = along_zl[:rows_here]
     far = [(raw_far - mean).astype(BF16), move(along_zl[rows_here:], 0, 2)]
-    gathered = jnp.concatenate([along_zl, along_x, move(along_x, 1, 0)] + far)
+    early = jnp.concatenate([along_zl, along_x])
+    late = jnp.concatenate([move(along_x, 1, 0)] + far)
+    gathered = jnp.concatenate([early, late])
 
     half = rows_here // 2
     piece = half // ys
 
-    def half_gram(which):
+    def half_gram(which, rows):
         own = lax.dynamic_slice_in_dim(centered, which * half, half, 0)
         own = lax.dynamic_slice_in_dim(jnp.concatenate([own, own]), y * piece, half, 0)
         return lax.dot_general(
-            own, gathered, (((1,), (1,)), ((), ())), preferred_element_type=F32
+            own, rows, (((1,), (1,)), ((), ())), preferred_element_type=F32
         )
 
-    from_pair = lax.ppermute(half_gram(1 - core), "core", SWAP)
-    from_pair, here = lax.optimization_barrier((from_pair, half_gram(core)))
-    chip_half = here + from_pair
+    from_pair = [lax.ppermute(half_gram(1 - core, rows), "core", SWAP) for rows in (early, late)]
+    here = [half_gram(core, rows) for rows in (early, late)]
+    from_pair, here = lax.optimization_barrier((from_pair, here))
+    chip_half = jnp.concatenate([a + b for a, b in zip(from_pair, here)], axis=1)
     chunks = [chip_half[k * piece : (k + 1) * piece] for k in range(ys)]
-    over_y = chunks[0] + sum(shift(chunks[k], "y", k) for k in (2, 1, 3))
+    over_y = chunks[0] + sum(shift(chunks[k], "y", k) for k in (1, 3, 2))
 
-    gathered_f32 = gathered.astype(F32)
-    col_norms = jnp.sum(gathered_f32 * gathered_f32, axis=0)
+    halves = [rows.astype(F32) for rows in (early, late)]
+    col_norms = sum(jnp.sum(rows * rows, axis=0) for rows in halves)
     block_share = (
         25.0 * lanes(jax.nn.relu(1.0 - std)) - lanes(col_norms * col_norms) / (scale * scale)
     ) / (width * rows_count)
@@ -128,19 +148,27 @@
     blocks = [mine, back[2], back[1], back[3]]
     my_half = jnp.concatenate([block[:, :n_all] for block in blocks])
     other_half = lax.ppermute(my_half, "core", SWAP)
-    blocks_share = sum(block[0, n_all:] for block in blocks)
-    share = lanes(my_half * my_half) / (scale * scale * width) + blocks_share
-    shares = spread(jnp.broadcast_to(share, (8, 128)), ROWS + ("core",), rows_count * 2)
+    shares_here = pl.pallas_call(
+        functools.partial(share_kernel, n_all, 1.0 / (float(n_all - 1) ** 2 * width)),
+        out_shape=jax.ShapeDtypeStruct((rows_count * 2, 8, 128), F32),
+        in_specs=whole(ys),
+        out_specs=whole(1)[0],
+        name="share",
+    )(*(pltpu.with_memory_space_constraint(block, pltpu.VMEM) for block in blocks))
+    shares = lax.all_to_all(shares_here, ROWS + ("core",), 0, 0)
 
-    gram = jnp.zeros((rows_here, n_all), F32)
-    for k, away in enumerate((0, 2, 1, 3)):
-        owner = lax.rem(y + ys - away, ys)
-        for c, rows in enumerate((my_half, other_half)):
-            block = rows[k * piece : (k + 1) * piece]
-            start = lax.rem(core + c, 2) * half + owner * piece
-            gram = lax.dynamic_update_slice_in_dim(gram, block, start, 0)
-    terms = jnp.dot(three_terms(gram), gathered, preferred_element_type=F32)
-    product = terms[:rows_here] + terms[rows_here : 2 * rows_here] + terms[2 * rows_here :]
+    product = jnp.zeros((rows_here, col_width), F32)
+    for c, rows in enumerate((my_half, other_half)):
+        gram = jnp.zeros((half, n_all), F32)
+        for k, away in enumerate((0, 2, 1, 3)):
+            owner = lax.rem(y + ys - away, ys)
+            gram = lax.dynamic_update_slice_in_dim(
+                gram, rows[k * piece : (k + 1) * piece], owner * piece, 0
+            )
+        terms = jnp.dot(three_terms(gram), gathered, preferred_element_type=F32)
+        part = terms[:half] + terms[half : 2 * half] + terms[2 * half :]
+        start = lax.rem(core + c, 2) * half
+        product = lax.dynamic_update_slice_in_dim(product, part, start, 0)
     grad_cov = (product - centered.astype(F32) * col_norms) / scale
     hinge = jnp.where(std < 1.0, cz / std, F32(0.0))
     grad_scaled = 4.0 / 25.0 * grad_cov - hinge

time: 70.8 us -> 69.8 us (0.986)
  waiting for transfers between devices: 18.2 us -> 14.7 us
  starting transfers between devices: 44.1 us -> 47.2 us
  other arithmetic: 3.35 us -> 2.34 us
    all_to_all x1, starting transfers between devices: 3.68 us -> 7.68 us  [on_device(): shares = lax.all_to_all(shares_here, ROWS + ('core',), 0, 0)]
    ppermute x1, starting transfers between devices: 4.19 us -> 0.2 us  [on_device(): other_half = lax.ppermute(my_half, 'core', SWAP)]
    ppermute x6, waiting for transfers between devices: 4.51 us -> 0.67 us  [move(): lax.ppermute(block, ROWS, [(z * xs + x, (z + along_zl) % zls * xs + (x +...]
    ppermute x1 -> x2, starting transfers between devices: 3.85 us -> 6.99 us  [on_device(): lax.ppermute(half_gram(1 - core, rows), 'core', SWAP)]
    all_to_all x1, waiting for transfers between devices: 4.12 us -> 2.74 us  [on_device(): shares = lax.all_to_all(shares_here, ROWS + ('core',), 0, 0)]
    neg x1, other arithmetic: 1 us -> 0.02 us  [on_device(): stats, raw, minus = lax.optimization_barrier((stats, raw, -embeddings))]
    all_to_all x1, waiting for transfers between devices: 1.3 us -> 2.24 us  [on_device(): stats = lax.all_to_all(stats_here, ROWS, 0, 0)]
    ppermute x1, waiting for transfers between devices: 0.01 us -> 0.91 us  [on_device(): other_half = lax.ppermute(my_half, 'core', SWAP)]
  transfers between devices with their start and end apart: 19 -> 20, of which waited for: 10 -> 11; matrix products, arithmetic and copies ran while one was open for 6% -> 5% of each run, Pallas kernels for 2% -> 2%
where the time goes in v7:
time: 69.8 us; the launch traced here: 69.6 us
  starting transfers between devices  47.2 us (68%)
  waiting for transfers between devices  14.7 us (21%)
  other arithmetic  2.34 us (3%)
  Pallas kernels  2.33 us (3%)
  matrix products  1.78 us (3%)
  between operations  1.01 us (1%)
    ppermute x9, starting transfers between devices, shift(): return lax.ppermute(block, axis, [(i, (i + k) % size) for i in range(size)])  19.5 us
    ppermute x6, starting transfers between devices, move(): lax.ppermute(block, ROWS, [(z * xs + x, (z + along_zl) % zls * xs + (x +...  9.53 us
    all_to_all x1, starting transfers between devices, on_device(): shares = lax.all_to_all(shares_here, ROWS + ('core',), 0, 0)  7.68 us
    ppermute x9, waiting for transfers between devices, shift(): return lax.ppermute(block, axis, [(i, (i + k) % size) for i in range(size)])  7.58 us
    ppermute x2, starting transfers between devices, on_device(): lax.ppermute(half_gram(1 - core, rows), 'core', SWAP)  6.99 us
    all_to_all x1, starting transfers between devices, on_device(): stats = lax.all_to_all(stats_here, ROWS, 0, 0)  3.34 us
    all_to_all x1, waiting for transfers between devices, on_device(): shares = lax.all_to_all(shares_here, ROWS + ('core',), 0, 0)  2.74 us
    all_to_all x1, waiting for transfers between devices, on_device(): stats = lax.all_to_all(stats_here, ROWS, 0, 0)  2.24 us
  transfers between devices with their start and end apart: 20, of which 11 were waited for; matrix products, arithmetic and copies ran while one was open for 5% of the time, Pallas kernels for 2%

profile of v7, /device:TPU:1, one launch (start us, length us, event | category | flops | bytes accessed | tf_op | source)
XLA Modules:
  0.0 69.6 jit_solution(4166470187877981054)
XLA Ops:
  0.6 2.6 %collective-permute-start = (f32[128,512]{1,0:T(8,128)}, f32[128,512]{1,0:T(8,128)S(1)}, u32[]{:S(2)}, u32[]{:S(2)}) collective-permute-start(f32[128,512]{1,0:T(8,128)} %block_ref.1), channel_id=1, source_target_pairs={{0,128},{32,160},{64,192},{96,224},{128,0},{160,32},{192,64},{224,... | collective-permute-start | bytes 786440 | tf_op jit(solution)/shard_map/ppermute | solution.py:31
  3.2 1.2 %collective-permute-start.1 = (f32[128,512]{1,0:T(8,128)}, f32[128,512]{1,0:T(8,128)S(1)}, u32[]{:S(2)}, u32[]{:S(2)}) collective-permute-start(f32[128,512]{1,0:T(8,128)} %block_ref.1), channel_id=1, source_target_pairs={{0,32},{32,64},{64,96},{96,0},{128,160},{160,192},{192,224},{224,1... | collective-permute-start | bytes 786440 | tf_op jit(solution)/shard_map/ppermute | solution.py:31
  4.4 1.5 %collective-permute-start.2 = (f32[128,512]{1,0:T(8,128)}, f32[128,512]{1,0:T(8,128)S(1)}, u32[]{:S(2)}, u32[]{:S(2)}) collective-permute-start(f32[128,512]{1,0:T(8,128)} %block_ref.1), channel_id=1, source_target_pairs={{0,96},{32,0},{64,32},{96,64},{128,224},{160,128},{192,160},{224,1... | collective-permute-start | bytes 786440 | tf_op jit(solution)/shard_map/ppermute | solution.py:31
  5.9 1.7 %stats.1 = f32[8,2,512]{2,1,0:T(2,128)} custom-call(f32[128,512]{1,0:T(8,128)} %block_ref.1), custom_call_target="tpu_custom_call" | custom-call | tf_op jit(solution)/shard_map/stats/pallas_call | solution.py:97
  7.5 3.3 %all-to-all-start = ((f32[8,2,512]{2,1,0:T(2,128)}), f32[8,2,512]{2,1,0:T(2,128)S(1)}, u32[]{:S(2)}, u32[]{:S(2)}) async-start(f32[8,2,512]{2,1,0:T(2,128)} %stats.1), calls=%async_computation | async-start | bytes 65536 | tf_op jit(solution)/shard_map/all_to_all | solution.py:104
  10.9 2.9 %collective-permute-start.5 = (f32[128,512]{1,0:T(8,128)S(1)}, f32[128,512]{1,0:T(8,128)S(1)}, u32[]{:S(2)}, u32[]{:S(2)}) collective-permute-start(f32[128,512]{1,0:T(8,128)S(1)} %copy-done), channel_id=1, source_target_pairs={{0,64},{32,96},{64,0},{96,32},{128,192},{160,224},{192,128},{224,1... | collective-permute-start | bytes 786440 | tf_op jit(solution)/shard_map/ppermute | solution.py:31
  13.8 2.2 %all-to-all-done = f32[8,2,512]{2,1,0:T(2,128)S(1)} async-done(((f32[8,2,512]{2,1,0:T(2,128)}), f32[8,2,512]{2,1,0:T(2,128)S(1)}, u32[]{:S(2)}, u32[]{:S(2)}) %all-to-all-start) | async-done | bytes 32800 | tf_op jit(solution)/shard_map/all_to_all | solution.py:104
  16.6 1.1 %collective-permute-start.6 = (bf16[128,512]{1,0:T(8,128)(2,1)S(1)}, bf16[128,512]{1,0:T(8,128)(2,1)S(1)}, u32[]{:S(2)}, u32[]{:S(2)}) collective-permute-start(bf16[128,512]{1,0:T(8,128)(2,1)S(1)} %get-tuple-element.39), channel_id=1, source_target_pairs={{0,64},{32,96},{64,0},{96,32},{128,192},{160,224},{192,128},{224,1... | collective-permute-start | bytes 393224 | tf_op jit(solution)/shard_map/ppermute | solution.py:31
  18.5 3.0 %collective-permute-start.3 = (f32[64,512]{1,0:T(8,128)S(1)}, f32[64,512]{1,0:T(8,128)S(1)}, u32[]{:S(2)}, u32[]{:S(2)}) collective-permute-start(f32[64,512]{1,0:T(8,128)S(1)} %fusion.27), channel_id=1, source_target_pairs={{0,1},{1,0},{2,3},{3,2},{4,5},{5,4},{6,7},{7,6},{8,9},{9,8},{10,11... | collective-permute-start | bytes 393224 | tf_op jit(solution)/shard_map/ppermute | solution.py:133
  21.7 0.6 collective-permute-done.6
  22.5 4.0 %collective-permute-start.7 = (f32[64,512]{1,0:T(8,128)S(1)}, f32[64,512]{1,0:T(8,128)S(1)}, u32[]{:S(2)}, u32[]{:S(2)}) collective-permute-start(f32[64,512]{1,0:T(8,128)S(1)} %fusion.29), channel_id=1, source_target_pairs={{0,1},{1,0},{2,3},{3,2},{4,5},{5,4},{6,7},{7,6},{8,9},{9,8},{10,11... | collective-permute-start | bytes 393224 | tf_op jit(solution)/shard_map/ppermute | solution.py:133
  27.0 0.5 collective-permute-done.7
  27.6 3.0 %collective-permute-start.10 = (f32[16,1024]{1,0:T(8,128)S(1)}, f32[16,1024]{1,0:T(8,128)S(1)}, u32[]{:S(2)}, u32[]{:S(2)}) collective-permute-start(f32[16,1024]{1,0:T(8,128)S(1)} %get-tuple-element.50), channel_id=1, source_target_pairs={{0,16},{8,24},{16,0},{24,8},{1,17},{9,25},{17,1},{25,9},{2,18},{10... | collective-permute-start | bytes 196616 | tf_op jit(solution)/shard_map/ppermute | solution.py:23
  30.6 0.4 collective-permute-start.8
  31.0 2.3 %collective-permute-start.9 = (f32[16,1024]{1,0:T(8,128)S(1)}, f32[16,1024]{1,0:T(8,128)S(1)}, u32[]{:S(2)}, u32[]{:S(2)}) collective-permute-start(f32[16,1024]{1,0:T(8,128)S(1)} %get-tuple-element.48), channel_id=1, source_target_pairs={{0,24},{8,0},{16,8},{24,16},{1,25},{9,1},{17,9},{25,17},{2,26},{10... | collective-permute-start | bytes 196616 | tf_op jit(solution)/shard_map/ppermute | solution.py:23
  33.3 1.6 %collective-permute-done.8 = f32[16,1024]{1,0:T(8,128)S(1)} collective-permute-done((f32[16,1024]{1,0:T(8,128)S(1)}, f32[16,1024]{1,0:T(8,128)S(1)}, u32[]{:S(2)}, u32[]{:S(2)}) %collective-permute-start.8) | collective-permute-done | bytes 65568 | tf_op jit(solution)/shard_map/ppermute | solution.py:23
  34.9 6.3 %collective-permute-start.11 = (f32[16,1152]{1,0:T(8,128)S(1)}, f32[16,1152]{1,0:T(8,128)S(1)}, u32[]{:S(2)}, u32[]{:S(2)}) collective-permute-start(f32[16,1152]{1,0:T(8,128)S(1)} %pad_maximum_fusion.4), channel_id=1, source_target_pairs={{0,4},{2,6},{4,0},{6,2},{1,5},{3,7},{5,1},{7,3},{8,12},{10,14},{12... | collective-permute-start | bytes 221192 | tf_op jit(solution)/shard_map/ppermute | solution.py:23
  41.3 1.2 %collective-permute-start.12 = (f32[16,1152]{1,0:T(8,128)S(1)}, f32[16,1152]{1,0:T(8,128)S(1)}, u32[]{:S(2)}, u32[]{:S(2)}) collective-permute-start(f32[16,1152]{1,0:T(8,128)S(1)} %pad_maximum_fusion.4), channel_id=1, source_target_pairs={{0,2},{2,4},{4,6},{6,0},{1,3},{3,5},{5,7},{7,1},{8,10},{10,12},{12... | collective-permute-start | bytes 221192 | tf_op jit(solution)/shard_map/ppermute | solution.py:23
  42.5 2.4 %collective-permute-start.13 = (f32[16,1152]{1,0:T(8,128)S(1)}, f32[16,1152]{1,0:T(8,128)S(1)}, u32[]{:S(2)}, u32[]{:S(2)}) collective-permute-start(f32[16,1152]{1,0:T(8,128)S(1)} %pad_maximum_fusion.4), channel_id=1, source_target_pairs={{0,6},{2,0},{4,2},{6,4},{1,7},{3,1},{5,3},{7,5},{8,14},{10,8},{12,... | collective-permute-start | bytes 221192 | tf_op jit(solution)/shard_map/ppermute | solution.py:23
  44.9 2.5 %collective-permute-done.12 = f32[16,1152]{1,0:T(8,128)S(1)} collective-permute-done((f32[16,1152]{1,0:T(8,128)S(1)}, f32[16,1152]{1,0:T(8,128)S(1)}, u32[]{:S(2)}, u32[]{:S(2)}) %collective-permute-start.12) | collective-permute-done | bytes 73760 | tf_op jit(solution)/shard_map/ppermute | solution.py:23
  47.4 1.7 %collective-permute-done.13 = f32[16,1152]{1,0:T(8,128)S(1)} collective-permute-done((f32[16,1152]{1,0:T(8,128)S(1)}, f32[16,1152]{1,0:T(8,128)S(1)}, u32[]{:S(2)}, u32[]{:S(2)}) %collective-permute-start.13) | collective-permute-done | bytes 73760 | tf_op jit(solution)/shard_map/ppermute | solution.py:23
  49.2 1.2 %collective-permute-start.14 = (f32[16,1152]{1,0:T(8,128)S(1)}, f32[16,1152]{1,0:T(8,128)S(1)}, u32[]{:S(2)}, u32[]{:S(2)}) collective-permute-start(f32[16,1152]{1,0:T(8,128)S(1)} %add_add_fusion.refs_0_), channel_id=1, source_target_pairs={{0,16},{8,24},{16,0},{24,8},{1,17},{9,25},{17,1},{25,9},{2,18},{10... | collective-permute-start | bytes 221192 | tf_op jit(solution)/shard_map/ppermute | solution.py:23
  50.4 0.6 collective-permute-start.15
  51.0 2.1 %collective-permute-start.16 = (f32[16,1152]{1,0:T(8,128)S(1)}, f32[16,1152]{1,0:T(8,128)S(1)}, u32[]{:S(2)}, u32[]{:S(2)}) collective-permute-start(f32[16,1152]{1,0:T(8,128)S(1)} %add_add_fusion.refs_0_), channel_id=1, source_target_pairs={{0,24},{8,0},{16,8},{24,16},{1,25},{9,1},{17,9},{25,17},{2,26},{10... | collective-permute-start | bytes 221192 | tf_op jit(solution)/shard_map/ppermute | solution.py:23
  53.1 0.9 %collective-permute-done.14.refs_1_ = f32[16,1152]{1,0:T(8,128)S(1)} collective-permute-done((f32[16,1152]{1,0:T(8,128)S(1)}, f32[16,1152]{1,0:T(8,128)S(1)}, u32[]{:S(2)}, u32[]{:S(2)}) %collective-permute-start.14) | collective-permute-done | bytes 73760 | tf_op jit(solution)/shard_map/ppermute | solution.py:23
  54.0 0.8 %collective-permute-done.15.refs_2_ = f32[16,1152]{1,0:T(8,128)S(1)} collective-permute-done((f32[16,1152]{1,0:T(8,128)S(1)}, f32[16,1152]{1,0:T(8,128)S(1)}, u32[]{:S(2)}, u32[]{:S(2)}) %collective-permute-start.15) | collective-permute-done | bytes 73760 | tf_op jit(solution)/shard_map/ppermute | solution.py:23
  54.8 0.7 share.1
  55.5 7.7 %all-to-all-start.1 = ((f32[16,8,128]{2,1,0:T(8,128)}), f32[16,8,128]{2,1,0:T(8,128)S(1)}, u32[]{:S(2)}, u32[]{:S(2)}) async-start(f32[16,8,128]{2,1,0:T(8,128)} %share.1), calls=%async_computation.1 | async-start | bytes 131072 | tf_op jit(solution)/shard_map/all_to_all | solution.py:158
  63.9 0.9 %collective-permute-done.17 = f32[64,1024]{1,0:T(8,128)S(1)} collective-permute-done((f32[64,1024]{1,0:T(8,128)S(1)}, f32[64,1024]{1,0:T(8,128)S(1)}, u32[]{:S(2)}, u32[]{:S(2)}) %collective-permute-start.17) | collective-permute-done | bytes 262176 | tf_op jit(solution)/shard_map/ppermute | solution.py:150
  65.4 0.8 %select_subtract_fusion = f32[128,512]{1,0:T(8,128)} fusion(f32[128,512]{1,0:T(8,128)S(1)} %fusion.15, bf16[128,512]{1,0:T(8,128)(2,1)S(1)} %get-tuple-element.41, f32[128,512]{1,0:T(8,128)S(1)} %neg.6, f32[512]{0:T(512)S(1)} %get-tuple-element.27, f32[512]{0:T(512)S(1)} %get-tuple-element.29, f32[512]{0:T(512)S(1)} %broadcast_multiply_fusion, ...), kind=kLoop, calls=%fused_computation.34 | loop fusion | flops 589824 | bytes 924160 | tf_op jit(solution)/shard_map/sub | solution.py:174
  66.2 2.7 %all-to-all-done.1 = f32[16,8,128]{2,1,0:T(8,128)S(1)} async-done(((f32[16,8,128]{2,1,0:T(8,128)}), f32[16,8,128]{2,1,0:T(8,128)S(1)}, u32[]{:S(2)}, u32[]{:S(2)}) %all-to-all-start.1) | async-done | bytes 65568 | tf_op jit(solution)/shard_map/all_to_all | solution.py:158
  69.0 0.6 slice_reduce_fusion.2
  (62 shorter events, 3.5 us)
Async XLA Ops:
  0.6 10.3 %copy-start = (f32[128,512]{1,0:T(8,128)S(1)}, f32[128,512]{1,0:T(8,128)}, u32[]{:S(2)}) copy-start(f32[128,512]{1,0:T(8,128)} %block_ref.1) | copy-start | bytes 786436
  0.6 15.4 %collective-permute-start = (f32[128,512]{1,0:T(8,128)}, f32[128,512]{1,0:T(8,128)S(1)}, u32[]{:S(2)}, u32[]{:S(2)}) collective-permute-start(f32[128,512]{1,0:T(8,128)} %block_ref.1), channel_id=1, source_target_pairs={{0,128},{32,160},{64,192},{96,224},{128,0},{160,32},{192,64},{224,... | collective-permute-start | bytes 786440 | tf_op jit(solution)/shard_map/ppermute | solution.py:31
  3.2 12.9 %collective-permute-start.1 = (f32[128,512]{1,0:T(8,128)}, f32[128,512]{1,0:T(8,128)S(1)}, u32[]{:S(2)}, u32[]{:S(2)}) collective-permute-start(f32[128,512]{1,0:T(8,128)} %block_ref.1), channel_id=1, source_target_pairs={{0,32},{32,64},{64,96},{96,0},{128,160},{160,192},{192,224},{224,1... | collective-permute-start | bytes 786440 | tf_op jit(solution)/shard_map/ppermute | solution.py:31
  4.4 11.7 %collective-permute-start.2 = (f32[128,512]{1,0:T(8,128)}, f32[128,512]{1,0:T(8,128)S(1)}, u32[]{:S(2)}, u32[]{:S(2)}) collective-permute-start(f32[128,512]{1,0:T(8,128)} %block_ref.1), channel_id=1, source_target_pairs={{0,96},{32,0},{64,32},{96,64},{128,224},{160,128},{192,160},{224,1... | collective-permute-start | bytes 786440 | tf_op jit(solution)/shard_map/ppermute | solution.py:31
  7.5 8.5 %all-to-all-start = ((f32[8,2,512]{2,1,0:T(2,128)}), f32[8,2,512]{2,1,0:T(2,128)S(1)}, u32[]{:S(2)}, u32[]{:S(2)}) async-start(f32[8,2,512]{2,1,0:T(2,128)} %stats.1), calls=%async_computation | async-start | bytes 65536 | tf_op jit(solution)/shard_map/all_to_all | solution.py:104
  10.9 10.8 %collective-permute-start.5 = (f32[128,512]{1,0:T(8,128)S(1)}, f32[128,512]{1,0:T(8,128)S(1)}, u32[]{:S(2)}, u32[]{:S(2)}) collective-permute-start(f32[128,512]{1,0:T(8,128)S(1)} %copy-done), channel_id=1, source_target_pairs={{0,64},{32,96},{64,0},{96,32},{128,192},{160,224},{192,128},{224,1... | collective-permute-start | bytes 786440 | tf_op jit(solution)/shard_map/ppermute | solution.py:31
  16.3 5.3 %collective-permute-start.4 = (bf16[256,512]{1,0:T(8,128)(2,1)S(1)}, bf16[256,512]{1,0:T(8,128)(2,1)S(1)}, u32[]{:S(2)}, u32[]{:S(2)}) collective-permute-start(bf16[256,512]{1,0:T(8,128)(2,1)S(1)} %pad_maximum_fusion.2), channel_id=1, source_target_pairs={{0,128},{32,160},{64,192},{96,224},{128,0},{160,32},{192,64},{224,... | collective-permute-start | bytes 786440 | tf_op jit(solution)/shard_map/ppermute | solution.py:31
  16.6 5.7 %collective-permute-start.6 = (bf16[128,512]{1,0:T(8,128)(2,1)S(1)}, bf16[128,512]{1,0:T(8,128)(2,1)S(1)}, u32[]{:S(2)}, u32[]{:S(2)}) collective-permute-start(bf16[128,512]{1,0:T(8,128)(2,1)S(1)} %get-tuple-element.39), channel_id=1, source_target_pairs={{0,64},{32,96},{64,0},{96,32},{128,192},{160,224},{192,128},{224,1... | collective-permute-start | bytes 393224 | tf_op jit(solution)/shard_map/ppermute | solution.py:31
  18.5 8.5 %collective-permute-start.3 = (f32[64,512]{1,0:T(8,128)S(1)}, f32[64,512]{1,0:T(8,128)S(1)}, u32[]{:S(2)}, u32[]{:S(2)}) collective-permute-start(f32[64,512]{1,0:T(8,128)S(1)} %fusion.27), channel_id=1, source_target_pairs={{0,1},{1,0},{2,3},{3,2},{4,5},{5,4},{6,7},{7,6},{8,9},{9,8},{10,11... | collective-permute-start | bytes 393224 | tf_op jit(solution)/shard_map/ppermute | solution.py:133
  22.5 4.9 %collective-permute-start.7 = (f32[64,512]{1,0:T(8,128)S(1)}, f32[64,512]{1,0:T(8,128)S(1)}, u32[]{:S(2)}, u32[]{:S(2)}) collective-permute-start(f32[64,512]{1,0:T(8,128)S(1)} %fusion.29), channel_id=1, source_target_pairs={{0,1},{1,0},{2,3},{3,2},{4,5},{5,4},{6,7},{7,6},{8,9},{9,8},{10,11... | collective-permute-start | bytes 393224 | tf_op jit(solution)/shard_map/ppermute | solution.py:133
  27.6 5.7 %collective-permute-start.10 = (f32[16,1024]{1,0:T(8,128)S(1)}, f32[16,1024]{1,0:T(8,128)S(1)}, u32[]{:S(2)}, u32[]{:S(2)}) collective-permute-start(f32[16,1024]{1,0:T(8,128)S(1)} %get-tuple-element.50), channel_id=1, source_target_pairs={{0,16},{8,24},{16,0},{24,8},{1,17},{9,25},{17,1},{25,9},{2,18},{10... | collective-permute-start | bytes 196616 | tf_op jit(solution)/shard_map/ppermute | solution.py:23
  30.6 4.3 %collective-permute-start.8 = (f32[16,1024]{1,0:T(8,128)S(1)}, f32[16,1024]{1,0:T(8,128)S(1)}, u32[]{:S(2)}, u32[]{:S(2)}) collective-permute-start(f32[16,1024]{1,0:T(8,128)S(1)} %get-tuple-element.49), channel_id=1, source_target_pairs={{0,8},{8,16},{16,24},{24,0},{1,9},{9,17},{17,25},{25,1},{2,10},{10... | collective-permute-start | bytes 196616 | tf_op jit(solution)/shard_map/ppermute | solution.py:23
  31.0 3.9 %collective-permute-start.9 = (f32[16,1024]{1,0:T(8,128)S(1)}, f32[16,1024]{1,0:T(8,128)S(1)}, u32[]{:S(2)}, u32[]{:S(2)}) collective-permute-start(f32[16,1024]{1,0:T(8,128)S(1)} %get-tuple-element.48), channel_id=1, source_target_pairs={{0,24},{8,0},{16,8},{24,16},{1,25},{9,1},{17,9},{25,17},{2,26},{10... | collective-permute-start | bytes 196616 | tf_op jit(solution)/shard_map/ppermute | solution.py:23
  34.9 9.9 %collective-permute-start.11 = (f32[16,1152]{1,0:T(8,128)S(1)}, f32[16,1152]{1,0:T(8,128)S(1)}, u32[]{:S(2)}, u32[]{:S(2)}) collective-permute-start(f32[16,1152]{1,0:T(8,128)S(1)} %pad_maximum_fusion.4), channel_id=1, source_target_pairs={{0,4},{2,6},{4,0},{6,2},{1,5},{3,7},{5,1},{7,3},{8,12},{10,14},{12... | collective-permute-start | bytes 221192 | tf_op jit(solution)/shard_map/ppermute | solution.py:23
  41.3 6.1 %collective-permute-start.12 = (f32[16,1152]{1,0:T(8,128)S(1)}, f32[16,1152]{1,0:T(8,128)S(1)}, u32[]{:S(2)}, u32[]{:S(2)}) collective-permute-start(f32[16,1152]{1,0:T(8,128)S(1)} %pad_maximum_fusion.4), channel_id=1, source_target_pairs={{0,2},{2,4},{4,6},{6,0},{1,3},{3,5},{5,7},{7,1},{8,10},{10,12},{12... | collective-permute-start | bytes 221192 | tf_op jit(solution)/shard_map/ppermute | solution.py:23
  42.5 6.7 %collective-permute-start.13 = (f32[16,1152]{1,0:T(8,128)S(1)}, f32[16,1152]{1,0:T(8,128)S(1)}, u32[]{:S(2)}, u32[]{:S(2)}) collective-permute-start(f32[16,1152]{1,0:T(8,128)S(1)} %pad_maximum_fusion.4), channel_id=1, source_target_pairs={{0,6},{2,0},{4,2},{6,4},{1,7},{3,1},{5,3},{7,5},{8,14},{10,8},{12,... | collective-permute-start | bytes 221192 | tf_op jit(solution)/shard_map/ppermute | solution.py:23
  49.2 4.8 %collective-permute-start.14 = (f32[16,1152]{1,0:T(8,128)S(1)}, f32[16,1152]{1,0:T(8,128)S(1)}, u32[]{:S(2)}, u32[]{:S(2)}) collective-permute-start(f32[16,1152]{1,0:T(8,128)S(1)} %add_add_fusion.refs_0_), channel_id=1, source_target_pairs={{0,16},{8,24},{16,0},{24,8},{1,17},{9,25},{17,1},{25,9},{2,18},{10... | collective-permute-start | bytes 221192 | tf_op jit(solution)/shard_map/ppermute | solution.py:23
  50.4 4.4 %collective-permute-start.15 = (f32[16,1152]{1,0:T(8,128)S(1)}, f32[16,1152]{1,0:T(8,128)S(1)}, u32[]{:S(2)}, u32[]{:S(2)}) collective-permute-start(f32[16,1152]{1,0:T(8,128)S(1)} %add_add_fusion.refs_0_), channel_id=1, source_target_pairs={{0,8},{8,16},{16,24},{24,0},{1,9},{9,17},{17,25},{25,1},{2,10},{10... | collective-permute-start | bytes 221192 | tf_op jit(solution)/shard_map/ppermute | solution.py:23
  51.0 3.8 %collective-permute-start.16 = (f32[16,1152]{1,0:T(8,128)S(1)}, f32[16,1152]{1,0:T(8,128)S(1)}, u32[]{:S(2)}, u32[]{:S(2)}) collective-permute-start(f32[16,1152]{1,0:T(8,128)S(1)} %add_add_fusion.refs_0_), channel_id=1, source_target_pairs={{0,24},{8,0},{16,8},{24,16},{1,25},{9,1},{17,9},{25,17},{2,26},{10... | collective-permute-start | bytes 221192 | tf_op jit(solution)/shard_map/ppermute | solution.py:23
  55.5 13.5 %all-to-all-start.1 = ((f32[16,8,128]{2,1,0:T(8,128)}), f32[16,8,128]{2,1,0:T(8,128)S(1)}, u32[]{:S(2)}, u32[]{:S(2)}) async-start(f32[16,8,128]{2,1,0:T(8,128)} %share.1), calls=%async_computation.1 | async-start | bytes 131072 | tf_op jit(solution)/shard_map/all_to_all | solution.py:158
  63.2 1.6 %collective-permute-start.17 = (f32[64,1024]{1,0:T(8,128)S(1)}, f32[64,1024]{1,0:T(8,128)S(1)}, u32[]{:S(2)}, u32[]{:S(2)}) collective-permute-start(f32[64,1024]{1,0:T(8,128)S(1)} %pad_maximum_fusion.3), channel_id=1, source_target_pairs={{0,1},{1,0},{2,3},{3,2},{4,5},{5,4},{6,7},{7,6},{8,9},{9,8},{10,11... | collective-permute-start | bytes 786440 | tf_op jit(solution)/shard_map/ppermute | solution.py:150

commit v8 on v7

--- a/solution.py
+++ b/solution.py
@@ -91,9 +91,6 @@
     width = col_width * cols_count
     scale = F32(n_all - 1)
 
-    raw = [move(embeddings, *by) for by in RAW_MOVES]
-    raw_far = move(embeddings, 0, 2)
-
     stats_here = pl.pallas_call(
         stats_kernel,
         out_shape=jax.ShapeDtypeStruct((rows_count, 2, col_width), F32),
@@ -101,6 +98,9 @@
         out_specs=whole(1)[0],
         name="stats",
     )(embeddings)
+    stats_here, sent = lax.optimization_barrier((stats_here, embeddings))
+    raw = [move(sent, *by) for by in RAW_MOVES]
+    raw_far = move(sent, 0, 2)
     stats = lax.all_to_all(stats_here, ROWS, 0, 0)
     stats, raw, minus = lax.optimization_barrier((stats, raw, -embeddings))
     sums, squares = stats[:, 0], stats[:, 1]

time: 69.8 us -> 69.8 us (level)
  transfers between devices with their start and end apart: 20 -> 20, of which waited for: 11 -> 11; matrix products, arithmetic and copies ran while one was open for 5% -> 5% of each run, Pallas kernels for 2% -> 0%
where the time goes in v8:
time: 69.8 us; the launch traced here: 69.5 us
  starting transfers between devices  46.9 us (67%)
  waiting for transfers between devices  14.9 us (21%)
  Pallas kernels  2.36 us (3%)
  other arithmetic  2.34 us (3%)
  matrix products  1.78 us (3%)
  between operations  1 us (1%)
    ppermute x9, starting transfers between devices, shift(): return lax.ppermute(block, axis, [(i, (i + k) % size) for i in range(size)])  19.5 us
    ppermute x6, starting transfers between devices, move(): lax.ppermute(block, ROWS, [(z * xs + x, (z + along_zl) % zls * xs + (x +...  9.45 us
    all_to_all x1, starting transfers between devices, on_device(): shares = lax.all_to_all(shares_here, ROWS + ('core',), 0, 0)  7.69 us
    ppermute x9, waiting for transfers between devices, shift(): return lax.ppermute(block, axis, [(i, (i + k) % size) for i in range(size)])  7.6 us
    ppermute x2, starting transfers between devices, on_device(): lax.ppermute(half_gram(1 - core, rows), 'core', SWAP)  6.81 us
    all_to_all x1, starting transfers between devices, on_device(): stats = lax.all_to_all(stats_here, ROWS, 0, 0)  3.34 us
    all_to_all x1, waiting for transfers between devices, on_device(): shares = lax.all_to_all(shares_here, ROWS + ('core',), 0, 0)  2.74 us
    all_to_all x1, waiting for transfers between devices, on_device(): stats = lax.all_to_all(stats_here, ROWS, 0, 0)  2.25 us
  transfers between devices with their start and end apart: 20, of which 11 were waited for; matrix products, arithmetic and copies ran while one was open for 5% of the time, Pallas kernels for 0%

profile of v8, /device:TPU:1, one launch (start us, length us, event | category | flops | bytes accessed | tf_op | source)
XLA Modules:
  0.0 69.5 jit_solution(17709218685555759818)
XLA Ops:
  0.6 1.7 %stats.1 = f32[8,2,512]{2,1,0:T(2,128)} custom-call(f32[128,512]{1,0:T(8,128)} %block_ref.1), custom_call_target="tpu_custom_call" | custom-call | tf_op jit(solution)/shard_map/stats/pallas_call | solution.py:94
  2.3 2.5 %collective-permute-start = (f32[128,512]{1,0:T(8,128)S(1)}, f32[128,512]{1,0:T(8,128)S(1)}, u32[]{:S(2)}, u32[]{:S(2)}) collective-permute-start(f32[128,512]{1,0:T(8,128)S(1)} %copy-done), channel_id=1, source_target_pairs={{0,128},{32,160},{64,192},{96,224},{128,0},{160,32},{192,64},{224,... | collective-permute-start | bytes 786440 | tf_op jit(solution)/shard_map/ppermute | solution.py:31
  4.8 1.2 %collective-permute-start.1 = (f32[128,512]{1,0:T(8,128)S(1)}, f32[128,512]{1,0:T(8,128)S(1)}, u32[]{:S(2)}, u32[]{:S(2)}) collective-permute-start(f32[128,512]{1,0:T(8,128)S(1)} %copy-done), channel_id=1, source_target_pairs={{0,32},{32,64},{64,96},{96,0},{128,160},{160,192},{192,224},{224,1... | collective-permute-start | bytes 786440 | tf_op jit(solution)/shard_map/ppermute | solution.py:31
  6.0 1.5 %collective-permute-start.2 = (f32[128,512]{1,0:T(8,128)S(1)}, f32[128,512]{1,0:T(8,128)S(1)}, u32[]{:S(2)}, u32[]{:S(2)}) collective-permute-start(f32[128,512]{1,0:T(8,128)S(1)} %copy-done), channel_id=1, source_target_pairs={{0,96},{32,0},{64,32},{96,64},{128,224},{160,128},{192,160},{224,1... | collective-permute-start | bytes 786440 | tf_op jit(solution)/shard_map/ppermute | solution.py:31
  7.5 3.3 %all-to-all-start = ((f32[8,2,512]{2,1,0:T(2,128)}), f32[8,2,512]{2,1,0:T(2,128)S(1)}, u32[]{:S(2)}, u32[]{:S(2)}) async-start(f32[8,2,512]{2,1,0:T(2,128)} %stats.1), calls=%async_computation | async-start | bytes 65536 | tf_op jit(solution)/shard_map/all_to_all | solution.py:104
  10.8 2.9 %collective-permute-start.5 = (f32[128,512]{1,0:T(8,128)S(1)}, f32[128,512]{1,0:T(8,128)S(1)}, u32[]{:S(2)}, u32[]{:S(2)}) collective-permute-start(f32[128,512]{1,0:T(8,128)S(1)} %copy-done), channel_id=1, source_target_pairs={{0,64},{32,96},{64,0},{96,32},{128,192},{160,224},{192,128},{224,1... | collective-permute-start | bytes 786440 | tf_op jit(solution)/shard_map/ppermute | solution.py:31
  13.8 2.2 %all-to-all-done = f32[8,2,512]{2,1,0:T(2,128)S(1)} async-done(((f32[8,2,512]{2,1,0:T(2,128)}), f32[8,2,512]{2,1,0:T(2,128)S(1)}, u32[]{:S(2)}, u32[]{:S(2)}) %all-to-all-start) | async-done | bytes 32800 | tf_op jit(solution)/shard_map/all_to_all | solution.py:104
  16.6 1.1 %collective-permute-start.6 = (bf16[128,512]{1,0:T(8,128)(2,1)S(1)}, bf16[128,512]{1,0:T(8,128)(2,1)S(1)}, u32[]{:S(2)}, u32[]{:S(2)}) collective-permute-start(bf16[128,512]{1,0:T(8,128)(2,1)S(1)} %get-tuple-element.43), channel_id=1, source_target_pairs={{0,64},{32,96},{64,0},{96,32},{128,192},{160,224},{192,128},{224,1... | collective-permute-start | bytes 393224 | tf_op jit(solution)/shard_map/ppermute | solution.py:31
  18.4 3.0 %collective-permute-start.3 = (f32[64,512]{1,0:T(8,128)S(1)}, f32[64,512]{1,0:T(8,128)S(1)}, u32[]{:S(2)}, u32[]{:S(2)}) collective-permute-start(f32[64,512]{1,0:T(8,128)S(1)} %fusion.27), channel_id=1, source_target_pairs={{0,1},{1,0},{2,3},{3,2},{4,5},{5,4},{6,7},{7,6},{8,9},{9,8},{10,11... | collective-permute-start | bytes 393224 | tf_op jit(solution)/shard_map/ppermute | solution.py:133
  21.8 0.6 collective-permute-done.6
  22.7 3.8 %collective-permute-start.7 = (f32[64,512]{1,0:T(8,128)S(1)}, f32[64,512]{1,0:T(8,128)S(1)}, u32[]{:S(2)}, u32[]{:S(2)}) collective-permute-start(f32[64,512]{1,0:T(8,128)S(1)} %fusion.29), channel_id=1, source_target_pairs={{0,1},{1,0},{2,3},{3,2},{4,5},{5,4},{6,7},{7,6},{8,9},{9,8},{10,11... | collective-permute-start | bytes 393224 | tf_op jit(solution)/shard_map/ppermute | solution.py:133
  26.9 0.5 collective-permute-done.7
  27.5 3.0 %collective-permute-start.10 = (f32[16,1024]{1,0:T(8,128)S(1)}, f32[16,1024]{1,0:T(8,128)S(1)}, u32[]{:S(2)}, u32[]{:S(2)}) collective-permute-start(f32[16,1024]{1,0:T(8,128)S(1)} %get-tuple-element.54), channel_id=1, source_target_pairs={{0,16},{8,24},{16,0},{24,8},{1,17},{9,25},{17,1},{25,9},{2,18},{10... | collective-permute-start | bytes 196616 | tf_op jit(solution)/shard_map/ppermute | solution.py:23
  30.5 0.4 collective-permute-start.8
  30.9 2.3 %collective-permute-start.9 = (f32[16,1024]{1,0:T(8,128)S(1)}, f32[16,1024]{1,0:T(8,128)S(1)}, u32[]{:S(2)}, u32[]{:S(2)}) collective-permute-start(f32[16,1024]{1,0:T(8,128)S(1)} %get-tuple-element.52), channel_id=1, source_target_pairs={{0,24},{8,0},{16,8},{24,16},{1,25},{9,1},{17,9},{25,17},{2,26},{10... | collective-permute-start | bytes 196616 | tf_op jit(solution)/shard_map/ppermute | solution.py:23
  33.2 1.6 %collective-permute-done.8 = f32[16,1024]{1,0:T(8,128)S(1)} collective-permute-done((f32[16,1024]{1,0:T(8,128)S(1)}, f32[16,1024]{1,0:T(8,128)S(1)}, u32[]{:S(2)}, u32[]{:S(2)}) %collective-permute-start.8) | collective-permute-done | bytes 65568 | tf_op jit(solution)/shard_map/ppermute | solution.py:23
  34.9 6.4 %collective-permute-start.11 = (f32[16,1152]{1,0:T(8,128)S(1)}, f32[16,1152]{1,0:T(8,128)S(1)}, u32[]{:S(2)}, u32[]{:S(2)}) collective-permute-start(f32[16,1152]{1,0:T(8,128)S(1)} %pad_maximum_fusion.4), channel_id=1, source_target_pairs={{0,4},{2,6},{4,0},{6,2},{1,5},{3,7},{5,1},{7,3},{8,12},{10,14},{12... | collective-permute-start | bytes 221192 | tf_op jit(solution)/shard_map/ppermute | solution.py:23
  41.2 1.2 %collective-permute-start.12 = (f32[16,1152]{1,0:T(8,128)S(1)}, f32[16,1152]{1,0:T(8,128)S(1)}, u32[]{:S(2)}, u32[]{:S(2)}) collective-permute-start(f32[16,1152]{1,0:T(8,128)S(1)} %pad_maximum_fusion.4), channel_id=1, source_target_pairs={{0,2},{2,4},{4,6},{6,0},{1,3},{3,5},{5,7},{7,1},{8,10},{10,12},{12... | collective-permute-start | bytes 221192 | tf_op jit(solution)/shard_map/ppermute | solution.py:23
  42.4 2.4 %collective-permute-start.13 = (f32[16,1152]{1,0:T(8,128)S(1)}, f32[16,1152]{1,0:T(8,128)S(1)}, u32[]{:S(2)}, u32[]{:S(2)}) collective-permute-start(f32[16,1152]{1,0:T(8,128)S(1)} %pad_maximum_fusion.4), channel_id=1, source_target_pairs={{0,6},{2,0},{4,2},{6,4},{1,7},{3,1},{5,3},{7,5},{8,14},{10,8},{12,... | collective-permute-start | bytes 221192 | tf_op jit(solution)/shard_map/ppermute | solution.py:23
  44.8 2.5 %collective-permute-done.12 = f32[16,1152]{1,0:T(8,128)S(1)} collective-permute-done((f32[16,1152]{1,0:T(8,128)S(1)}, f32[16,1152]{1,0:T(8,128)S(1)}, u32[]{:S(2)}, u32[]{:S(2)}) %collective-permute-start.12) | collective-permute-done | bytes 73760 | tf_op jit(solution)/shard_map/ppermute | solution.py:23
  47.4 1.7 %collective-permute-done.13 = f32[16,1152]{1,0:T(8,128)S(1)} collective-permute-done((f32[16,1152]{1,0:T(8,128)S(1)}, f32[16,1152]{1,0:T(8,128)S(1)}, u32[]{:S(2)}, u32[]{:S(2)}) %collective-permute-start.13) | collective-permute-done | bytes 73760 | tf_op jit(solution)/shard_map/ppermute | solution.py:23
  49.1 1.2 %collective-permute-start.14 = (f32[16,1152]{1,0:T(8,128)S(1)}, f32[16,1152]{1,0:T(8,128)S(1)}, u32[]{:S(2)}, u32[]{:S(2)}) collective-permute-start(f32[16,1152]{1,0:T(8,128)S(1)} %add_add_fusion.refs_0_), channel_id=1, source_target_pairs={{0,16},{8,24},{16,0},{24,8},{1,17},{9,25},{17,1},{25,9},{2,18},{10... | collective-permute-start | bytes 221192 | tf_op jit(solution)/shard_map/ppermute | solution.py:23
  50.3 0.6 collective-permute-start.15
  50.9 2.1 %collective-permute-start.16 = (f32[16,1152]{1,0:T(8,128)S(1)}, f32[16,1152]{1,0:T(8,128)S(1)}, u32[]{:S(2)}, u32[]{:S(2)}) collective-permute-start(f32[16,1152]{1,0:T(8,128)S(1)} %add_add_fusion.refs_0_), channel_id=1, source_target_pairs={{0,24},{8,0},{16,8},{24,16},{1,25},{9,1},{17,9},{25,17},{2,26},{10... | collective-permute-start | bytes 221192 | tf_op jit(solution)/shard_map/ppermute | solution.py:23
  53.0 0.9 %collective-permute-done.14.refs_1_ = f32[16,1152]{1,0:T(8,128)S(1)} collective-permute-done((f32[16,1152]{1,0:T(8,128)S(1)}, f32[16,1152]{1,0:T(8,128)S(1)}, u32[]{:S(2)}, u32[]{:S(2)}) %collective-permute-start.14) | collective-permute-done | bytes 73760 | tf_op jit(solution)/shard_map/ppermute | solution.py:23
  53.9 0.8 %collective-permute-done.15.refs_2_ = f32[16,1152]{1,0:T(8,128)S(1)} collective-permute-done((f32[16,1152]{1,0:T(8,128)S(1)}, f32[16,1152]{1,0:T(8,128)S(1)}, u32[]{:S(2)}, u32[]{:S(2)}) %collective-permute-start.15) | collective-permute-done | bytes 73760 | tf_op jit(solution)/shard_map/ppermute | solution.py:23
  54.7 0.7 share.1
  55.4 7.7 %all-to-all-start.1 = ((f32[16,8,128]{2,1,0:T(8,128)}), f32[16,8,128]{2,1,0:T(8,128)S(1)}, u32[]{:S(2)}, u32[]{:S(2)}) async-start(f32[16,8,128]{2,1,0:T(8,128)} %share.1), calls=%async_computation.1 | async-start | bytes 131072 | tf_op jit(solution)/shard_map/all_to_all | solution.py:158
  63.9 0.9 %collective-permute-done.17 = f32[64,1024]{1,0:T(8,128)S(1)} collective-permute-done((f32[64,1024]{1,0:T(8,128)S(1)}, f32[64,1024]{1,0:T(8,128)S(1)}, u32[]{:S(2)}, u32[]{:S(2)}) %collective-permute-start.17) | collective-permute-done | bytes 262176 | tf_op jit(solution)/shard_map/ppermute | solution.py:150
  65.4 0.8 %select_subtract_fusion = f32[128,512]{1,0:T(8,128)} fusion(f32[128,512]{1,0:T(8,128)S(1)} %fusion.15, bf16[128,512]{1,0:T(8,128)(2,1)S(1)} %get-tuple-element.45, f32[128,512]{1,0:T(8,128)S(1)} %neg.6, f32[512]{0:T(512)S(1)} %get-tuple-element.31, f32[512]{0:T(512)S(1)} %get-tuple-element.33, f32[512]{0:T(512)S(1)} %broadcast_multiply_fusion, ...), kind=kLoop, calls=%fused_computation.34 | loop fusion | flops 589824 | bytes 924160 | tf_op jit(solution)/shard_map/sub | solution.py:174
  66.2 2.7 %all-to-all-done.1 = f32[16,8,128]{2,1,0:T(8,128)S(1)} async-done(((f32[16,8,128]{2,1,0:T(8,128)}), f32[16,8,128]{2,1,0:T(8,128)S(1)}, u32[]{:S(2)}, u32[]{:S(2)}) %all-to-all-start.1) | async-done | bytes 65568 | tf_op jit(solution)/shard_map/all_to_all | solution.py:158
  68.9 0.6 slice_reduce_fusion.2
  (62 shorter events, 3.7 us)
Async XLA Ops:
  0.6 1.7 %copy-start = (f32[128,512]{1,0:T(8,128)S(1)}, f32[128,512]{1,0:T(8,128)}, u32[]{:S(2)}) copy-start(f32[128,512]{1,0:T(8,128)} %block_ref.1) | copy-start | bytes 786436
  2.3 13.7 %collective-permute-start = (f32[128,512]{1,0:T(8,128)S(1)}, f32[128,512]{1,0:T(8,128)S(1)}, u32[]{:S(2)}, u32[]{:S(2)}) collective-permute-start(f32[128,512]{1,0:T(8,128)S(1)} %copy-done), channel_id=1, source_target_pairs={{0,128},{32,160},{64,192},{96,224},{128,0},{160,32},{192,64},{224,... | collective-permute-start | bytes 786440 | tf_op jit(solution)/shard_map/ppermute | solution.py:31
  4.8 11.2 %collective-permute-start.1 = (f32[128,512]{1,0:T(8,128)S(1)}, f32[128,512]{1,0:T(8,128)S(1)}, u32[]{:S(2)}, u32[]{:S(2)}) collective-permute-start(f32[128,512]{1,0:T(8,128)S(1)} %copy-done), channel_id=1, source_target_pairs={{0,32},{32,64},{64,96},{96,0},{128,160},{160,192},{192,224},{224,1... | collective-permute-start | bytes 786440 | tf_op jit(solution)/shard_map/ppermute | solution.py:31
  6.0 10.0 %collective-permute-start.2 = (f32[128,512]{1,0:T(8,128)S(1)}, f32[128,512]{1,0:T(8,128)S(1)}, u32[]{:S(2)}, u32[]{:S(2)}) collective-permute-start(f32[128,512]{1,0:T(8,128)S(1)} %copy-done), channel_id=1, source_target_pairs={{0,96},{32,0},{64,32},{96,64},{128,224},{160,128},{192,160},{224,1... | collective-permute-start | bytes 786440 | tf_op jit(solution)/shard_map/ppermute | solution.py:31
  7.5 8.5 %all-to-all-start = ((f32[8,2,512]{2,1,0:T(2,128)}), f32[8,2,512]{2,1,0:T(2,128)S(1)}, u32[]{:S(2)}, u32[]{:S(2)}) async-start(f32[8,2,512]{2,1,0:T(2,128)} %stats.1), calls=%async_computation | async-start | bytes 65536 | tf_op jit(solution)/shard_map/all_to_all | solution.py:104
  10.8 10.9 %collective-permute-start.5 = (f32[128,512]{1,0:T(8,128)S(1)}, f32[128,512]{1,0:T(8,128)S(1)}, u32[]{:S(2)}, u32[]{:S(2)}) collective-permute-start(f32[128,512]{1,0:T(8,128)S(1)} %copy-done), channel_id=1, source_target_pairs={{0,64},{32,96},{64,0},{96,32},{128,192},{160,224},{192,128},{224,1... | collective-permute-start | bytes 786440 | tf_op jit(solution)/shard_map/ppermute | solution.py:31
  16.3 5.5 %collective-permute-start.4 = (bf16[256,512]{1,0:T(8,128)(2,1)S(1)}, bf16[256,512]{1,0:T(8,128)(2,1)S(1)}, u32[]{:S(2)}, u32[]{:S(2)}) collective-permute-start(bf16[256,512]{1,0:T(8,128)(2,1)S(1)} %pad_maximum_fusion.2), channel_id=1, source_target_pairs={{0,128},{32,160},{64,192},{96,224},{128,0},{160,32},{192,64},{224,... | collective-permute-start | bytes 786440 | tf_op jit(solution)/shard_map/ppermute | solution.py:31
  16.6 5.8 %collective-permute-start.6 = (bf16[128,512]{1,0:T(8,128)(2,1)S(1)}, bf16[128,512]{1,0:T(8,128)(2,1)S(1)}, u32[]{:S(2)}, u32[]{:S(2)}) collective-permute-start(bf16[128,512]{1,0:T(8,128)(2,1)S(1)} %get-tuple-element.43), channel_id=1, source_target_pairs={{0,64},{32,96},{64,0},{96,32},{128,192},{160,224},{192,128},{224,1... | collective-permute-start | bytes 393224 | tf_op jit(solution)/shard_map/ppermute | solution.py:31
  18.4 8.5 %collective-permute-start.3 = (f32[64,512]{1,0:T(8,128)S(1)}, f32[64,512]{1,0:T(8,128)S(1)}, u32[]{:S(2)}, u32[]{:S(2)}) collective-permute-start(f32[64,512]{1,0:T(8,128)S(1)} %fusion.27), channel_id=1, source_target_pairs={{0,1},{1,0},{2,3},{3,2},{4,5},{5,4},{6,7},{7,6},{8,9},{9,8},{10,11... | collective-permute-start | bytes 393224 | tf_op jit(solution)/shard_map/ppermute | solution.py:133
  22.7 4.8 %collective-permute-start.7 = (f32[64,512]{1,0:T(8,128)S(1)}, f32[64,512]{1,0:T(8,128)S(1)}, u32[]{:S(2)}, u32[]{:S(2)}) collective-permute-start(f32[64,512]{1,0:T(8,128)S(1)} %fusion.29), channel_id=1, source_target_pairs={{0,1},{1,0},{2,3},{3,2},{4,5},{5,4},{6,7},{7,6},{8,9},{9,8},{10,11... | collective-permute-start | bytes 393224 | tf_op jit(solution)/shard_map/ppermute | solution.py:133
  27.5 5.7 %collective-permute-start.10 = (f32[16,1024]{1,0:T(8,128)S(1)}, f32[16,1024]{1,0:T(8,128)S(1)}, u32[]{:S(2)}, u32[]{:S(2)}) collective-permute-start(f32[16,1024]{1,0:T(8,128)S(1)} %get-tuple-element.54), channel_id=1, source_target_pairs={{0,16},{8,24},{16,0},{24,8},{1,17},{9,25},{17,1},{25,9},{2,18},{10... | collective-permute-start | bytes 196616 | tf_op jit(solution)/shard_map/ppermute | solution.py:23
  30.5 4.3 %collective-permute-start.8 = (f32[16,1024]{1,0:T(8,128)S(1)}, f32[16,1024]{1,0:T(8,128)S(1)}, u32[]{:S(2)}, u32[]{:S(2)}) collective-permute-start(f32[16,1024]{1,0:T(8,128)S(1)} %get-tuple-element.53), channel_id=1, source_target_pairs={{0,8},{8,16},{16,24},{24,0},{1,9},{9,17},{17,25},{25,1},{2,10},{10... | collective-permute-start | bytes 196616 | tf_op jit(solution)/shard_map/ppermute | solution.py:23
  30.9 3.9 %collective-permute-start.9 = (f32[16,1024]{1,0:T(8,128)S(1)}, f32[16,1024]{1,0:T(8,128)S(1)}, u32[]{:S(2)}, u32[]{:S(2)}) collective-permute-start(f32[16,1024]{1,0:T(8,128)S(1)} %get-tuple-element.52), channel_id=1, source_target_pairs={{0,24},{8,0},{16,8},{24,16},{1,25},{9,1},{17,9},{25,17},{2,26},{10... | collective-permute-start | bytes 196616 | tf_op jit(solution)/shard_map/ppermute | solution.py:23
  34.9 9.9 %collective-permute-start.11 = (f32[16,1152]{1,0:T(8,128)S(1)}, f32[16,1152]{1,0:T(8,128)S(1)}, u32[]{:S(2)}, u32[]{:S(2)}) collective-permute-start(f32[16,1152]{1,0:T(8,128)S(1)} %pad_maximum_fusion.4), channel_id=1, source_target_pairs={{0,4},{2,6},{4,0},{6,2},{1,5},{3,7},{5,1},{7,3},{8,12},{10,14},{12... | collective-permute-start | bytes 221192 | tf_op jit(solution)/shard_map/ppermute | solution.py:23
  41.2 6.1 %collective-permute-start.12 = (f32[16,1152]{1,0:T(8,128)S(1)}, f32[16,1152]{1,0:T(8,128)S(1)}, u32[]{:S(2)}, u32[]{:S(2)}) collective-permute-start(f32[16,1152]{1,0:T(8,128)S(1)} %pad_maximum_fusion.4), channel_id=1, source_target_pairs={{0,2},{2,4},{4,6},{6,0},{1,3},{3,5},{5,7},{7,1},{8,10},{10,12},{12... | collective-permute-start | bytes 221192 | tf_op jit(solution)/shard_map/ppermute | solution.py:23
  42.4 6.7 %collective-permute-start.13 = (f32[16,1152]{1,0:T(8,128)S(1)}, f32[16,1152]{1,0:T(8,128)S(1)}, u32[]{:S(2)}, u32[]{:S(2)}) collective-permute-start(f32[16,1152]{1,0:T(8,128)S(1)} %pad_maximum_fusion.4), channel_id=1, source_target_pairs={{0,6},{2,0},{4,2},{6,4},{1,7},{3,1},{5,3},{7,5},{8,14},{10,8},{12,... | collective-permute-start | bytes 221192 | tf_op jit(solution)/shard_map/ppermute | solution.py:23
  49.1 4.8 %collective-permute-start.14 = (f32[16,1152]{1,0:T(8,128)S(1)}, f32[16,1152]{1,0:T(8,128)S(1)}, u32[]{:S(2)}, u32[]{:S(2)}) collective-permute-start(f32[16,1152]{1,0:T(8,128)S(1)} %add_add_fusion.refs_0_), channel_id=1, source_target_pairs={{0,16},{8,24},{16,0},{24,8},{1,17},{9,25},{17,1},{25,9},{2,18},{10... | collective-permute-start | bytes 221192 | tf_op jit(solution)/shard_map/ppermute | solution.py:23
  50.3 4.4 %collective-permute-start.15 = (f32[16,1152]{1,0:T(8,128)S(1)}, f32[16,1152]{1,0:T(8,128)S(1)}, u32[]{:S(2)}, u32[]{:S(2)}) collective-permute-start(f32[16,1152]{1,0:T(8,128)S(1)} %add_add_fusion.refs_0_), channel_id=1, source_target_pairs={{0,8},{8,16},{16,24},{24,0},{1,9},{9,17},{17,25},{25,1},{2,10},{10... | collective-permute-start | bytes 221192 | tf_op jit(solution)/shard_map/ppermute | solution.py:23
  50.9 3.8 %collective-permute-start.16 = (f32[16,1152]{1,0:T(8,128)S(1)}, f32[16,1152]{1,0:T(8,128)S(1)}, u32[]{:S(2)}, u32[]{:S(2)}) collective-permute-start(f32[16,1152]{1,0:T(8,128)S(1)} %add_add_fusion.refs_0_), channel_id=1, source_target_pairs={{0,24},{8,0},{16,8},{24,16},{1,25},{9,1},{17,9},{25,17},{2,26},{10... | collective-permute-start | bytes 221192 | tf_op jit(solution)/shard_map/ppermute | solution.py:23
  55.4 13.5 %all-to-all-start.1 = ((f32[16,8,128]{2,1,0:T(8,128)}), f32[16,8,128]{2,1,0:T(8,128)S(1)}, u32[]{:S(2)}, u32[]{:S(2)}) async-start(f32[16,8,128]{2,1,0:T(8,128)} %share.1), calls=%async_computation.1 | async-start | bytes 131072 | tf_op jit(solution)/shard_map/all_to_all | solution.py:158
  63.2 1.6 %collective-permute-start.17 = (f32[64,1024]{1,0:T(8,128)S(1)}, f32[64,1024]{1,0:T(8,128)S(1)}, u32[]{:S(2)}, u32[]{:S(2)}) collective-permute-start(f32[64,1024]{1,0:T(8,128)S(1)} %pad_maximum_fusion.3), channel_id=1, source_target_pairs={{0,1},{1,0},{2,3},{3,2},{4,5},{5,4},{6,7},{7,6},{8,9},{9,8},{10,11... | collective-permute-start | bytes 786440 | tf_op jit(solution)/shard_map/ppermute | solution.py:150

commit v9 on v7

--- a/solution.py
+++ b/solution.py
@@ -39,10 +39,25 @@
     )
 
 
-def stats_kernel(block_ref, out_ref):
-    block = block_ref[...]
-    total = jnp.sum(block, axis=0, keepdims=True)
-    off = block - total / block.shape[0]
+def stats_kernel(source_ref, out_ref, block_ref, sems):
+    pieces = sems.shape[0]
+    rows = block_ref.shape[0] // pieces
+    copies = [
+        pltpu.make_async_copy(
+            source_ref.at[k * rows : (k + 1) * rows],
+            block_ref.at[k * rows : (k + 1) * rows],
+            sems.at[k],
+        )
+        for k in range(pieces)
+    ]
+    for copy in copies:
+        copy.start()
+    partial = jnp.zeros((rows, block_ref.shape[1]), F32)
+    for k, copy in enumerate(copies):
+        copy.wait()
+        partial += block_ref[k * rows : (k + 1) * rows]
+    total = jnp.sum(partial, axis=0, keepdims=True)
+    off = block_ref[...] - total / block_ref.shape[0]
     squares = jnp.sum(off * off, axis=0, keepdims=True)
     both = jnp.concatenate([total, squares], axis=0)
     for k in range(out_ref.shape[0]):
@@ -61,7 +76,7 @@
         beside += block_ref[:1, n_all:]
     share = jnp.sum(squares, axis=0, keepdims=True) * factor + beside
     for k in range(out_ref.shape[0]):
-        out_ref[k] = jnp.broadcast_to(share, (8, 128))
+        out_ref[k] = jnp.broadcast_to(share, (2, 128))
 
 
 def whole(count):
@@ -97,8 +112,12 @@
     stats_here = pl.pallas_call(
         stats_kernel,
         out_shape=jax.ShapeDtypeStruct((rows_count, 2, col_width), F32),
-        in_specs=whole(1),
+        in_specs=[pl.BlockSpec(memory_space=pltpu.HBM)],
         out_specs=whole(1)[0],
+        scratch_shapes=[
+            pltpu.VMEM((rows_here, col_width), F32),
+            pltpu.SemaphoreType.DMA((8,)),
+        ],
         name="stats",
     )(embeddings)
     stats = lax.all_to_all(stats_here, ROWS, 0, 0)
@@ -150,7 +169,7 @@
     other_half = lax.ppermute(my_half, "core", SWAP)
     shares_here = pl.pallas_call(
         functools.partial(share_kernel, n_all, 1.0 / (float(n_all - 1) ** 2 * width)),
-        out_shape=jax.ShapeDtypeStruct((rows_count * 2, 8, 128), F32),
+        out_shape=jax.ShapeDtypeStruct((rows_count * 2, 2, 128), F32),
         in_specs=whole(ys),
         out_specs=whole(1)[0],
         name="share",

time: 69.8 us -> 69.7 us (level)
  no operation moved by 1% of the time
where the time goes in v9:
time: 69.7 us; the launch traced here: 69.5 us
  starting transfers between devices  47.2 us (68%)
  waiting for transfers between devices  14.7 us (21%)
  other arithmetic  2.34 us (3%)
  Pallas kernels  2.25 us (3%)
  matrix products  1.77 us (3%)
  between operations  1.02 us (1%)
    ppermute x9, starting transfers between devices, shift(): return lax.ppermute(block, axis, [(i, (i + k) % size) for i in range(size)])  19.5 us
    ppermute x6, starting transfers between devices, move(): lax.ppermute(block, ROWS, [(z * xs + x, (z + along_zl) % zls * xs + (x +...  9.53 us
    all_to_all x1, starting transfers between devices, on_device(): shares = lax.all_to_all(shares_here, ROWS + ('core',), 0, 0)  7.68 us
    ppermute x9, waiting for transfers between devices, shift(): return lax.ppermute(block, axis, [(i, (i + k) % size) for i in range(size)])  7.58 us
    ppermute x2, starting transfers between devices, on_device(): lax.ppermute(half_gram(1 - core, rows), 'core', SWAP)  6.99 us
    all_to_all x1, starting transfers between devices, on_device(): stats = lax.all_to_all(stats_here, ROWS, 0, 0)  3.35 us
    all_to_all x1, waiting for transfers between devices, on_device(): shares = lax.all_to_all(shares_here, ROWS + ('core',), 0, 0)  2.7 us
    all_to_all x1, waiting for transfers between devices, on_device(): stats = lax.all_to_all(stats_here, ROWS, 0, 0)  2.24 us
  transfers between devices with their start and end apart: 20, of which 11 were waited for; matrix products, arithmetic and copies ran while one was open for 5% of the time, Pallas kernels for 2%

profile of v9, /device:TPU:1, one launch (start us, length us, event | category | flops | bytes accessed | tf_op | source)
XLA Modules:
  0.0 69.5 jit_solution(11431831405531633939)
XLA Ops:
  0.6 2.6 %collective-permute-start = (f32[128,512]{1,0:T(8,128)}, f32[128,512]{1,0:T(8,128)S(1)}, u32[]{:S(2)}, u32[]{:S(2)}) collective-permute-start(f32[128,512]{1,0:T(8,128)} %source_ref.1), channel_id=1, source_target_pairs={{0,128},{32,160},{64,192},{96,224},{128,0},{160,32},{192,64},{224,... | collective-permute-start | bytes 786440 | tf_op jit(solution)/shard_map/ppermute | solution.py:31
  3.2 1.2 %collective-permute-start.1 = (f32[128,512]{1,0:T(8,128)}, f32[128,512]{1,0:T(8,128)S(1)}, u32[]{:S(2)}, u32[]{:S(2)}) collective-permute-start(f32[128,512]{1,0:T(8,128)} %source_ref.1), channel_id=1, source_target_pairs={{0,32},{32,64},{64,96},{96,0},{128,160},{160,192},{192,224},{224,1... | collective-permute-start | bytes 786440 | tf_op jit(solution)/shard_map/ppermute | solution.py:31
  4.4 1.5 %collective-permute-start.2 = (f32[128,512]{1,0:T(8,128)}, f32[128,512]{1,0:T(8,128)S(1)}, u32[]{:S(2)}, u32[]{:S(2)}) collective-permute-start(f32[128,512]{1,0:T(8,128)} %source_ref.1), channel_id=1, source_target_pairs={{0,96},{32,0},{64,32},{96,64},{128,224},{160,128},{192,160},{224,1... | collective-permute-start | bytes 786440 | tf_op jit(solution)/shard_map/ppermute | solution.py:31
  5.9 1.6 %stats.1 = f32[8,2,512]{2,1,0:T(2,128)} custom-call(f32[128,512]{1,0:T(8,128)} %source_ref.1), custom_call_target="tpu_custom_call" | custom-call | tf_op jit(solution)/shard_map/stats/pallas_call | solution.py:112
  7.5 3.4 %all-to-all-start = ((f32[8,2,512]{2,1,0:T(2,128)}), f32[8,2,512]{2,1,0:T(2,128)S(1)}, u32[]{:S(2)}, u32[]{:S(2)}) async-start(f32[8,2,512]{2,1,0:T(2,128)} %stats.1), calls=%async_computation | async-start | bytes 65536 | tf_op jit(solution)/shard_map/all_to_all | solution.py:123
  10.9 2.9 %collective-permute-start.5 = (f32[128,512]{1,0:T(8,128)S(1)}, f32[128,512]{1,0:T(8,128)S(1)}, u32[]{:S(2)}, u32[]{:S(2)}) collective-permute-start(f32[128,512]{1,0:T(8,128)S(1)} %copy-done), channel_id=1, source_target_pairs={{0,64},{32,96},{64,0},{96,32},{128,192},{160,224},{192,128},{224,1... | collective-permute-start | bytes 786440 | tf_op jit(solution)/shard_map/ppermute | solution.py:31
  13.8 2.2 %all-to-all-done = f32[8,2,512]{2,1,0:T(2,128)S(1)} async-done(((f32[8,2,512]{2,1,0:T(2,128)}), f32[8,2,512]{2,1,0:T(2,128)S(1)}, u32[]{:S(2)}, u32[]{:S(2)}) %all-to-all-start) | async-done | bytes 32800 | tf_op jit(solution)/shard_map/all_to_all | solution.py:123
  16.6 1.1 %collective-permute-start.6 = (bf16[128,512]{1,0:T(8,128)(2,1)S(1)}, bf16[128,512]{1,0:T(8,128)(2,1)S(1)}, u32[]{:S(2)}, u32[]{:S(2)}) collective-permute-start(bf16[128,512]{1,0:T(8,128)(2,1)S(1)} %get-tuple-element.39), channel_id=1, source_target_pairs={{0,64},{32,96},{64,0},{96,32},{128,192},{160,224},{192,128},{224,1... | collective-permute-start | bytes 393224 | tf_op jit(solution)/shard_map/ppermute | solution.py:31
  18.4 3.0 %collective-permute-start.3 = (f32[64,512]{1,0:T(8,128)S(1)}, f32[64,512]{1,0:T(8,128)S(1)}, u32[]{:S(2)}, u32[]{:S(2)}) collective-permute-start(f32[64,512]{1,0:T(8,128)S(1)} %fusion.27), channel_id=1, source_target_pairs={{0,1},{1,0},{2,3},{3,2},{4,5},{5,4},{6,7},{7,6},{8,9},{9,8},{10,11... | collective-permute-start | bytes 393224 | tf_op jit(solution)/shard_map/ppermute | solution.py:152
  21.6 0.6 collective-permute-done.6
  22.5 4.0 %collective-permute-start.7 = (f32[64,512]{1,0:T(8,128)S(1)}, f32[64,512]{1,0:T(8,128)S(1)}, u32[]{:S(2)}, u32[]{:S(2)}) collective-permute-start(f32[64,512]{1,0:T(8,128)S(1)} %fusion.29), channel_id=1, source_target_pairs={{0,1},{1,0},{2,3},{3,2},{4,5},{5,4},{6,7},{7,6},{8,9},{9,8},{10,11... | collective-permute-start | bytes 393224 | tf_op jit(solution)/shard_map/ppermute | solution.py:152
  26.9 0.5 collective-permute-done.7
  27.5 3.0 %collective-permute-start.10 = (f32[16,1024]{1,0:T(8,128)S(1)}, f32[16,1024]{1,0:T(8,128)S(1)}, u32[]{:S(2)}, u32[]{:S(2)}) collective-permute-start(f32[16,1024]{1,0:T(8,128)S(1)} %get-tuple-element.50), channel_id=1, source_target_pairs={{0,16},{8,24},{16,0},{24,8},{1,17},{9,25},{17,1},{25,9},{2,18},{10... | collective-permute-start | bytes 196616 | tf_op jit(solution)/shard_map/ppermute | solution.py:23
  30.5 0.4 collective-permute-start.8
  30.9 2.3 %collective-permute-start.9 = (f32[16,1024]{1,0:T(8,128)S(1)}, f32[16,1024]{1,0:T(8,128)S(1)}, u32[]{:S(2)}, u32[]{:S(2)}) collective-permute-start(f32[16,1024]{1,0:T(8,128)S(1)} %get-tuple-element.48), channel_id=1, source_target_pairs={{0,24},{8,0},{16,8},{24,16},{1,25},{9,1},{17,9},{25,17},{2,26},{10... | collective-permute-start | bytes 196616 | tf_op jit(solution)/shard_map/ppermute | solution.py:23
  33.2 1.6 %collective-permute-done.8 = f32[16,1024]{1,0:T(8,128)S(1)} collective-permute-done((f32[16,1024]{1,0:T(8,128)S(1)}, f32[16,1024]{1,0:T(8,128)S(1)}, u32[]{:S(2)}, u32[]{:S(2)}) %collective-permute-start.8) | collective-permute-done | bytes 65568 | tf_op jit(solution)/shard_map/ppermute | solution.py:23
  34.9 6.3 %collective-permute-start.11 = (f32[16,1152]{1,0:T(8,128)S(1)}, f32[16,1152]{1,0:T(8,128)S(1)}, u32[]{:S(2)}, u32[]{:S(2)}) collective-permute-start(f32[16,1152]{1,0:T(8,128)S(1)} %pad_maximum_fusion.4), channel_id=1, source_target_pairs={{0,4},{2,6},{4,0},{6,2},{1,5},{3,7},{5,1},{7,3},{8,12},{10,14},{12... | collective-permute-start | bytes 221192 | tf_op jit(solution)/shard_map/ppermute | solution.py:23
  41.2 1.2 %collective-permute-start.12 = (f32[16,1152]{1,0:T(8,128)S(1)}, f32[16,1152]{1,0:T(8,128)S(1)}, u32[]{:S(2)}, u32[]{:S(2)}) collective-permute-start(f32[16,1152]{1,0:T(8,128)S(1)} %pad_maximum_fusion.4), channel_id=1, source_target_pairs={{0,2},{2,4},{4,6},{6,0},{1,3},{3,5},{5,7},{7,1},{8,10},{10,12},{12... | collective-permute-start | bytes 221192 | tf_op jit(solution)/shard_map/ppermute | solution.py:23
  42.4 2.4 %collective-permute-start.13 = (f32[16,1152]{1,0:T(8,128)S(1)}, f32[16,1152]{1,0:T(8,128)S(1)}, u32[]{:S(2)}, u32[]{:S(2)}) collective-permute-start(f32[16,1152]{1,0:T(8,128)S(1)} %pad_maximum_fusion.4), channel_id=1, source_target_pairs={{0,6},{2,0},{4,2},{6,4},{1,7},{3,1},{5,3},{7,5},{8,14},{10,8},{12,... | collective-permute-start | bytes 221192 | tf_op jit(solution)/shard_map/ppermute | solution.py:23
  44.8 2.5 %collective-permute-done.12 = f32[16,1152]{1,0:T(8,128)S(1)} collective-permute-done((f32[16,1152]{1,0:T(8,128)S(1)}, f32[16,1152]{1,0:T(8,128)S(1)}, u32[]{:S(2)}, u32[]{:S(2)}) %collective-permute-start.12) | collective-permute-done | bytes 73760 | tf_op jit(solution)/shard_map/ppermute | solution.py:23
  47.4 1.7 %collective-permute-done.13 = f32[16,1152]{1,0:T(8,128)S(1)} collective-permute-done((f32[16,1152]{1,0:T(8,128)S(1)}, f32[16,1152]{1,0:T(8,128)S(1)}, u32[]{:S(2)}, u32[]{:S(2)}) %collective-permute-start.13) | collective-permute-done | bytes 73760 | tf_op jit(solution)/shard_map/ppermute | solution.py:23
  49.1 1.2 %collective-permute-start.14 = (f32[16,1152]{1,0:T(8,128)S(1)}, f32[16,1152]{1,0:T(8,128)S(1)}, u32[]{:S(2)}, u32[]{:S(2)}) collective-permute-start(f32[16,1152]{1,0:T(8,128)S(1)} %add_add_fusion.refs_0_), channel_id=1, source_target_pairs={{0,16},{8,24},{16,0},{24,8},{1,17},{9,25},{17,1},{25,9},{2,18},{10... | collective-permute-start | bytes 221192 | tf_op jit(solution)/shard_map/ppermute | solution.py:23
  50.3 0.6 collective-permute-start.15
  50.9 2.1 %collective-permute-start.16 = (f32[16,1152]{1,0:T(8,128)S(1)}, f32[16,1152]{1,0:T(8,128)S(1)}, u32[]{:S(2)}, u32[]{:S(2)}) collective-permute-start(f32[16,1152]{1,0:T(8,128)S(1)} %add_add_fusion.refs_0_), channel_id=1, source_target_pairs={{0,24},{8,0},{16,8},{24,16},{1,25},{9,1},{17,9},{25,17},{2,26},{10... | collective-permute-start | bytes 221192 | tf_op jit(solution)/shard_map/ppermute | solution.py:23
  53.0 0.9 %collective-permute-done.14.refs_1_ = f32[16,1152]{1,0:T(8,128)S(1)} collective-permute-done((f32[16,1152]{1,0:T(8,128)S(1)}, f32[16,1152]{1,0:T(8,128)S(1)}, u32[]{:S(2)}, u32[]{:S(2)}) %collective-permute-start.14) | collective-permute-done | bytes 73760 | tf_op jit(solution)/shard_map/ppermute | solution.py:23
  53.9 0.8 %collective-permute-done.15.refs_2_ = f32[16,1152]{1,0:T(8,128)S(1)} collective-permute-done((f32[16,1152]{1,0:T(8,128)S(1)}, f32[16,1152]{1,0:T(8,128)S(1)}, u32[]{:S(2)}, u32[]{:S(2)}) %collective-permute-start.15) | collective-permute-done | bytes 73760 | tf_op jit(solution)/shard_map/ppermute | solution.py:23
  54.7 0.6 share.1
  55.4 7.7 %all-to-all-start.1 = ((f32[16,2,128]{2,1,0:T(2,128)}), f32[16,2,128]{2,1,0:T(2,128)S(1)}, u32[]{:S(2)}, u32[]{:S(2)}) async-start(f32[16,2,128]{2,1,0:T(2,128)} %share.1), calls=%async_computation.1 | async-start | bytes 32768 | tf_op jit(solution)/shard_map/all_to_all | solution.py:177
  63.9 0.9 %collective-permute-done.17 = f32[64,1024]{1,0:T(8,128)S(1)} collective-permute-done((f32[64,1024]{1,0:T(8,128)S(1)}, f32[64,1024]{1,0:T(8,128)S(1)}, u32[]{:S(2)}, u32[]{:S(2)}) %collective-permute-start.17) | collective-permute-done | bytes 262176 | tf_op jit(solution)/shard_map/ppermute | solution.py:169
  65.4 0.8 %select_subtract_fusion = f32[128,512]{1,0:T(8,128)} fusion(f32[128,512]{1,0:T(8,128)S(1)} %fusion.15, bf16[128,512]{1,0:T(8,128)(2,1)S(1)} %get-tuple-element.41, f32[128,512]{1,0:T(8,128)S(1)} %neg.6, f32[512]{0:T(512)S(1)} %get-tuple-element.27, f32[512]{0:T(512)S(1)} %get-tuple-element.29, f32[512]{0:T(512)S(1)} %broadcast_multiply_fusion, ...), kind=kLoop, calls=%fused_computation.34 | loop fusion | flops 589824 | bytes 924160 | tf_op jit(solution)/shard_map/sub | solution.py:193
  66.2 2.7 %all-to-all-done.1 = f32[16,2,128]{2,1,0:T(2,128)S(1)} async-done(((f32[16,2,128]{2,1,0:T(2,128)}), f32[16,2,128]{2,1,0:T(2,128)S(1)}, u32[]{:S(2)}, u32[]{:S(2)}) %all-to-all-start.1) | async-done | bytes 16416 | tf_op jit(solution)/shard_map/all_to_all | solution.py:177
  68.9 0.6 slice_reduce_fusion.2
  (62 shorter events, 3.5 us)
Async XLA Ops:
  0.6 10.2 %copy-start = (f32[128,512]{1,0:T(8,128)S(1)}, f32[128,512]{1,0:T(8,128)}, u32[]{:S(2)}) copy-start(f32[128,512]{1,0:T(8,128)} %source_ref.1) | copy-start | bytes 786436
  0.6 15.4 %collective-permute-start = (f32[128,512]{1,0:T(8,128)}, f32[128,512]{1,0:T(8,128)S(1)}, u32[]{:S(2)}, u32[]{:S(2)}) collective-permute-start(f32[128,512]{1,0:T(8,128)} %source_ref.1), channel_id=1, source_target_pairs={{0,128},{32,160},{64,192},{96,224},{128,0},{160,32},{192,64},{224,... | collective-permute-start | bytes 786440 | tf_op jit(solution)/shard_map/ppermute | solution.py:31
  3.2 12.8 %collective-permute-start.1 = (f32[128,512]{1,0:T(8,128)}, f32[128,512]{1,0:T(8,128)S(1)}, u32[]{:S(2)}, u32[]{:S(2)}) collective-permute-start(f32[128,512]{1,0:T(8,128)} %source_ref.1), channel_id=1, source_target_pairs={{0,32},{32,64},{64,96},{96,0},{128,160},{160,192},{192,224},{224,1... | collective-permute-start | bytes 786440 | tf_op jit(solution)/shard_map/ppermute | solution.py:31
  4.4 11.6 %collective-permute-start.2 = (f32[128,512]{1,0:T(8,128)}, f32[128,512]{1,0:T(8,128)S(1)}, u32[]{:S(2)}, u32[]{:S(2)}) collective-permute-start(f32[128,512]{1,0:T(8,128)} %source_ref.1), channel_id=1, source_target_pairs={{0,96},{32,0},{64,32},{96,64},{128,224},{160,128},{192,160},{224,1... | collective-permute-start | bytes 786440 | tf_op jit(solution)/shard_map/ppermute | solution.py:31
  7.5 8.5 %all-to-all-start = ((f32[8,2,512]{2,1,0:T(2,128)}), f32[8,2,512]{2,1,0:T(2,128)S(1)}, u32[]{:S(2)}, u32[]{:S(2)}) async-start(f32[8,2,512]{2,1,0:T(2,128)} %stats.1), calls=%async_computation | async-start | bytes 65536 | tf_op jit(solution)/shard_map/all_to_all | solution.py:123
  10.9 10.8 %collective-permute-start.5 = (f32[128,512]{1,0:T(8,128)S(1)}, f32[128,512]{1,0:T(8,128)S(1)}, u32[]{:S(2)}, u32[]{:S(2)}) collective-permute-start(f32[128,512]{1,0:T(8,128)S(1)} %copy-done), channel_id=1, source_target_pairs={{0,64},{32,96},{64,0},{96,32},{128,192},{160,224},{192,128},{224,1... | collective-permute-start | bytes 786440 | tf_op jit(solution)/shard_map/ppermute | solution.py:31
  16.3 5.3 %collective-permute-start.4 = (bf16[256,512]{1,0:T(8,128)(2,1)S(1)}, bf16[256,512]{1,0:T(8,128)(2,1)S(1)}, u32[]{:S(2)}, u32[]{:S(2)}) collective-permute-start(bf16[256,512]{1,0:T(8,128)(2,1)S(1)} %pad_maximum_fusion.2), channel_id=1, source_target_pairs={{0,128},{32,160},{64,192},{96,224},{128,0},{160,32},{192,64},{224,... | collective-permute-start | bytes 786440 | tf_op jit(solution)/shard_map/ppermute | solution.py:31
  16.6 5.7 %collective-permute-start.6 = (bf16[128,512]{1,0:T(8,128)(2,1)S(1)}, bf16[128,512]{1,0:T(8,128)(2,1)S(1)}, u32[]{:S(2)}, u32[]{:S(2)}) collective-permute-start(bf16[128,512]{1,0:T(8,128)(2,1)S(1)} %get-tuple-element.39), channel_id=1, source_target_pairs={{0,64},{32,96},{64,0},{96,32},{128,192},{160,224},{192,128},{224,1... | collective-permute-start | bytes 393224 | tf_op jit(solution)/shard_map/ppermute | solution.py:31
  18.4 8.5 %collective-permute-start.3 = (f32[64,512]{1,0:T(8,128)S(1)}, f32[64,512]{1,0:T(8,128)S(1)}, u32[]{:S(2)}, u32[]{:S(2)}) collective-permute-start(f32[64,512]{1,0:T(8,128)S(1)} %fusion.27), channel_id=1, source_target_pairs={{0,1},{1,0},{2,3},{3,2},{4,5},{5,4},{6,7},{7,6},{8,9},{9,8},{10,11... | collective-permute-start | bytes 393224 | tf_op jit(solution)/shard_map/ppermute | solution.py:152
  22.5 4.9 %collective-permute-start.7 = (f32[64,512]{1,0:T(8,128)S(1)}, f32[64,512]{1,0:T(8,128)S(1)}, u32[]{:S(2)}, u32[]{:S(2)}) collective-permute-start(f32[64,512]{1,0:T(8,128)S(1)} %fusion.29), channel_id=1, source_target_pairs={{0,1},{1,0},{2,3},{3,2},{4,5},{5,4},{6,7},{7,6},{8,9},{9,8},{10,11... | collective-permute-start | bytes 393224 | tf_op jit(solution)/shard_map/ppermute | solution.py:152
  27.5 5.7 %collective-permute-start.10 = (f32[16,1024]{1,0:T(8,128)S(1)}, f32[16,1024]{1,0:T(8,128)S(1)}, u32[]{:S(2)}, u32[]{:S(2)}) collective-permute-start(f32[16,1024]{1,0:T(8,128)S(1)} %get-tuple-element.50), channel_id=1, source_target_pairs={{0,16},{8,24},{16,0},{24,8},{1,17},{9,25},{17,1},{25,9},{2,18},{10... | collective-permute-start | bytes 196616 | tf_op jit(solution)/shard_map/ppermute | solution.py:23
  30.5 4.3 %collective-permute-start.8 = (f32[16,1024]{1,0:T(8,128)S(1)}, f32[16,1024]{1,0:T(8,128)S(1)}, u32[]{:S(2)}, u32[]{:S(2)}) collective-permute-start(f32[16,1024]{1,0:T(8,128)S(1)} %get-tuple-element.49), channel_id=1, source_target_pairs={{0,8},{8,16},{16,24},{24,0},{1,9},{9,17},{17,25},{25,1},{2,10},{10... | collective-permute-start | bytes 196616 | tf_op jit(solution)/shard_map/ppermute | solution.py:23
  30.9 3.9 %collective-permute-start.9 = (f32[16,1024]{1,0:T(8,128)S(1)}, f32[16,1024]{1,0:T(8,128)S(1)}, u32[]{:S(2)}, u32[]{:S(2)}) collective-permute-start(f32[16,1024]{1,0:T(8,128)S(1)} %get-tuple-element.48), channel_id=1, source_target_pairs={{0,24},{8,0},{16,8},{24,16},{1,25},{9,1},{17,9},{25,17},{2,26},{10... | collective-permute-start | bytes 196616 | tf_op jit(solution)/shard_map/ppermute | solution.py:23
  34.9 9.9 %collective-permute-start.11 = (f32[16,1152]{1,0:T(8,128)S(1)}, f32[16,1152]{1,0:T(8,128)S(1)}, u32[]{:S(2)}, u32[]{:S(2)}) collective-permute-start(f32[16,1152]{1,0:T(8,128)S(1)} %pad_maximum_fusion.4), channel_id=1, source_target_pairs={{0,4},{2,6},{4,0},{6,2},{1,5},{3,7},{5,1},{7,3},{8,12},{10,14},{12... | collective-permute-start | bytes 221192 | tf_op jit(solution)/shard_map/ppermute | solution.py:23
  41.2 6.1 %collective-permute-start.12 = (f32[16,1152]{1,0:T(8,128)S(1)}, f32[16,1152]{1,0:T(8,128)S(1)}, u32[]{:S(2)}, u32[]{:S(2)}) collective-permute-start(f32[16,1152]{1,0:T(8,128)S(1)} %pad_maximum_fusion.4), channel_id=1, source_target_pairs={{0,2},{2,4},{4,6},{6,0},{1,3},{3,5},{5,7},{7,1},{8,10},{10,12},{12... | collective-permute-start | bytes 221192 | tf_op jit(solution)/shard_map/ppermute | solution.py:23
  42.4 6.7 %collective-permute-start.13 = (f32[16,1152]{1,0:T(8,128)S(1)}, f32[16,1152]{1,0:T(8,128)S(1)}, u32[]{:S(2)}, u32[]{:S(2)}) collective-permute-start(f32[16,1152]{1,0:T(8,128)S(1)} %pad_maximum_fusion.4), channel_id=1, source_target_pairs={{0,6},{2,0},{4,2},{6,4},{1,7},{3,1},{5,3},{7,5},{8,14},{10,8},{12,... | collective-permute-start | bytes 221192 | tf_op jit(solution)/shard_map/ppermute | solution.py:23
  49.1 4.8 %collective-permute-start.14 = (f32[16,1152]{1,0:T(8,128)S(1)}, f32[16,1152]{1,0:T(8,128)S(1)}, u32[]{:S(2)}, u32[]{:S(2)}) collective-permute-start(f32[16,1152]{1,0:T(8,128)S(1)} %add_add_fusion.refs_0_), channel_id=1, source_target_pairs={{0,16},{8,24},{16,0},{24,8},{1,17},{9,25},{17,1},{25,9},{2,18},{10... | collective-permute-start | bytes 221192 | tf_op jit(solution)/shard_map/ppermute | solution.py:23
  50.3 4.4 %collective-permute-start.15 = (f32[16,1152]{1,0:T(8,128)S(1)}, f32[16,1152]{1,0:T(8,128)S(1)}, u32[]{:S(2)}, u32[]{:S(2)}) collective-permute-start(f32[16,1152]{1,0:T(8,128)S(1)} %add_add_fusion.refs_0_), channel_id=1, source_target_pairs={{0,8},{8,16},{16,24},{24,0},{1,9},{9,17},{17,25},{25,1},{2,10},{10... | collective-permute-start | bytes 221192 | tf_op jit(solution)/shard_map/ppermute | solution.py:23
  50.9 3.8 %collective-permute-start.16 = (f32[16,1152]{1,0:T(8,128)S(1)}, f32[16,1152]{1,0:T(8,128)S(1)}, u32[]{:S(2)}, u32[]{:S(2)}) collective-permute-start(f32[16,1152]{1,0:T(8,128)S(1)} %add_add_fusion.refs_0_), channel_id=1, source_target_pairs={{0,24},{8,0},{16,8},{24,16},{1,25},{9,1},{17,9},{25,17},{2,26},{10... | collective-permute-start | bytes 221192 | tf_op jit(solution)/shard_map/ppermute | solution.py:23
  55.4 13.5 %all-to-all-start.1 = ((f32[16,2,128]{2,1,0:T(2,128)}), f32[16,2,128]{2,1,0:T(2,128)S(1)}, u32[]{:S(2)}, u32[]{:S(2)}) async-start(f32[16,2,128]{2,1,0:T(2,128)} %share.1), calls=%async_computation.1 | async-start | bytes 32768 | tf_op jit(solution)/shard_map/all_to_all | solution.py:177
  63.1 1.6 %collective-permute-start.17 = (f32[64,1024]{1,0:T(8,128)S(1)}, f32[64,1024]{1,0:T(8,128)S(1)}, u32[]{:S(2)}, u32[]{:S(2)}) collective-permute-start(f32[64,1024]{1,0:T(8,128)S(1)} %pad_maximum_fusion.3), channel_id=1, source_target_pairs={{0,1},{1,0},{2,3},{3,2},{4,5},{5,4},{6,7},{7,6},{8,9},{9,8},{10,11... | collective-permute-start | bytes 786440 | tf_op jit(solution)/shard_map/ppermute | solution.py:169
